TPU v7x, 32 devices: a whole 2x2x4 slice. The times are simulated.
32 devices in a mesh: head: 4 (over z), seq: 8 (over y, x, core).
Axes of the slice: x: 2, y: 2, z: 4, core: 2. Of those that a mesh axis runs over, the one named last changes fastest.
Arguments:
- query_mla: bfloat16 [256, 24576], P(None, 'head'), may hold values from -6 to 6
- key_mla: bfloat16 [4096, 24576], P('seq', 'head'), may hold values from -6 to 6
- lse: float32 [256, 128], P(None, 'head'), may hold values from 3 to 6
- query_index: bfloat16 [256, 8192], P(None, 'head'), may hold values from -0.5 to 0.5
- key_index: bfloat16 [4096, 128], P('seq'), may hold values from -6 to 6
- head_weight: float32 [256, 64], P(None, 'head'), may hold values from -25 to 25
- query_pos: int32 [256], replicated, may hold values from 1024 to 4095
- key_block: int32 [8], P('seq'), may hold values from 0 to 7, each once
Outputs:
- kl: bfloat16 [256], replicated
- grad_query_index: bfloat16 [256, 8192], P(None, 'head')
- grad_head_weight: bfloat16 [256, 64], P(None, 'head')
- grad_key_index: bfloat16 [4096, 128], P('seq')
Inputs may be any that keep to these rules, and one draw needn't show every extreme that they name: key_block is a permutation of 0 to 7; the keys of index d of seq hold the positions key_block[d] * 512 to key_block[d] * 512 + 511.
All inputs are finite; a program needn't handle non-finite values.
Results may differ from a plain program's by a relative error of at most 0.012.
Values may be sent and summed in bfloat16 or wider, within the bound.
No kernel may reach another device: no remote copies, remote signals or barrier semaphores. Data moves between devices by JAX's collectives and lax.ppermute only.
A program may use at most 128 MiB of HBM per device.

v0:
```python
import jax
import jax.numpy as jnp
from jax import lax
from jax.sharding import PartitionSpec as P


def local(query_mla, key_mla, lse, query_index, key_index, head_weight, query_pos, key_block):
    row_count = query_mla.shape[0]
    key_count = key_mla.shape[0]
    mla_heads = lse.shape[1]
    head_width = query_mla.shape[1] // mla_heads
    index_heads = head_weight.shape[1]
    index_width = key_index.shape[1]
    queries = query_mla.reshape(row_count, mla_heads, head_width)
    mla_keys = key_mla.reshape(key_count, mla_heads, head_width)
    positions = key_block[0] * key_count + jnp.arange(key_count, dtype=jnp.int32)
    valid = positions[None, :] <= query_pos[:, None]
    score = jnp.einsum(
        "thd,jhd->htj", queries, mla_keys, preferred_element_type=jnp.float32
    ) * head_width ** (-0.5)
    attention_part = jnp.sum(
        jnp.where(valid[None], jnp.exp(score - lse.T[:, :, None]), 0.0), axis=0
    )
    indexer_q = query_index.reshape(row_count, index_heads, index_width)
    dots = jnp.einsum("tid,jd->tij", indexer_q, key_index, preferred_element_type=jnp.float32)
    rectified = jnp.maximum(dots, 0.0)
    logit_part = jnp.sum(head_weight[:, :, None] * rectified, axis=1)
    attention, logit = lax.psum((attention_part, logit_part), "head")
    masked = jnp.where(valid, logit, -1e30)
    local_peak = jnp.max(masked, axis=1)
    peak = lax.pmax(local_peak, "seq")
    shifted = jnp.where(valid, jnp.exp(masked - peak[:, None]), 0.0)
    norm, total = lax.psum((jnp.sum(shifted, axis=1), jnp.sum(attention, axis=1)), "seq")
    target = attention / total[:, None]
    log_prob = masked - peak[:, None] - jnp.log(norm)[:, None]
    prob = jnp.where(valid, jnp.exp(log_prob), 0.0)
    log_target = jnp.log(jnp.where(valid, attention, 1.0)) - jnp.log(total)[:, None]
    kl_part = jnp.sum(jnp.where(valid, target * (log_target - log_prob), 0.0), axis=1)
    dlogit = jnp.where(valid, prob - target, 0.0).astype(jnp.bfloat16)
    grad_rows = dlogit.astype(jnp.float32)
    weight_part = jnp.sum(grad_rows[:, None, :] * rectified, axis=2)
    opened = dots > 0
    gated = jnp.where(opened, dlogit[:, None, :], 0)
    query_part = jnp.einsum(
        "tij,jd->tid", gated, key_index, preferred_element_type=jnp.float32
    ).reshape(row_count, index_heads * index_width)
    coef = jnp.where(opened, grad_rows[:, None, :] * head_weight[:, :, None], 0.0).astype(
        jnp.bfloat16
    )
    key_part = jnp.einsum("tij,tid->jd", coef, indexer_q, preferred_element_type=jnp.float32)
    grad_key_index = lax.psum(key_part, "head").astype(jnp.bfloat16)
    query_sum, weight_sum, kl_sum = lax.psum((query_part, weight_part, kl_part), "seq")
    scaled = query_sum.reshape(row_count, index_heads, index_width) * head_weight[:, :, None]
    grad_query_index = scaled.reshape(row_count, index_heads * index_width).astype(jnp.bfloat16)
    grad_head_weight = weight_sum.astype(jnp.bfloat16)
    kl = kl_sum.astype(jnp.bfloat16)
    return (kl, grad_query_index, grad_head_weight, grad_key_index)


def solution(mesh):
    placed = (
        P(None, "head"),
        P("seq", "head"),
        P(None, "head"),
        P(None, "head"),
        P("seq", None),
        P(None, "head"),
        P(),
        P("seq"),
    )
    return jax.shard_map(
        local,
        mesh=mesh,
        in_specs=placed,
        out_specs=(P(), P(None, "head"), P(None, "head"), P("seq", None)),
        check_vma=False,
    )
```

profile of v0, /device:TPU:0, one launch (start us, length us, event | category | flops | bytes accessed | tf_op | source)
XLA Modules:
  0.0 196.1 jit_solution(2507266443124204139)
XLA Ops:
  7.2 0.0 copy-start
  7.2 0.0 copy-start.5
  7.2 0.0 copy-start.4
  7.2 0.0 copy-start.3
  7.2 0.0 all-reduce.9.cloned.1.call-start
  7.3 4.7 %copy.20 = bf16[256,6144]{0,1:T(8,128)(2,1)} copy(bf16[256,6144]{1,0:T(8,128)(2,1)} %param.8) | data formatting | bytes 6291456 | tf_op args[0]
  12.0 0.0 copy-start.6
  12.0 8.6 %copy.21 = bf16[512,6144]{0,1:T(8,128)(2,1)} copy(bf16[512,6144]{1,0:T(8,128)(2,1)} %param.9) | data formatting | bytes 12582912 | tf_op args[1]
  20.6 0.0 copy-start.1
  20.6 0.0 copy-start.2
  21.4 0.0 copy-done.5
  21.4 0.1 broadcast_compare_fusion
  21.6 0.0 copy-done
  21.6 0.0 copy-done.4
  21.6 0.0 copy-done.3
  21.6 5.4 %multiply_reduce_fusion.1 = (f32[256,512]{1,0:T(8,128)}, f32[256,16,512]{2,0,1:T(8,128)}) fusion(f32[256,16]{0,1:T(8,128)S(1)} %copy-done.4, bf16[512,128]{1,0:T(8,128)(2,1)S(1)} %copy-done.3, bf16[256,2048]{1,0:T(8,128)(2,1)S(1)} %copy-done), kind=kOutput, calls=%fused_computation.7 | convolution fusion | flops 543031296 | bytes 10108928 | tf_op jit(solution)/shard_map/tid,jd->tij/dot_general | solution.py:25
  27.0 0.0 copy-done.6
  27.0 0.0 copy-done.1
  27.0 0.0 copy-done.2
  27.0 7.2 %select_reduce_fusion = f32[256,512]{1,0:T(8,128)} fusion(bf16[256,32,192]{0,2,1:T(8,128)(2,1)S(1)} %bitcast.38, bf16[512,32,192]{0,2,1:T(8,128)(2,1)S(1)} %bitcast.37, f32[32,256]{1,0:T(8,128)S(1)} %bitcast.40, pred[256,512]{1,0:T(8,128)(4,1)S(1)} %broadcast_compare_fusion), kind=kOutput, calls=%fused_computation | convolution fusion | flops 1627258880 | bytes 10125312 | tf_op jit(solution)/shard_map/thd,jhd->htj/dot_general | solution.py:18
  34.2 0.0 all-reduce.9.cloned.1.call-update
  34.2 0.0 all-reduce.7.cloned.1.call-start
  34.3 0.1 copy.25
  34.4 4.5 %fusion.3 = u16[256,512]{1,0:T(8,128)(2,1)S(1)} fusion(f32[256,16,512]{2,0,1:T(8,128)} %get-tuple-element.14), kind=kLoop, calls=%fused_computation.8 | loop fusion | flops 10354688 | bytes 8650752
  38.8 50.4 %all-reduce.9.cloned.1.call-done = (f32[256,512]{1,0:T(8,128)}, f32[256,512]{1,0:T(8,128)}) async-done(((f32[256,512]{1,0:T(8,128)}, f32[256,512]{1,0:T(8,128)}), (f32[256,512]{1,0:T(8,128)}, f32[256,512]{1,0:T(8,128)})) %all-reduce.9.cloned.1.call-update) | async-done | bytes 1048592 | tf_op jit(solution)/shard_map/psum | solution.py:28
  89.2 1.2 fusion.31
  90.5 13.8 %pmax.7 = f32[256]{0:T(256)S(1)} all-reduce(f32[256]{0:T(256)S(1)} %fusion.31), channel_id=1, replica_groups=mesh['head'=4,'seq'=8] {'seq'}, use_global_device_ids=true, to_apply=%region_7.8 | all-reduce | flops 256 | bytes 2048 | tf_op jit(solution)/shard_map/pmax | solution.py:31
  104.3 1.3 fusion.26
  105.6 1.2 reduce_sum.55
  106.8 11.8 %all-reduce.1 = (f32[256]{0:T(256)S(1)}, f32[256]{0:T(256)S(1)}) all-reduce(f32[256]{0:T(256)S(1)} %fusion.26, f32[256]{0:T(256)S(1)} %reduce_sum.55), channel_id=1, replica_groups=mesh['head'=4,'seq'=8] {'seq'}, use_global_device_ids=true, to_apply=%region_9.10 | all-reduce | flops 512 | bytes 4096 | tf_op jit(solution)/shard_map/psum | solution.py:33
  118.6 1.7 fusion.38
  120.3 2.8 %fusion.4 = f32[256,16,128]{0,2,1:T(8,128)} fusion(u16[256,512]{1,0:T(8,128)(2,1)S(1)} %fusion.3, bf16[256,512]{1,0:T(8,128)(2,1)S(1)} %get-tuple-element.11, bf16[512,128]{1,0:T(8,128)(2,1)S(1)} %copy-done.3), kind=kOutput, calls=%fused_computation.9 | convolution fusion | flops 547356672 | bytes 2752512 | tf_op jit(solution)/shard_map/tij,jd->tid/dot_general | solution.py:44
  123.1 3.0 %copy.24 = f32[256,2048]{1,0:T(8,128)} copy(f32[256,2048]{0,1:T(8,128)} %bitcast.39) | data formatting | bytes 4194304 | tf_op jit(solution)/shard_map/reshape | solution.py:46
  126.1 0.0 all-reduce.7.cloned.1.call-update
  126.1 2.2 %fusion.14 = f32[512,128]{1,0:T(8,128)S(1)} fusion(f32[256,512]{1,0:T(8,128)S(1)} %get-tuple-element.10, f32[256,16]{0,1:T(8,128)S(1)} %copy-done.4, u16[256,512]{1,0:T(8,128)(2,1)S(1)} %fusion.3, bf16[256,2048]{1,0:T(8,128)(2,1)S(1)} %copy-done), kind=kOutput, calls=%fused_computation.18 | convolution fusion | flops 551550976 | bytes 2113536 | tf_op jit(solution)/shard_map/tij,tid->jd/dot_general | solution.py:50
  128.3 4.6 %multiply_reduce_fusion = f32[256,16]{0,1:T(8,128)S(1)} fusion(f32[256,16,512]{2,0,1:T(8,128)} %get-tuple-element.14, f32[256,512]{1,0:T(8,128)S(1)} %get-tuple-element.10), kind=kLoop, calls=%fused_computation.6 | loop fusion | flops 6287360 | bytes 8929280 | tf_op jit(solution)/shard_map/reduce_sum | solution.py:41
  132.9 23.2 %all-reduce = (bf16[256]{0:T(256)(128)(2,1)}, bf16[256,16]{0,1:T(8,128)(2,1)}) all-reduce(f32[256]{0:T(256)S(1)} %get-tuple-element.12, f32[256,16]{0,1:T(8,128)S(1)} %multiply_reduce_fusion), channel_id=1, replica_groups=mesh['head'=4,'seq'=8] {'seq'}, use_global_device_ids=true, to_apply=%region_11.12 | all-reduce | flops 4352 | bytes 26112 | tf_op jit(solution)/shard_map/psum | solution.py:52
  156.2 22.4 %all-reduce.10 = bf16[512,128]{1,0:T(8,128)(2,1)} all-reduce(f32[512,128]{1,0:T(8,128)S(1)} %fusion.14), channel_id=1, replica_groups=mesh['head'=4,'seq'=8] {'head'}, use_global_device_ids=true, to_apply=%region_15.16 | all-reduce | flops 65536 | bytes 393216 | tf_op jit(solution)/shard_map/psum | solution.py:51
  178.5 6.9 %all-reduce.7.cloned.1.call-done = f32[256,2048]{1,0:T(8,128)} async-done(((f32[256,2048]{1,0:T(8,128)}), f32[256,2048]{1,0:T(8,128)}) %all-reduce.7.cloned.1.call-update) | async-done | bytes 2097168 | tf_op jit(solution)/shard_map/psum | solution.py:52
  185.4 0.6 mul.58
  186.0 3.3 %fusion.11 = bf16[256,2048]{1,0:T(8,128)(2,1)} fusion(f32[256,2048]{1,0:T(8,128)} %all-reduce.7.cloned.1.call-done, f32[32,8,16,128]{3,2,1,0:T(8,128)S(1)} %bitcast.36), kind=kLoop, calls=%fused_computation.15 | loop fusion | flops 1048576 | bytes 5242880 | tf_op jit(solution)/shard_map/convert_element_type | solution.py:54
  (3 shorter events, 0.0 us)
Async XLA Ops:
  7.2 14.4 %copy-start = (bf16[256,2048]{1,0:T(8,128)(2,1)S(1)}, bf16[256,2048]{1,0:T(8,128)(2,1)}, u32[]{:S(2)}) copy-start(bf16[256,2048]{1,0:T(8,128)(2,1)} %param.11) | copy-start | bytes 3145732
  7.2 14.2 %copy-start.5 = (s32[256]{0:T(256)S(1)}, s32[256]{0:T(256)}, u32[]{:S(2)}) copy-start(s32[256]{0:T(256)} %param.14) | copy-start | bytes 3076
  7.2 14.4 %copy-start.4 = (f32[256,16]{0,1:T(8,128)S(1)}, f32[256,16]{0,1:T(8,128)}, u32[]{:S(2)}) copy-start(f32[256,16]{0,1:T(8,128)} %param.13) | copy-start | bytes 49156
  7.2 14.4 %copy-start.3 = (bf16[512,128]{1,0:T(8,128)(2,1)S(1)}, bf16[512,128]{1,0:T(8,128)(2,1)}, u32[]{:S(2)}) copy-start(bf16[512,128]{1,0:T(8,128)(2,1)} %param.12) | copy-start | bytes 393220
  7.2 82.0 %all-reduce.9.cloned.1.call-start = ((), (), s32[]{:S(2)}) async-start(), calls=%async_computation.1 | async-start | bytes 2097152 | tf_op jit(solution)/shard_map/psum | solution.py:28
  12.0 15.0 %copy-start.6 = (f32[256,32]{0,1:T(8,128)S(1)}, f32[256,32]{0,1:T(8,128)}, u32[]{:S(2)}) copy-start(f32[256,32]{0,1:T(8,128)} %param.10) | copy-start | bytes 98308
  20.6 6.4 %copy-start.1 = (bf16[512,6144]{0,1:T(8,128)(2,1)S(1)}, bf16[512,6144]{0,1:T(8,128)(2,1)}, u32[]{:S(2)}) copy-start(bf16[512,6144]{0,1:T(8,128)(2,1)} %copy.21) | copy-start | bytes 18874372
  20.6 6.4 %copy-start.2 = (bf16[256,6144]{0,1:T(8,128)(2,1)S(1)}, bf16[256,6144]{0,1:T(8,128)(2,1)}, u32[]{:S(2)}) copy-start(bf16[256,6144]{0,1:T(8,128)(2,1)} %copy.20) | copy-start | bytes 9437188
  34.2 151.2 %all-reduce.7.cloned.1.call-start = ((), (), s32[]{:S(2)}) async-start(), calls=%async_computation | async-start | bytes 4194304 | tf_op jit(solution)/shard_map/psum | solution.py:52
Sparse Core Ops, SparseCore 0:
  34.3 54.8 all-reduce.8
  126.2 59.1 all-reduce.6
where the time goes:
time: 197 us; the launch traced here: 196 us
  blocking collectives  71.2 us (36%)
  waiting for transfers between devices  57.3 us (29%)
  other arithmetic  18 us (9%)
  matrix products  17.6 us (9%)
  local copies, waits for them, and re-layouts  17 us (9%)
  between operations  14.9 us (8%)
    psum x1, waiting for transfers between devices, local(): attention, logit = lax.psum((attention_part, logit_part), 'head')  50.4 us
    psum x1, blocking collectives, local(): lax.psum((query_part, weight_part, kl_part), 'seq')  23.2 us
    psum x1, blocking collectives, local(): grad_key_index = lax.psum(key_part, 'head').astype(jnp.bfloat16)  22.4 us
    pmax x1, blocking collectives, local(): peak = lax.pmax(local_peak, 'seq')  13.8 us
    unnamed x17, local copies, waits for them, and re-layouts  13.5 us
    psum x1, blocking collectives, local(): lax.psum((jnp.sum(shifted, axis=1), jnp.sum(attention, axis=1)), 'seq')  11.8 us
    dot_general x1, matrix products, local(): jnp.einsum('thd,jhd->htj', queries, mla_keys, preferred_element_type=jnp....  7.19 us
    psum x1, waiting for transfers between devices, local(): lax.psum((query_part, weight_part, kl_part), 'seq')  6.85 us
  transfers between devices with their start and end apart: 2, of which 2 were waited for; matrix products, arithmetic and copies ran while one was open for 6% of the time, Pallas kernels for 0%

commit v1 on v0

--- a/solution.py
+++ b/solution.py
@@ -1,10 +1,340 @@
+import functools
+import math
+
 import jax
 import jax.numpy as jnp
 from jax import lax
+from jax.experimental import pallas as pl
+from jax.experimental.pallas import tpu as pltpu
 from jax.sharding import PartitionSpec as P
 
-
-def local(query_mla, key_mla, lse, query_index, key_index, head_weight, query_pos, key_block):
+BF16 = jnp.bfloat16
+F32 = jnp.float32
+LANES = 128
+NT = (((1,), (1,)), ((), ()))
+
+
+def vmem_spec():
+    return pl.BlockSpec(memory_space=pltpu.VMEM)
+
+
+def smem_spec():
+    return pl.BlockSpec(memory_space=pltpu.SMEM)
+
+
+def bits(n):
+    return [1 << b for b in range(n.bit_length() - 1)]
+
+
+def attention_kernel(heads_step, width, split, me_ref, block_ref, q_ref, k_ref, lse_ref, qi_ref, hw_ref, out_ref, acc_ref):
+    step = pl.program_id(0)
+    rows, keys = q_ref.shape[0], k_ref.shape[0]
+    log2e = math.log2(math.e)
+    scale = width ** (-0.5) * log2e
+    lanes = lax.broadcasted_iota(jnp.int32, lse_ref.shape, 1)
+    total = None
+    for a in range(heads_step):
+        low, high = a * width, (a + 1) * width
+        start = low // LANES * LANES
+        stop = -(-high // LANES) * LANES
+        q = q_ref[:, start:stop]
+        if start != low or stop != high:
+            at = lax.broadcasted_iota(jnp.int32, q.shape, 1) + start
+            q = jnp.where((at >= low) & (at < high), q, jnp.zeros_like(q))
+        score = lax.dot_general(q, k_ref[:, start:stop], NT, preferred_element_type=F32)
+        shift = jnp.sum(jnp.where(lanes == step * heads_step + a, lse_ref[...], 0.0), axis=1, keepdims=True) * log2e
+        value = jnp.exp2(score * scale - shift)
+        total = value if total is None else total + value
+
+    @pl.when(step == 0)
+    def _():
+        acc_ref[...] = total
+
+    @pl.when(step > 0)
+    def _():
+        acc_ref[...] += total
+
+    @pl.when(step == pl.num_programs(0) - 1)
+    def _():
+        out_ref[:, :keys] = acc_ref[...].astype(BF16)
+        cols = qi_ref.shape[1] // split
+        out_ref[:, keys : keys + cols] = qi_ref[:, pl.ds(pl.multiple_of(me_ref[0] * cols, LANES), cols)]
+        n = hw_ref.shape[1]
+        weight = hw_ref[...]
+        high = weight.astype(BF16)
+        rest = weight - high.astype(F32)
+        mid = rest.astype(BF16)
+        low = (rest - mid.astype(F32)).astype(BF16)
+        row = lax.broadcasted_iota(jnp.int32, (n, LANES), 0)
+        col = lax.broadcasted_iota(jnp.int32, (n, LANES), 1)
+        side = jnp.where(
+            lax.broadcasted_iota(jnp.int32, (rows, LANES), 1) == 3 * n, block_ref[0].astype(F32), 0.0
+        )
+        for e, term in enumerate((high, mid, low)):
+            place = jnp.where(col == row + e * n, 1.0, 0.0).astype(BF16)
+            side = side + jnp.dot(term, place, preferred_element_type=F32)
+        out_ref[:, keys + cols :] = side.astype(BF16)
+
+
+def rows_kernel(n_seq, n_head, own, me_ref, pos_ref, got_ref, *refs):
+    key_refs = refs[:n_seq]
+    gq_refs = refs[n_seq : n_seq + n_head]
+    near_ref, far_ref = refs[n_seq + n_head : n_seq + n_head + 2]
+    (keys_ref, q_ref, wide_ref, dots_ref, logit_ref, att_ref, valid_ref, dl_ref, gq_ref) = refs[n_seq + n_head + 2 :]
+    s, h = me_ref[0], me_ref[1]
+    keys, width = key_refs[0].shape
+    heads_all = q_ref.shape[0] // own
+    heads = heads_all // n_head
+    per = heads // n_seq
+    cols = per * width
+    group = n_head * own
+    for k in range(n_seq):
+        keys_ref[k] = key_refs[k][...]
+    for hh in range(n_head):
+        for ss in range(n_seq):
+            at = (ss * n_head + hh) * own
+            base = at // (2 * own) * 2 * own
+            both = got_ref[base : base + 2 * own, keys : keys + cols].astype(F32)
+            part = both[at - base : at - base + own]
+            tiles = [part[:, e * width : (e + 1) * width] for e in range(per)]
+            first = (hh * heads + ss * per) * own
+            q_ref[first : first + per * own, :] = jnp.concatenate(tiles, axis=0).astype(BF16)
+        at = hh * own
+        base = at // (2 * own) * 2 * own
+        side = got_ref[base : base + 2 * own, keys + cols :].astype(F32)[at - base : at - base + own]
+        for i in range(heads):
+            one = side[:, i : i + 1] + side[:, heads + i : heads + i + 1] + side[:, 2 * heads + i : 2 * heads + i + 1]
+            wide_ref[hh * heads + i] = jnp.broadcast_to(one, (own, LANES))
+    first_row = (s * n_head + h) * own
+    sub = lax.broadcasted_iota(jnp.int32, (own, keys), 0)
+    place = jnp.zeros((own, keys), F32)
+    for t in range(own):
+        place = jnp.where(sub == t, pos_ref[first_row + t].astype(F32), place)
+    lane = lax.broadcasted_iota(jnp.int32, (own, keys), 1).astype(F32)
+
+    def forward(k, peak):
+        dots = lax.dot_general(q_ref[...], keys_ref[k], NT, preferred_element_type=F32)
+        dots_ref[k] = dots.astype(BF16)
+        cube = jnp.maximum(dots, 0.0).reshape(heads_all, own, keys)
+        parts = []
+        for c in range(keys // LANES):
+            parts.append(jnp.sum(cube[:, :, c * LANES : (c + 1) * LANES] * wide_ref[...], axis=0))
+        logit = jnp.concatenate(parts, axis=1)
+        src = pl.multiple_of((s ^ k) * group, group)
+        share = got_ref[pl.ds(src, group), :keys].astype(F32).reshape(n_head, own, keys)
+        side = got_ref[pl.ds(src, 2 * own), keys + cols :].astype(F32)
+        block = side[:own, 3 * heads : 3 * heads + 1]
+        valid = block * float(keys) + lane <= place
+        logit = jnp.where(valid, logit, -1e30)
+        logit_ref[k] = logit
+        att_ref[k] = jnp.where(valid, jnp.sum(share, axis=0), 0.0)
+        valid_ref[k] = jnp.where(valid, 1.0, 0.0)
+        return jnp.maximum(peak, jnp.max(logit, axis=1, keepdims=True))
+
+    peak = lax.fori_loop(0, n_seq, forward, jnp.full((own, 1), -1e30, F32))
+    valid = valid_ref[...] > 0.0
+    att = att_ref[...]
+    logit = logit_ref[...]
+
+    def row_sum(x):
+        return jnp.sum(jnp.sum(x, axis=0), axis=1, keepdims=True)
+
+    total = row_sum(att)
+    shifted = jnp.where(valid, jnp.exp(logit - peak[None]), 0.0)
+    norm = row_sum(shifted)
+    target = att / total[None]
+    log_prob = logit - peak[None] - jnp.log(norm)[None]
+    prob = jnp.where(valid, jnp.exp(log_prob), 0.0)
+    log_target = jnp.log(jnp.where(valid, att, 1.0)) - jnp.log(total)[None]
+    kl = row_sum(jnp.where(valid, target * (log_target - log_prob), 0.0))
+    dl = jnp.where(valid, prob - target, 0.0)
+    dl_ref[...] = jnp.concatenate([dl, dl], axis=1).astype(BF16)
+    wide = wide_ref[...].reshape(heads_all * own, LANES)
+    weighted = jnp.transpose(q_ref[...].astype(F32) * wide).astype(BF16)
+
+    def backward(k, _):
+        dots = dots_ref[k].astype(F32).reshape(heads_all // 2, 2 * own, keys)
+        one = dl_ref[k].astype(F32)[None]
+        gated = jnp.where(dots > 0.0, one, 0.0).reshape(heads_all * own, keys).astype(BF16)
+        term = jnp.dot(gated, keys_ref[k], preferred_element_type=F32)
+        gq_ref[...] = jnp.where(k == 0, 0.0, gq_ref[...]) + term
+        side = jnp.dot(weighted, gated, preferred_element_type=F32)
+
+        @pl.when(k % 2 == 0)
+        def _():
+            near_ref[k // 2] = side
+
+        @pl.when(k % 2 == 1)
+        def _():
+            far_ref[k // 2] = side.astype(BF16)
+
+        return 0
+
+    lax.fori_loop(0, n_seq, backward, 0)
+    lane = lax.broadcasted_iota(jnp.int32, (own, LANES), 1)
+    for m in range(n_head):
+        first = pl.multiple_of((h ^ m) * heads * own, heads * own)
+        term = gq_ref[pl.ds(first, heads * own), :]
+        factor = wide_ref[pl.ds((h ^ m) * heads, heads)]
+        query = q_ref[pl.ds(first, heads * own), :].astype(F32)
+        per_head = jnp.sum(term * query, axis=1, keepdims=True).reshape(heads, own, 1)
+        scaled = term.reshape(heads, own, width) * factor
+        extra = jnp.where(lane == heads, kl, 0.0)
+        for i in range(heads):
+            gq_refs[m][:, i * width : (i + 1) * width] = scaled[i].astype(BF16)
+            extra = jnp.where(lane == i, per_head[i], extra)
+        gq_refs[m][:, heads * width :] = extra.astype(BF16)
+
+
+def order_kernel(n_head, me_ref, *refs):
+    pieces, out_ref, cube_ref = refs[:n_head], refs[n_head], refs[n_head + 1]
+    h = me_ref[1]
+    for m in range(n_head):
+        cube_ref[h ^ m] = pieces[m][...].astype(F32)
+    out_ref[...] = cube_ref[...].reshape(out_ref.shape).astype(BF16)
+
+
+def place_kernel(n_seq, heads, me_ref, *refs):
+    pieces = refs[:n_seq]
+    kl_ref, gq_ref, hw_ref, side_ref = refs[n_seq:]
+    s = me_ref[0]
+    rows, cols = pieces[0].shape[0], gq_ref.shape[1]
+    for k in range(n_seq):
+        at = pl.ds(pl.multiple_of((s ^ k) * rows, rows), rows)
+        gq_ref[at, :] = pieces[k][:, :cols]
+        side_ref[at, :] = pieces[k][:, cols:].astype(F32)
+    side = side_ref[...]
+    hw_ref[...] = side[:, :heads].astype(BF16)
+    kl_ref[...] = jnp.transpose(side)[heads : heads + 1, :].astype(BF16)
+
+
+def turn_kernel(a_ref, b_ref, out_ref):
+    out_ref[...] = jnp.transpose(a_ref[...] + b_ref[...].astype(F32)).astype(BF16)
+
+
+def fast_local(n_seq, n_head, query_mla, key_mla, lse, query_index, key_index, head_weight, query_pos, key_block):
+    rows, keys = query_mla.shape[0], key_mla.shape[0]
+    mla_heads = lse.shape[1]
+    mla_width = query_mla.shape[1] // mla_heads
+    heads, width = head_weight.shape[1], key_index.shape[1]
+    own = rows // (n_seq * n_head)
+    heads_all = heads * n_head
+    s, h = lax.axis_index("seq"), lax.axis_index("head")
+    me = jnp.stack([s, h]).astype(jnp.int32)
+
+    def swap(x, axis, n, mask):
+        return lax.ppermute(x, axis, [(i, i ^ mask) for i in range(n)])
+
+    key_pieces = {0: key_index}
+    for k in range(2, n_seq, 2):
+        key_pieces[k] = swap(key_index, "seq", n_seq, k)
+    for k in range(0, n_seq, 2):
+        key_pieces[k + 1] = swap(key_pieces[k], "seq", n_seq, 1)
+
+    heads_step = 4
+    cols = query_index.shape[1] // n_seq
+    whole = lambda i: (0, 0)
+    sent = pl.pallas_call(
+        functools.partial(attention_kernel, heads_step, mla_width, n_seq),
+        grid=(mla_heads // heads_step,),
+        in_specs=[
+            smem_spec(),
+            smem_spec(),
+            pl.BlockSpec((rows, heads_step * mla_width), lambda i: (0, i)),
+            pl.BlockSpec((keys, heads_step * mla_width), lambda i: (0, i)),
+            pl.BlockSpec(lse.shape, whole),
+            pl.BlockSpec(query_index.shape, whole),
+            pl.BlockSpec(head_weight.shape, whole),
+        ],
+        out_specs=pl.BlockSpec((rows, keys + cols + LANES), whole),
+        out_shape=jax.ShapeDtypeStruct((rows, keys + cols + LANES), BF16),
+        scratch_shapes=[pltpu.VMEM((rows, keys), F32)],
+        compiler_params=pltpu.CompilerParams(vmem_limit_bytes=32 * 2**20),
+        cost_estimate=pl.CostEstimate(
+            flops=2 * rows * keys * mla_heads * mla_width,
+            bytes_accessed=2 * (rows + keys) * mla_heads * mla_width,
+            transcendentals=rows * keys * mla_heads,
+        ),
+        name="attention",
+    )(me, key_block, query_mla, key_mla, lse, query_index, head_weight)
+    got = lax.all_to_all(sent, ("seq", "head"), 0, 0, tiled=True)
+
+    wide_cols = heads * width + LANES
+    half = n_seq // 2
+    outs = pl.pallas_call(
+        functools.partial(rows_kernel, n_seq, n_head, own),
+        in_specs=[smem_spec(), smem_spec()] + [vmem_spec()] * (1 + n_seq),
+        out_specs=[vmem_spec()] * (n_head + 2),
+        out_shape=[jax.ShapeDtypeStruct((own, wide_cols), BF16)] * n_head
+        + [
+            jax.ShapeDtypeStruct((half, width, keys), F32),
+            jax.ShapeDtypeStruct((half, width, keys), BF16),
+        ],
+        scratch_shapes=[
+            pltpu.VMEM((n_seq, keys, width), BF16),
+            pltpu.VMEM((heads_all * own, width), BF16),
+            pltpu.VMEM((heads_all, own, LANES), F32),
+            pltpu.VMEM((n_seq, heads_all * own, keys), BF16),
+            pltpu.VMEM((n_seq, own, keys), F32),
+            pltpu.VMEM((n_seq, own, keys), F32),
+            pltpu.VMEM((n_seq, own, keys), F32),
+            pltpu.VMEM((n_seq, 2 * own, keys), BF16),
+            pltpu.VMEM((heads_all * own, width), F32),
+        ],
+        compiler_params=pltpu.CompilerParams(vmem_limit_bytes=40 * 2**20),
+        cost_estimate=pl.CostEstimate(
+            flops=6 * own * heads_all * n_seq * keys * width, bytes_accessed=2**21, transcendentals=0
+        ),
+        name="rows",
+    )(me, query_pos, got, *[key_pieces[k] for k in range(n_seq)])
+    pieces, near, far = outs[:n_head], outs[n_head], outs[n_head + 1]
+
+    paired = near + swap(far, "seq", n_seq, 1).astype(F32)
+    mine = paired[0]
+    for e in range(1, half):
+        mine = mine + swap(paired[e].astype(BF16), "seq", n_seq, 2 * e).astype(F32)
+    steps = bits(n_head)
+    for mask in steps[:-1]:
+        mine = mine + swap(mine.astype(BF16), "head", n_head, mask).astype(F32)
+    last = swap(mine.astype(BF16), "head", n_head, steps[-1])
+    grad_key_index = pl.pallas_call(
+        turn_kernel,
+        in_specs=[vmem_spec()] * 2,
+        out_specs=vmem_spec(),
+        out_shape=jax.ShapeDtypeStruct((keys, width), BF16),
+        name="turn",
+    )(mine, last)
+
+    row_pieces = [pieces[0]] + [swap(pieces[m], "head", n_head, m) for m in range(1, n_head)]
+    ordered = pl.pallas_call(
+        functools.partial(order_kernel, n_head),
+        in_specs=[smem_spec()] + [vmem_spec()] * n_head,
+        out_specs=vmem_spec(),
+        out_shape=jax.ShapeDtypeStruct((n_head * own, wide_cols), BF16),
+        scratch_shapes=[pltpu.VMEM((n_head, own, wide_cols), F32)],
+        name="order",
+    )(me, *row_pieces)
+    all_rows = {0: ordered}
+    for k in range(2, n_seq, 2):
+        all_rows[k] = swap(ordered, "seq", n_seq, k)
+    for k in range(0, n_seq, 2):
+        all_rows[k + 1] = swap(all_rows[k], "seq", n_seq, 1)
+    kl, grad_query_index, grad_head_weight = pl.pallas_call(
+        functools.partial(place_kernel, n_seq, heads),
+        in_specs=[smem_spec()] + [vmem_spec()] * n_seq,
+        out_specs=[vmem_spec()] * 3,
+        out_shape=[
+            jax.ShapeDtypeStruct((1, rows), BF16),
+            jax.ShapeDtypeStruct((rows, heads * width), BF16),
+            jax.ShapeDtypeStruct((rows, heads), BF16),
+        ],
+        scratch_shapes=[pltpu.VMEM((rows, LANES), F32)],
+        name="place",
+    )(me, *[all_rows[k] for k in range(n_seq)])
+    return kl.reshape(rows), grad_query_index, grad_head_weight, grad_key_index
+
+
+def plain_local(query_mla, key_mla, lse, query_index, key_index, head_weight, query_pos, key_block):
     row_count = query_mla.shape[0]
     key_count = key_mla.shape[0]
     mla_heads = lse.shape[1]
@@ -68,6 +398,14 @@
         P(),
         P("seq"),
     )
+    n_seq, n_head = mesh.shape["seq"], mesh.shape["head"]
+
+    def local(*args):
+        rows, heads = args[0].shape[0], args[5].shape[1]
+        if rows == 8 * n_seq * n_head and heads % n_seq == 0:
+            return fast_local(n_seq, n_head, *args)
+        return plain_local(*args)
+
     return jax.shard_map(
         local,
         mesh=mesh,

time: 197 us -> 85.4 us (0.43)
  blocking collectives: 71.2 us -> 0 us
  waiting for transfers between devices: 57.3 us -> 21.3 us
  starting transfers between devices: 0.08 us -> 27.4 us
  Pallas kernels: 0 us -> 20.6 us
  matrix products: 17.6 us -> 0 us
  other arithmetic: 18 us -> 2.36 us
  between operations: 14.9 us -> 1.5 us
  local copies, waits for them, and re-layouts: 17 us -> 11.8 us
    psum x3 -> x0, blocking collectives: 57.4 us -> none  [the longest x1 23.2 us: local(): lax.psum((query_part, weight_part, kl_part), 'seq')]
    psum x2 -> x0, waiting for transfers between devices: 57.2 us -> none  [the longest x1 50.4 us: local(): attention, logit = lax.psum((attention_part, logit_part), 'head')]
    ppermute x0 -> x23, waiting for transfers between devices: none -> 21.3 us  [swap(): return lax.ppermute(x, axis, [(i, i ^ mask) for i in range(n)])]
    pallas_call x0 -> x5, Pallas kernels: none -> 20.6 us  [the longest x1 7.46 us: fast_local(): pl.pallas_call(functools.partial(attention_kernel, heads_step, mla_width,...]
    ppermute x0 -> x23, starting transfers between devices: none -> 20.1 us  [swap(): return lax.ppermute(x, axis, [(i, i ^ mask) for i in range(n)])]
    dot_general x4 -> x0, matrix products: 17.6 us -> none  [the longest x1 7.19 us: local(): jnp.einsum('thd,jhd->htj', queries, mla_keys, preferred_element_type=jnp....]
    pmax x1 -> x0, blocking collectives: 13.8 us -> none  [local(): peak = lax.pmax(local_peak, 'seq')]
    all_to_all x0 -> x1, starting transfers between devices: none -> 7.3 us  [fast_local(): got = lax.all_to_all(sent, ('seq', 'head'), 0, 0, tiled=True)]
  transfers between devices with their start and end apart: 2 -> 24, of which waited for: 2 -> 11; matrix products, arithmetic and copies ran while one was open for 6% -> 4% of each run, Pallas kernels for 0% -> 5%
where the time goes in v1:
time: 85.4 us; the launch traced here: 84.9 us
  starting transfers between devices  27.4 us (32%)
  waiting for transfers between devices  21.3 us (25%)
  Pallas kernels  20.6 us (24%)
  local copies, waits for them, and re-layouts  11.8 us (14%)
  other arithmetic  2.36 us (3%)
  between operations  1.5 us (2%)
    ppermute x23, waiting for transfers between devices, swap(): return lax.ppermute(x, axis, [(i, i ^ mask) for i in range(n)])  21.3 us
    ppermute x23, starting transfers between devices, swap(): return lax.ppermute(x, axis, [(i, i ^ mask) for i in range(n)])  20.1 us
    unnamed x39, local copies, waits for them, and re-layouts  11.8 us
    pallas_call x1, Pallas kernels, fast_local(): pl.pallas_call(functools.partial(attention_kernel, heads_step, mla_width,...  7.46 us
    pallas_call x1, Pallas kernels, fast_local(): pl.pallas_call(functools.partial(rows_kernel, n_seq, n_head, own), in_spe...  7.46 us
    all_to_all x1, starting transfers between devices, fast_local(): got = lax.all_to_all(sent, ('seq', 'head'), 0, 0, tiled=True)  7.3 us
    pallas_call x1, Pallas kernels, fast_local(): pl.pallas_call(functools.partial(place_kernel, n_seq, heads), in_specs=[s...  2.38 us
    pallas_call x1, Pallas kernels, fast_local(): pl.pallas_call(turn_kernel, in_specs=[vmem_spec()] * 2, out_specs=vmem_sp...  1.74 us
  transfers between devices with their start and end apart: 24, of which 11 were waited for; matrix products, arithmetic and copies ran while one was open for 4% of the time, Pallas kernels for 5%

profile of v1, /device:TPU:0, one launch (start us, length us, event | category | flops | bytes accessed | tf_op | source)
XLA Modules:
  0.0 84.9 jit_solution(4229192161568800874)
XLA Ops:
  0.7 0.9 %copy.12.lse_ref = f32[256,32]{1,0:T(8,128)S(1)} copy(f32[256,32]{0,1:T(8,128)} %param.10) | data formatting | bytes 65536 | tf_op args[2]
  1.5 0.8 copy.13.hw_ref
  3.0 0.1 pad_add_fusion.me_ref
  3.1 2.8 %copy-done = bf16[512,6144]{1,0:T(8,128)(2,1)S(1)} copy-done((bf16[512,6144]{1,0:T(8,128)(2,1)S(1)}, bf16[512,6144]{1,0:T(8,128)(2,1)}, u32[]{:S(2)}) %copy-start) | copy-done | bytes 6291480
  5.9 1.9 %copy-done.1 = bf16[256,6144]{1,0:T(8,128)(2,1)S(1)} copy-done((bf16[256,6144]{1,0:T(8,128)(2,1)S(1)}, bf16[256,6144]{1,0:T(8,128)(2,1)}, u32[]{:S(2)}) %copy-start.1) | copy-done | bytes 3145752
  7.8 1.2 %copy-done.2 = bf16[256,2048]{1,0:T(8,128)(2,1)S(1)} copy-done((bf16[256,2048]{1,0:T(8,128)(2,1)S(1)}, bf16[256,2048]{1,0:T(8,128)(2,1)}, u32[]{:S(2)}) %copy-start.2) | copy-done | bytes 1048600
  9.0 7.5 %attention.1 = bf16[256,896]{1,0:T(8,128)(2,1)} custom-call(s32[2]{0:T(128)S(1)} %pad_add_fusion.me_ref, s32[1]{0:T(128)S(6)} %copy.15.block_ref, bf16[256,6144]{1,0:T(8,128)(2,1)S(1)} %copy-done.1, bf16[512,6144]{1,0:T(8,128)(2,1)S(1)} %copy-done, f32[256,32]{1,0:T(8,128)S(1)} %copy.12.lse_ref, bf16[256,2048]{1,0:T(8,128)(2,1)S(1)} %copy-done.2, ...), custom_call_target="tpu_custom_call" | custom-call | flops 1610612736 | bytes 9437184 | tf_op jit(solution)/shard_map/attention/pallas_call | solution.py:237
  16.5 7.3 %all-to-all-start = ((bf16[32,8,896]{2,1,0:T(8,128)(2,1)}), bf16[32,8,896]{2,1,0:T(8,128)(2,1)S(1)}, u32[]{:S(2)}, u32[]{:S(2)}) async-start(bf16[32,8,896]{2,1,0:T(8,128)(2,1)} %bitcast.2), calls=%async_computation | async-start | bytes 917504 | tf_op jit(solution)/shard_map/all_to_all | solution.py:260
  23.8 1.8 %collective-permute-start.1 = (bf16[512,128]{1,0:T(8,128)(2,1)S(1)}, bf16[512,128]{1,0:T(8,128)(2,1)S(1)}, u32[]{:S(2)}, u32[]{:S(2)}) collective-permute-start(bf16[512,128]{1,0:T(8,128)(2,1)S(1)} %copy-done.5), channel_id=1, source_target_pairs={{0,2},{1,3},{2,0},{3,1},{4,6},{5,7},{6,4},{7,5},{8,10},{9,11},{10,... | collective-permute-start | bytes 393224 | tf_op jit(solution)/shard_map/ppermute | solution.py:226
  25.6 1.5 %collective-permute-start.3 = (bf16[512,128]{1,0:T(8,128)(2,1)S(1)}, bf16[512,128]{1,0:T(8,128)(2,1)S(1)}, u32[]{:S(2)}, u32[]{:S(2)}) collective-permute-start(bf16[512,128]{1,0:T(8,128)(2,1)S(1)} %copy-done.5), channel_id=1, source_target_pairs={{0,4},{1,5},{2,6},{3,7},{4,0},{5,1},{6,2},{7,3},{8,12},{9,13},{10,... | collective-permute-start | bytes 393224 | tf_op jit(solution)/shard_map/ppermute | solution.py:226
  27.1 0.3 collective-permute-start.5
  27.3 6.0 %collective-permute-done.1.refs_2_ = bf16[512,128]{1,0:T(8,128)(2,1)S(1)} collective-permute-done((bf16[512,128]{1,0:T(8,128)(2,1)S(1)}, bf16[512,128]{1,0:T(8,128)(2,1)S(1)}, u32[]{:S(2)}, u32[]{:S(2)}) %collective-permute-start.1) | collective-permute-done | bytes 131104 | tf_op jit(solution)/shard_map/ppermute | solution.py:226
  33.4 0.5 collective-permute-done.3.refs_4_
  33.9 4.2 %collective-permute-done.5.refs_6_ = bf16[512,128]{1,0:T(8,128)(2,1)S(1)} collective-permute-done((bf16[512,128]{1,0:T(8,128)(2,1)S(1)}, bf16[512,128]{1,0:T(8,128)(2,1)S(1)}, u32[]{:S(2)}, u32[]{:S(2)}) %collective-permute-start.5) | collective-permute-done | bytes 131104 | tf_op jit(solution)/shard_map/ppermute | solution.py:226
  38.2 1.3 %collective-permute-done.6.refs_7_ = bf16[512,128]{1,0:T(8,128)(2,1)S(1)} collective-permute-done((bf16[512,128]{1,0:T(8,128)(2,1)S(1)}, bf16[512,128]{1,0:T(8,128)(2,1)S(1)}, u32[]{:S(2)}, u32[]{:S(2)}) %collective-permute-start.6) | collective-permute-done | bytes 131104 | tf_op jit(solution)/shard_map/ppermute | solution.py:226
  39.5 7.5 %rows.1 = (bf16[8,2176]{1,0:T(8,128)(2,1)S(1)}, bf16[8,2176]{1,0:T(8,128)(2,1)S(1)}, bf16[8,2176]{1,0:T(8,128)(2,1)S(1)}, bf16[8,2176]{1,0:T(8,128)(2,1)S(1)}, f...) custom-call(s32[2]{0:T(128)S(1)} %pad_add_fusion.me_ref, s32[256]{0:T(256)S(1)} %copy-done.6, ...), custom_call_target="tpu_custom_call" | custom-call | flops 1610612736 | bytes 2097152 | tf_op jit(solution)/shard_map/rows/pallas_call | solution.py:264
  47.0 0.2 collective-permute-start.17
  47.2 1.8 %collective-permute-done.17 = bf16[4,128,512]{2,1,0:T(8,128)(2,1)S(1)} collective-permute-done((bf16[4,128,512]{2,1,0:T(8,128)(2,1)S(1)}, bf16[4,128,512]{2,1,0:T(8,128)(2,1)S(1)}, u32[]{:S(2)}, u32[]{:S(2)}) %collective-permute-start.17) | collective-permute-done | bytes 524320 | tf_op jit(solution)/shard_map/ppermute | solution.py:226
  49.0 0.2 fusion.5
  49.2 0.5 collective-permute-start.18
  49.8 0.3 collective-permute-start.19
  50.1 2.7 %collective-permute-start.20 = (bf16[128,512]{1,0:T(8,128)(2,1)S(1)}, bf16[128,512]{1,0:T(8,128)(2,1)S(1)}, u32[]{:S(2)}, u32[]{:S(2)}) collective-permute-start(bf16[128,512]{1,0:T(8,128)(2,1)S(1)} %get-tuple-element.31), channel_id=1, source_target_pairs={{0,6},{1,7},{2,4},{3,5},{4,2},{5,3},{6,0},{7,1},{8,14},{9,15},{10,... | collective-permute-start | bytes 393224 | tf_op jit(solution)/shard_map/ppermute | solution.py:226
  52.8 1.4 %collective-permute-start.7 = (bf16[8,2176]{1,0:T(8,128)(2,1)S(1)}, bf16[8,2176]{1,0:T(8,128)(2,1)S(1)}, u32[]{:S(2)}, u32[]{:S(2)}) collective-permute-start(bf16[8,2176]{1,0:T(8,128)(2,1)S(1)} %get-tuple-element.14), channel_id=1, source_target_pairs={{0,8},{8,0},{16,24},{24,16},{1,9},{9,1},{17,25},{25,17},{2,10},{10... | collective-permute-start | bytes 104456 | tf_op jit(solution)/shard_map/ppermute | solution.py:226
  54.2 2.5 %collective-permute-start.8 = (bf16[8,2176]{1,0:T(8,128)(2,1)S(1)}, bf16[8,2176]{1,0:T(8,128)(2,1)S(1)}, u32[]{:S(2)}, u32[]{:S(2)}) collective-permute-start(bf16[8,2176]{1,0:T(8,128)(2,1)S(1)} %get-tuple-element.15), channel_id=1, source_target_pairs={{0,16},{8,24},{16,0},{24,8},{1,17},{9,25},{17,1},{25,9},{2,18},{10... | collective-permute-start | bytes 104456 | tf_op jit(solution)/shard_map/ppermute | solution.py:226
  56.7 3.3 %collective-permute-start.9 = (bf16[8,2176]{1,0:T(8,128)(2,1)S(1)}, bf16[8,2176]{1,0:T(8,128)(2,1)S(1)}, u32[]{:S(2)}, u32[]{:S(2)}) collective-permute-start(bf16[8,2176]{1,0:T(8,128)(2,1)S(1)} %get-tuple-element.16), channel_id=1, source_target_pairs={{0,24},{8,16},{16,8},{24,0},{1,25},{9,17},{17,9},{25,1},{2,26},{10... | collective-permute-start | bytes 104456 | tf_op jit(solution)/shard_map/ppermute | solution.py:226
  60.1 2.4 %collective-permute-done.9.refs_3_ = bf16[8,2176]{1,0:T(8,128)(2,1)S(1)} collective-permute-done((bf16[8,2176]{1,0:T(8,128)(2,1)S(1)}, bf16[8,2176]{1,0:T(8,128)(2,1)S(1)}, u32[]{:S(2)}, u32[]{:S(2)}) %collective-permute-start.9) | collective-permute-done | bytes 34848 | tf_op jit(solution)/shard_map/ppermute | solution.py:226
  62.5 0.6 copy-done.17
  63.1 1.5 %order.1.refs_0_ = bf16[32,2176]{1,0:T(8,128)(2,1)} custom-call(s32[2]{0:T(128)} %copy-done.4, bf16[8,2176]{1,0:T(8,128)(2,1)} %copy-done.3, bf16[8,2176]{1,0:T(8,128)(2,1)} %copy-done.15, bf16[8,2176]{1,0:T(8,128)(2,1)} %copy-done.16, bf16[8,2176]{1,0:T(8,128)(2,1)} %copy-done.17), custom_call_target="tpu_custom_call" | custom-call | tf_op jit(solution)/shard_map/order/pallas_call | solution.py:309
  64.6 0.7 collective-permute-start.11
  65.3 0.5 collective-permute-start.13
  65.8 2.3 %collective-permute-start.15 = (bf16[32,2176]{1,0:T(8,128)(2,1)}, bf16[32,2176]{1,0:T(8,128)(2,1)S(1)}, u32[]{:S(2)}, u32[]{:S(2)}) collective-permute-start(bf16[32,2176]{1,0:T(8,128)(2,1)} %order.1.refs_0_), channel_id=1, source_target_pairs={{0,6},{1,7},{2,4},{3,5},{4,2},{5,3},{6,0},{7,1},{8,14},{9,15},{10,... | collective-permute-start | bytes 417800 | tf_op jit(solution)/shard_map/ppermute | solution.py:226
  68.1 0.1 fusion.3
  68.2 0.1 collective-permute-start.21
  68.3 0.1 collective-permute-start.10
  68.3 1.5 %collective-permute-done.11.refs_2_ = bf16[32,2176]{1,0:T(8,128)(2,1)S(1)} collective-permute-done((bf16[32,2176]{1,0:T(8,128)(2,1)}, bf16[32,2176]{1,0:T(8,128)(2,1)S(1)}, u32[]{:S(2)}, u32[]{:S(2)}) %collective-permute-start.11) | collective-permute-done | bytes 139296 | tf_op jit(solution)/shard_map/ppermute | solution.py:226
  69.9 0.7 collective-permute-done.13.refs_4_
  70.6 1.5 %collective-permute-done.15.refs_6_ = bf16[32,2176]{1,0:T(8,128)(2,1)S(1)} collective-permute-done((bf16[32,2176]{1,0:T(8,128)(2,1)}, bf16[32,2176]{1,0:T(8,128)(2,1)S(1)}, u32[]{:S(2)}, u32[]{:S(2)}) %collective-permute-start.15) | collective-permute-done | bytes 139296 | tf_op jit(solution)/shard_map/ppermute | solution.py:226
  72.0 1.2 %collective-permute-done.21 = bf16[128,512]{1,0:T(8,128)(2,1)S(1)} collective-permute-done((bf16[128,512]{1,0:T(8,128)(2,1)S(1)}, bf16[128,512]{1,0:T(8,128)(2,1)S(1)}, u32[]{:S(2)}, u32[]{:S(2)}) %collective-permute-start.21) | collective-permute-done | bytes 131104 | tf_op jit(solution)/shard_map/ppermute | solution.py:226
  73.2 0.8 fusion.4
  74.0 1.9 %collective-permute-start.22 = (bf16[128,512]{1,0:T(8,128)(2,1)S(1)}, bf16[128,512]{1,0:T(8,128)(2,1)S(1)}, u32[]{:S(2)}, u32[]{:S(2)}) collective-permute-start(bf16[128,512]{1,0:T(8,128)(2,1)S(1)} %get-tuple-element.26), channel_id=1, source_target_pairs={{0,16},{8,24},{16,0},{24,8},{1,17},{9,25},{17,1},{25,9},{2,18},{10... | collective-permute-start | bytes 393224 | tf_op jit(solution)/shard_map/ppermute | solution.py:226
  75.9 0.6 copy-done.10
  76.6 0.7 copy-done.13
  77.3 2.4 %place.1 = (bf16[1,256]{1,0:T(2,128)(2,1)}, bf16[256,2048]{1,0:T(8,128)(2,1)}, bf16[256,16]{1,0:T(8,128)(2,1)}) custom-call(s32[2]{0:T(128)} %copy-done.4, bf16[32,2176]{1,0:T(8,128)(2,1)} %order.1.refs_0_, bf16[32,2176]{1,0:T(8,128)(2,1)} %copy-done.10, bf16[32,2176]{1,0:T(8,128)(2,1)} %copy-done.7, bf16[32,2176]{1,0:T(8,128)(2,1)} %copy-done.11, ...), custom_call_target="tpu_custom_call" | custom-call | tf_op jit(solution)/shard_map/place/pallas_call | solution.py:322
  79.7 1.5 %copy.14 = bf16[256,16]{0,1:T(8,128)(2,1)} copy(bf16[256,16]{1,0:T(8,128)(2,1)} %get-tuple-element.24) | data formatting | bytes 16384
  81.2 1.2 %reduce = bf16[256]{0:T(256)(128)(2,1)} reduce(bf16[1,256]{1,0:T(2,128)(2,1)} %get-tuple-element.17, bf16[]{:T(256)} %constant.9), dimensions={0}, to_apply=%get-tuple-element.17.reduce_sub_computation | reduce | bytes 1026 | tf_op jit(solution)/shard_map/place/pallas_call | solution.py:322
  82.4 0.1 collective-permute-done.22.b_ref
  82.5 0.7 copy-done.14
  83.1 1.7 %turn.1 = bf16[512,128]{1,0:T(8,128)(2,1)} custom-call(f32[128,512]{1,0:T(8,128)} %get-tuple-element.27.a_ref, bf16[128,512]{1,0:T(8,128)(2,1)} %copy-done.14), custom_call_target="tpu_custom_call" | custom-call | tf_op jit(solution)/shard_map/turn/pallas_call | solution.py:300
  (50 shorter events, 0.3 us)
Async XLA Ops:
  0.6 23.1 %copy-start.5 = (bf16[512,128]{1,0:T(8,128)(2,1)S(1)}, bf16[512,128]{1,0:T(8,128)(2,1)}, u32[]{:S(2)}) copy-start(bf16[512,128]{1,0:T(8,128)(2,1)} %refs_0_.1) | copy-start | bytes 393220
  0.6 38.8 %copy-start.6 = (s32[256]{0:T(256)S(1)}, s32[256]{0:T(256)}, u32[]{:S(2)}) copy-start(s32[256]{0:T(256)} %pos_ref.1) | copy-start | bytes 3076
  3.1 2.8 %copy-start = (bf16[512,6144]{1,0:T(8,128)(2,1)S(1)}, bf16[512,6144]{1,0:T(8,128)(2,1)}, u32[]{:S(2)}) copy-start(bf16[512,6144]{1,0:T(8,128)(2,1)} %k_ref.1) | copy-start | bytes 18874372
  5.9 1.9 %copy-start.1 = (bf16[256,6144]{1,0:T(8,128)(2,1)S(1)}, bf16[256,6144]{1,0:T(8,128)(2,1)}, u32[]{:S(2)}) copy-start(bf16[256,6144]{1,0:T(8,128)(2,1)} %q_ref.1) | copy-start | bytes 9437188
  7.8 1.2 %copy-start.2 = (bf16[256,2048]{1,0:T(8,128)(2,1)S(1)}, bf16[256,2048]{1,0:T(8,128)(2,1)}, u32[]{:S(2)}) copy-start(bf16[256,2048]{1,0:T(8,128)(2,1)} %qi_ref.1) | copy-start | bytes 3145732
  9.0 38.0 %copy-start.4 = (s32[2]{0:T(128)}, s32[2]{0:T(128)S(1)}, u32[]{:S(2)}) copy-start(s32[2]{0:T(128)S(1)} %pad_add_fusion.me_ref) | copy-start | bytes 28
  16.5 23.0 %all-to-all-start = ((bf16[32,8,896]{2,1,0:T(8,128)(2,1)}), bf16[32,8,896]{2,1,0:T(8,128)(2,1)S(1)}, u32[]{:S(2)}, u32[]{:S(2)}) async-start(bf16[32,8,896]{2,1,0:T(8,128)(2,1)} %bitcast.2), calls=%async_computation | async-start | bytes 917504 | tf_op jit(solution)/shard_map/all_to_all | solution.py:260
  23.8 9.6 %collective-permute-start.1 = (bf16[512,128]{1,0:T(8,128)(2,1)S(1)}, bf16[512,128]{1,0:T(8,128)(2,1)S(1)}, u32[]{:S(2)}, u32[]{:S(2)}) collective-permute-start(bf16[512,128]{1,0:T(8,128)(2,1)S(1)} %copy-done.5), channel_id=1, source_target_pairs={{0,2},{1,3},{2,0},{3,1},{4,6},{5,7},{6,4},{7,5},{8,10},{9,11},{10,... | collective-permute-start | bytes 393224 | tf_op jit(solution)/shard_map/ppermute | solution.py:226
  25.6 8.3 %collective-permute-start.3 = (bf16[512,128]{1,0:T(8,128)(2,1)S(1)}, bf16[512,128]{1,0:T(8,128)(2,1)S(1)}, u32[]{:S(2)}, u32[]{:S(2)}) collective-permute-start(bf16[512,128]{1,0:T(8,128)(2,1)S(1)} %copy-done.5), channel_id=1, source_target_pairs={{0,4},{1,5},{2,6},{3,7},{4,0},{5,1},{6,2},{7,3},{8,12},{9,13},{10,... | collective-permute-start | bytes 393224 | tf_op jit(solution)/shard_map/ppermute | solution.py:226
  27.1 11.1 %collective-permute-start.5 = (bf16[512,128]{1,0:T(8,128)(2,1)S(1)}, bf16[512,128]{1,0:T(8,128)(2,1)S(1)}, u32[]{:S(2)}, u32[]{:S(2)}) collective-permute-start(bf16[512,128]{1,0:T(8,128)(2,1)S(1)} %copy-done.5), channel_id=1, source_target_pairs={{0,6},{1,7},{2,4},{3,5},{4,2},{5,3},{6,0},{7,1},{8,14},{9,15},{10,... | collective-permute-start | bytes 393224 | tf_op jit(solution)/shard_map/ppermute | solution.py:226
  27.3 10.8 %collective-permute-start = (bf16[512,128]{1,0:T(8,128)(2,1)S(1)}, bf16[512,128]{1,0:T(8,128)(2,1)S(1)}, u32[]{:S(2)}, u32[]{:S(2)}) collective-permute-start(bf16[512,128]{1,0:T(8,128)(2,1)S(1)} %copy-done.5), channel_id=1, source_target_pairs={{0,1},{1,0},{2,3},{3,2},{4,5},{5,4},{6,7},{7,6},{8,9},{9,8},{10,11... | collective-permute-start | bytes 393224 | tf_op jit(solution)/shard_map/ppermute | solution.py:226
  33.4 4.8 %collective-permute-start.2 = (bf16[512,128]{1,0:T(8,128)(2,1)S(1)}, bf16[512,128]{1,0:T(8,128)(2,1)S(1)}, u32[]{:S(2)}, u32[]{:S(2)}) collective-permute-start(bf16[512,128]{1,0:T(8,128)(2,1)S(1)} %collective-permute-done.1.refs_2_), channel_id=1, source_target_pairs={{0,1},{1,0},{2,3},{3,2},{4,5},{5,4},{6,7},{7,6},{8,9},{9,8},{10,11... | collective-permute-start | bytes 393224 | tf_op jit(solution)/shard_map/ppermute | solution.py:226
  33.9 4.2 %collective-permute-start.4 = (bf16[512,128]{1,0:T(8,128)(2,1)S(1)}, bf16[512,128]{1,0:T(8,128)(2,1)S(1)}, u32[]{:S(2)}, u32[]{:S(2)}) collective-permute-start(bf16[512,128]{1,0:T(8,128)(2,1)S(1)} %collective-permute-done.3.refs_4_), channel_id=1, source_target_pairs={{0,1},{1,0},{2,3},{3,2},{4,5},{5,4},{6,7},{7,6},{8,9},{9,8},{10,11... | collective-permute-start | bytes 393224 | tf_op jit(solution)/shard_map/ppermute | solution.py:226
  38.1 1.3 %collective-permute-start.6 = (bf16[512,128]{1,0:T(8,128)(2,1)S(1)}, bf16[512,128]{1,0:T(8,128)(2,1)S(1)}, u32[]{:S(2)}, u32[]{:S(2)}) collective-permute-start(bf16[512,128]{1,0:T(8,128)(2,1)S(1)} %collective-permute-done.5.refs_6_), channel_id=1, source_target_pairs={{0,1},{1,0},{2,3},{3,2},{4,5},{5,4},{6,7},{7,6},{8,9},{9,8},{10,11... | collective-permute-start | bytes 393224 | tf_op jit(solution)/shard_map/ppermute | solution.py:226
  47.0 2.2 %copy-start.3 = (bf16[8,2176]{1,0:T(8,128)(2,1)}, bf16[8,2176]{1,0:T(8,128)(2,1)S(1)}, u32[]{:S(2)}) copy-start(bf16[8,2176]{1,0:T(8,128)(2,1)S(1)} %get-tuple-element.13.refs_0_) | copy-start | bytes 104452
  47.0 2.0 %collective-permute-start.17 = (bf16[4,128,512]{2,1,0:T(8,128)(2,1)S(1)}, bf16[4,128,512]{2,1,0:T(8,128)(2,1)S(1)}, u32[]{:S(2)}, u32[]{:S(2)}) collective-permute-start(bf16[4,128,512]{2,1,0:T(8,128)(2,1)S(1)} %get-tuple-element.21), channel_id=1, source_target_pairs={{0,1},{1,0},{2,3},{3,2},{4,5},{5,4},{6,7},{7,6},{8,9},{9,8},{10,11... | collective-permute-start | bytes 1572872 | tf_op jit(solution)/shard_map/ppermute | solution.py:226
  49.2 16.6 %collective-permute-start.18 = (bf16[128,512]{1,0:T(8,128)(2,1)S(1)}, bf16[128,512]{1,0:T(8,128)(2,1)S(1)}, u32[]{:S(2)}, u32[]{:S(2)}) collective-permute-start(bf16[128,512]{1,0:T(8,128)(2,1)S(1)} %get-tuple-element.30), channel_id=1, source_target_pairs={{0,2},{1,3},{2,0},{3,1},{4,6},{5,7},{6,4},{7,5},{8,10},{9,11},{10,... | collective-permute-start | bytes 393224 | tf_op jit(solution)/shard_map/ppermute | solution.py:226
  49.8 18.3 %collective-permute-start.19 = (bf16[128,512]{1,0:T(8,128)(2,1)S(1)}, bf16[128,512]{1,0:T(8,128)(2,1)S(1)}, u32[]{:S(2)}, u32[]{:S(2)}) collective-permute-start(bf16[128,512]{1,0:T(8,128)(2,1)S(1)} %get-tuple-element.32), channel_id=1, source_target_pairs={{0,4},{1,5},{2,6},{3,7},{4,0},{5,1},{6,2},{7,3},{8,12},{9,13},{10,... | collective-permute-start | bytes 393224 | tf_op jit(solution)/shard_map/ppermute | solution.py:226
  50.1 18.1 %collective-permute-start.20 = (bf16[128,512]{1,0:T(8,128)(2,1)S(1)}, bf16[128,512]{1,0:T(8,128)(2,1)S(1)}, u32[]{:S(2)}, u32[]{:S(2)}) collective-permute-start(bf16[128,512]{1,0:T(8,128)(2,1)S(1)} %get-tuple-element.31), channel_id=1, source_target_pairs={{0,6},{1,7},{2,4},{3,5},{4,2},{5,3},{6,0},{7,1},{8,14},{9,15},{10,... | collective-permute-start | bytes 393224 | tf_op jit(solution)/shard_map/ppermute | solution.py:226
  52.8 3.9 %collective-permute-start.7 = (bf16[8,2176]{1,0:T(8,128)(2,1)S(1)}, bf16[8,2176]{1,0:T(8,128)(2,1)S(1)}, u32[]{:S(2)}, u32[]{:S(2)}) collective-permute-start(bf16[8,2176]{1,0:T(8,128)(2,1)S(1)} %get-tuple-element.14), channel_id=1, source_target_pairs={{0,8},{8,0},{16,24},{24,16},{1,9},{9,1},{17,25},{25,17},{2,10},{10... | collective-permute-start | bytes 104456 | tf_op jit(solution)/shard_map/ppermute | solution.py:226
  54.2 5.9 %collective-permute-start.8 = (bf16[8,2176]{1,0:T(8,128)(2,1)S(1)}, bf16[8,2176]{1,0:T(8,128)(2,1)S(1)}, u32[]{:S(2)}, u32[]{:S(2)}) collective-permute-start(bf16[8,2176]{1,0:T(8,128)(2,1)S(1)} %get-tuple-element.15), channel_id=1, source_target_pairs={{0,16},{8,24},{16,0},{24,8},{1,17},{9,25},{17,1},{25,9},{2,18},{10... | collective-permute-start | bytes 104456 | tf_op jit(solution)/shard_map/ppermute | solution.py:226
  56.7 5.7 %copy-start.15 = (bf16[8,2176]{1,0:T(8,128)(2,1)}, bf16[8,2176]{1,0:T(8,128)(2,1)S(1)}, u32[]{:S(2)}) copy-start(bf16[8,2176]{1,0:T(8,128)(2,1)S(1)} %collective-permute-done.7.refs_1_) | copy-start | bytes 104452
  56.7 5.7 %collective-permute-start.9 = (bf16[8,2176]{1,0:T(8,128)(2,1)S(1)}, bf16[8,2176]{1,0:T(8,128)(2,1)S(1)}, u32[]{:S(2)}, u32[]{:S(2)}) collective-permute-start(bf16[8,2176]{1,0:T(8,128)(2,1)S(1)} %get-tuple-element.16), channel_id=1, source_target_pairs={{0,24},{8,16},{16,8},{24,0},{1,25},{9,17},{17,9},{25,1},{2,26},{10... | collective-permute-start | bytes 104456 | tf_op jit(solution)/shard_map/ppermute | solution.py:226
  60.1 2.4 %copy-start.16 = (bf16[8,2176]{1,0:T(8,128)(2,1)}, bf16[8,2176]{1,0:T(8,128)(2,1)S(1)}, u32[]{:S(2)}) copy-start(bf16[8,2176]{1,0:T(8,128)(2,1)S(1)} %collective-permute-done.8.refs_2_) | copy-start | bytes 104452
  62.5 0.6 copy-start.17
  64.6 5.3 %collective-permute-start.11 = (bf16[32,2176]{1,0:T(8,128)(2,1)}, bf16[32,2176]{1,0:T(8,128)(2,1)S(1)}, u32[]{:S(2)}, u32[]{:S(2)}) collective-permute-start(bf16[32,2176]{1,0:T(8,128)(2,1)} %order.1.refs_0_), channel_id=1, source_target_pairs={{0,2},{1,3},{2,0},{3,1},{4,6},{5,7},{6,4},{7,5},{8,10},{9,11},{10,... | collective-permute-start | bytes 417800 | tf_op jit(solution)/shard_map/ppermute | solution.py:226
  65.3 5.3 %collective-permute-start.13 = (bf16[32,2176]{1,0:T(8,128)(2,1)}, bf16[32,2176]{1,0:T(8,128)(2,1)S(1)}, u32[]{:S(2)}, u32[]{:S(2)}) collective-permute-start(bf16[32,2176]{1,0:T(8,128)(2,1)} %order.1.refs_0_), channel_id=1, source_target_pairs={{0,4},{1,5},{2,6},{3,7},{4,0},{5,1},{6,2},{7,3},{8,12},{9,13},{10,... | collective-permute-start | bytes 417800 | tf_op jit(solution)/shard_map/ppermute | solution.py:226
  65.8 6.2 %collective-permute-start.15 = (bf16[32,2176]{1,0:T(8,128)(2,1)}, bf16[32,2176]{1,0:T(8,128)(2,1)S(1)}, u32[]{:S(2)}, u32[]{:S(2)}) collective-permute-start(bf16[32,2176]{1,0:T(8,128)(2,1)} %order.1.refs_0_), channel_id=1, source_target_pairs={{0,6},{1,7},{2,4},{3,5},{4,2},{5,3},{6,0},{7,1},{8,14},{9,15},{10,... | collective-permute-start | bytes 417800 | tf_op jit(solution)/shard_map/ppermute | solution.py:226
  68.2 5.0 %collective-permute-start.21 = (bf16[128,512]{1,0:T(8,128)(2,1)S(1)}, bf16[128,512]{1,0:T(8,128)(2,1)S(1)}, u32[]{:S(2)}, u32[]{:S(2)}) collective-permute-start(bf16[128,512]{1,0:T(8,128)(2,1)S(1)} %fusion.3), channel_id=1, source_target_pairs={{0,8},{8,0},{16,24},{24,16},{1,9},{9,1},{17,25},{25,17},{2,10},{10... | collective-permute-start | bytes 393224 | tf_op jit(solution)/shard_map/ppermute | solution.py:226
  68.3 7.6 %collective-permute-start.10 = (bf16[32,2176]{1,0:T(8,128)(2,1)}, bf16[32,2176]{1,0:T(8,128)(2,1)S(1)}, u32[]{:S(2)}, u32[]{:S(2)}) collective-permute-start(bf16[32,2176]{1,0:T(8,128)(2,1)} %order.1.refs_0_), channel_id=1, source_target_pairs={{0,1},{1,0},{2,3},{3,2},{4,5},{5,4},{6,7},{7,6},{8,9},{9,8},{10,11... | collective-permute-start | bytes 417800 | tf_op jit(solution)/shard_map/ppermute | solution.py:226
  69.9 6.0 %copy-start.7 = (bf16[32,2176]{1,0:T(8,128)(2,1)}, bf16[32,2176]{1,0:T(8,128)(2,1)S(1)}, u32[]{:S(2)}) copy-start(bf16[32,2176]{1,0:T(8,128)(2,1)S(1)} %collective-permute-done.11.refs_2_) | copy-start | bytes 417796
  69.9 6.0 %collective-permute-start.12 = (bf16[32,2176]{1,0:T(8,128)(2,1)S(1)}, bf16[32,2176]{1,0:T(8,128)(2,1)S(1)}, u32[]{:S(2)}, u32[]{:S(2)}) collective-permute-start(bf16[32,2176]{1,0:T(8,128)(2,1)S(1)} %collective-permute-done.11.refs_2_), channel_id=1, source_target_pairs={{0,1},{1,0},{2,3},{3,2},{4,5},{5,4},{6,7},{7,6},{8,9},{9,8},{10,11... | collective-permute-start | bytes 417800 | tf_op jit(solution)/shard_map/ppermute | solution.py:226
  70.6 5.4 %copy-start.8 = (bf16[32,2176]{1,0:T(8,128)(2,1)}, bf16[32,2176]{1,0:T(8,128)(2,1)S(1)}, u32[]{:S(2)}) copy-start(bf16[32,2176]{1,0:T(8,128)(2,1)S(1)} %collective-permute-done.13.refs_4_) | copy-start | bytes 417796
  70.6 5.3 %collective-permute-start.14 = (bf16[32,2176]{1,0:T(8,128)(2,1)S(1)}, bf16[32,2176]{1,0:T(8,128)(2,1)S(1)}, u32[]{:S(2)}, u32[]{:S(2)}) collective-permute-start(bf16[32,2176]{1,0:T(8,128)(2,1)S(1)} %collective-permute-done.13.refs_4_), channel_id=1, source_target_pairs={{0,1},{1,0},{2,3},{3,2},{4,5},{5,4},{6,7},{7,6},{8,9},{9,8},{10,11... | collective-permute-start | bytes 417800 | tf_op jit(solution)/shard_map/ppermute | solution.py:226
  72.0 3.9 %copy-start.9 = (bf16[32,2176]{1,0:T(8,128)(2,1)}, bf16[32,2176]{1,0:T(8,128)(2,1)S(1)}, u32[]{:S(2)}) copy-start(bf16[32,2176]{1,0:T(8,128)(2,1)S(1)} %collective-permute-done.15.refs_6_) | copy-start | bytes 417796
  72.0 3.9 %collective-permute-start.16 = (bf16[32,2176]{1,0:T(8,128)(2,1)S(1)}, bf16[32,2176]{1,0:T(8,128)(2,1)S(1)}, u32[]{:S(2)}, u32[]{:S(2)}) collective-permute-start(bf16[32,2176]{1,0:T(8,128)(2,1)S(1)} %collective-permute-done.15.refs_6_), channel_id=1, source_target_pairs={{0,1},{1,0},{2,3},{3,2},{4,5},{5,4},{6,7},{7,6},{8,9},{9,8},{10,11... | collective-permute-start | bytes 417800 | tf_op jit(solution)/shard_map/ppermute | solution.py:226
  74.0 8.5 %collective-permute-start.22 = (bf16[128,512]{1,0:T(8,128)(2,1)S(1)}, bf16[128,512]{1,0:T(8,128)(2,1)S(1)}, u32[]{:S(2)}, u32[]{:S(2)}) collective-permute-start(bf16[128,512]{1,0:T(8,128)(2,1)S(1)} %get-tuple-element.26), channel_id=1, source_target_pairs={{0,16},{8,24},{16,0},{24,8},{1,17},{9,25},{17,1},{25,9},{2,18},{10... | collective-permute-start | bytes 393224 | tf_op jit(solution)/shard_map/ppermute | solution.py:226
  75.9 0.7 copy-start.10
  75.9 0.7 copy-start.11
  75.9 0.7 copy-start.12
  76.6 0.7 copy-start.13
  82.5 0.7 copy-start.14

commit v2 on v0

--- a/solution.py
+++ b/solution.py
@@ -1,10 +1,343 @@
+import functools
+import math
+
 import jax
 import jax.numpy as jnp
 from jax import lax
+from jax.experimental import pallas as pl
+from jax.experimental.pallas import tpu as pltpu
 from jax.sharding import PartitionSpec as P
 
-
-def local(query_mla, key_mla, lse, query_index, key_index, head_weight, query_pos, key_block):
+BF16 = jnp.bfloat16
+F32 = jnp.float32
+LANES = 128
+NT = (((1,), (1,)), ((), ()))
+
+
+def vmem_spec():
+    return pl.BlockSpec(memory_space=pltpu.VMEM)
+
+
+def smem_spec():
+    return pl.BlockSpec(memory_space=pltpu.SMEM)
+
+
+def head_parts(heads, width):
+    least = LANES // math.gcd(LANES, width)
+    first = heads // 2 // least * least
+    return [first, heads - first] if first > 0 else [heads]
+
+
+def bits(n):
+    return [1 << b for b in range(n.bit_length() - 1)]
+
+
+def attention_kernel(
+    parts, me_ref, block_ref, pos_hbm, q_hbm, k_hbm, lse_hbm, qi_hbm, hw_hbm, out_ref,
+    pos_ref, q_ref, k_ref, lse_ref, hw_ref, acc_ref, sems, part_sems
+):
+    rows, keys = q_ref.shape[0], k_ref.shape[0]
+    mla_heads, heads = lse_ref.shape[0], hw_ref.shape[0]
+    width = q_ref.shape[1] // mla_heads
+    cols = out_ref.shape[1] - keys - LANES
+    log2e = math.log2(math.e)
+    scale = width ** (-0.5) * log2e
+    small = [
+        pltpu.make_async_copy(source, target, sems.at[i])
+        for i, (source, target) in enumerate(((lse_hbm, lse_ref), (hw_hbm, hw_ref), (pos_hbm, pos_ref)))
+    ]
+    share_at = pl.ds(pl.multiple_of(me_ref[0] * cols, LANES), cols)
+    share_copy = pltpu.make_async_copy(qi_hbm.at[:, share_at], out_ref.at[:, keys : keys + cols], sems.at[3])
+    large = []
+    first = 0
+    for i, n in enumerate(parts):
+        at = slice(first * width, (first + n) * width)
+        large.append(
+            (
+                pltpu.make_async_copy(q_hbm.at[:, at], q_ref.at[:, at], part_sems.at[0, i]),
+                pltpu.make_async_copy(k_hbm.at[:, at], k_ref.at[:, at], part_sems.at[1, i]),
+            )
+        )
+        first += n
+    for copy in large[0]:
+        copy.start()
+    for copy in small:
+        copy.start()
+    for pair in large[1:]:
+        for copy in pair:
+            copy.start()
+    share_copy.start()
+    for copy in small:
+        copy.wait()
+    padded = jnp.concatenate([hw_ref[...], jnp.zeros((LANES - heads, rows), F32)], axis=0)
+    weight = jnp.transpose(padded)
+    high = weight.astype(BF16).astype(F32)
+    rest = weight - high
+    mid = rest.astype(BF16).astype(F32)
+    side = high + pltpu.roll(mid, heads, 1) + pltpu.roll(rest - mid, 2 * heads, 1)
+    out_ref[:, keys + cols :] = side.astype(BF16)
+    first = 0
+    for i, n in enumerate(parts):
+        for copy in large[i]:
+            copy.wait()
+        total = None
+        for a in range(first, first + n):
+            low, high = a * width, (a + 1) * width
+            start, stop = low // LANES * LANES, -(-high // LANES) * LANES
+            q = q_ref[:, start:stop]
+            if start != low or stop != high:
+                at = lax.broadcasted_iota(jnp.int32, (1, stop - start), 1) + start
+                q = jnp.where((at >= low) & (at < high), q, jnp.zeros_like(q))
+            score = lax.dot_general(k_ref[:, start:stop], q, NT, preferred_element_type=F32)
+            value = jnp.exp2(score * scale - lse_ref[a : a + 1, :] * log2e)
+            total = value if total is None else total + value
+        if first == 0:
+            acc_ref[...] = total
+        else:
+            acc_ref[...] += total
+        first += n
+    position = block_ref[0] * keys + lax.broadcasted_iota(jnp.int32, (keys, rows), 0)
+    share = jnp.where(position <= pos_ref[...], acc_ref[...], -1.0)
+    out_ref[:, :keys] = jnp.transpose(share).astype(BF16)
+    share_copy.wait()
+
+
+def keys_kernel(n_seq, n_head, own, me_ref, got_ref, *refs):
+    key_refs = refs[:n_seq]
+    near_ref, far_ref, gated_ref, q_ref, wide_ref, kl_ref, dots_ref, logit_ref = refs[n_seq:]
+    s = me_ref[0]
+    keys, width = key_refs[0].shape
+    heads_all = wide_ref.shape[0]
+    heads = heads_all // n_head
+    per = heads // n_seq
+    cols = per * width
+    group = n_head * own
+    for ss in range(n_seq):
+        for pair in range(0, n_head, 2):
+            at = ss * group + pair * own
+            both = got_ref[at : at + 2 * own, keys : keys + cols].astype(F32)
+            for e in range(2):
+                part = both[e * own : (e + 1) * own]
+                tiles = [part[:, i * width : (i + 1) * width] for i in range(per)]
+                first = ((pair + e) * heads + ss * per) * own
+                q_ref[first : first + per * own, :] = jnp.concatenate(tiles, axis=0).astype(BF16)
+    for pair in range(0, n_head, 2):
+        both = got_ref[pair * own : (pair + 2) * own, keys + cols :].astype(F32)
+        for e in range(2):
+            side = both[e * own : (e + 1) * own]
+            for i in range(heads):
+                one = side[:, i : i + 1] + side[:, heads + i : heads + i + 1] + side[:, 2 * heads + i : 2 * heads + i + 1]
+                wide_ref[(pair + e) * heads + i] = jnp.broadcast_to(one, (own, LANES))
+    for k in range(n_seq):
+        dots = lax.dot_general(q_ref[...], key_refs[k][...], NT, preferred_element_type=F32)
+        dots_ref[k] = dots.astype(BF16)
+        cube = jnp.maximum(dots, 0.0).reshape(heads_all, own, keys)
+        for c in range(0, keys, LANES):
+            logit_ref[k, :, c : c + LANES] = jnp.sum(cube[:, :, c : c + LANES] * wide_ref[...], axis=0)
+    shares, valids, logits = [], [], []
+    peak = jnp.full((own, 1), -1e30, F32)
+    for k in range(n_seq):
+        src = pl.multiple_of((s ^ k) * group, group)
+        cube = got_ref[pl.ds(src, group), :keys].astype(F32).reshape(n_head, own, keys)
+        valid = cube[0] >= 0.0
+        shares.append(jnp.where(valid, jnp.sum(cube, axis=0), 0.0))
+        valids.append(valid)
+        logits.append(jnp.where(valid, logit_ref[k], -1e30))
+        peak = jnp.maximum(peak, jnp.max(logits[k], axis=1, keepdims=True))
+
+    def row_sum(parts):
+        return jnp.sum(sum(parts[1:], parts[0]), axis=1, keepdims=True)
+
+    total = row_sum(shares)
+    norm = row_sum([jnp.where(v, jnp.exp(x - peak), 0.0) for v, x in zip(valids, logits)])
+    log_norm, log_total, inverse = jnp.log(norm), jnp.log(total), 1.0 / total
+    weighted = jnp.transpose(q_ref[...].astype(F32) * wide_ref[...].reshape(q_ref.shape)).astype(BF16)
+    kls = []
+    for k in range(n_seq):
+        target = shares[k] * inverse
+        log_prob = logits[k] - peak - log_norm
+        prob = jnp.where(valids[k], jnp.exp(log_prob), 0.0)
+        log_target = jnp.log(jnp.where(valids[k], shares[k], 1.0)) - log_total
+        kls.append(jnp.where(valids[k], target * (log_target - log_prob), 0.0))
+        dlogit = jnp.where(valids[k], prob - target, 0.0).astype(BF16).astype(F32)
+        cube = dots_ref[k].astype(F32).reshape(heads_all, own, keys)
+        gated = jnp.where(cube > 0.0, dlogit[None], 0.0).reshape(heads_all * own, keys).astype(BF16)
+        gated_ref[k] = gated
+        side = jnp.transpose(jnp.dot(weighted, gated, preferred_element_type=F32))
+        if k % 2 == 0:
+            near_ref[k // 2] = side
+        else:
+            far_ref[k // 2] = side.astype(BF16)
+    kl_ref[...] = jnp.broadcast_to(row_sum(kls), kl_ref.shape)
+
+
+def queries_kernel(n_seq, n_head, own, gated_ref, q_ref, wide_ref, kl_ref, *refs):
+    key_refs, out_ref = refs[:n_seq], refs[n_seq]
+    keys, width = key_refs[0].shape
+    heads_all = wide_ref.shape[0]
+    heads = heads_all // n_head
+    term = None
+    for k in range(n_seq):
+        part = jnp.dot(gated_ref[k], key_refs[k][...], preferred_element_type=F32)
+        term = part if term is None else term + part
+    per_head = jnp.sum((term * q_ref[...].astype(F32)).reshape(heads_all, own, width), axis=2, keepdims=True)
+    scaled = term.reshape(heads_all, own, width) * wide_ref[...]
+    lane = lax.broadcasted_iota(jnp.int32, (own, LANES), 1)
+    for pair in range(0, n_head, 2):
+        rows = slice(pair * own, (pair + 2) * own)
+        one, two = pair * heads, (pair + 1) * heads
+        first = second = jnp.where(lane == heads, kl_ref[...], 0.0)
+        for i in range(heads):
+            both = jnp.concatenate([scaled[one + i], scaled[two + i]], axis=0)
+            out_ref[rows, i * width : (i + 1) * width] = both.astype(BF16)
+            first = jnp.where(lane == i, per_head[one + i], first)
+            second = jnp.where(lane == i, per_head[two + i], second)
+        out_ref[rows, heads * width :] = jnp.concatenate([first, second], axis=0).astype(BF16)
+
+
+def place_kernel(n_seq, me_ref, *refs):
+    pieces = refs[:n_seq]
+    gq_ref, hw_ref, kl_ref, side_ref, sems = refs[n_seq:]
+    s = me_ref[0]
+    rows, cols = pieces[0].shape[0], gq_ref.shape[1]
+    heads = hw_ref.shape[0]
+    copies = []
+    for k in range(n_seq):
+        at = pl.ds(pl.multiple_of((s ^ k) * rows, rows), rows)
+        copies.append(pltpu.make_async_copy(pieces[k].at[:, :cols], gq_ref.at[at, :], sems.at[k]))
+        copies[k].start()
+        side_ref[at, :] = pieces[k][:, cols:].astype(F32)
+    side = jnp.transpose(side_ref[...])
+    hw_ref[...] = side[:heads, :].astype(BF16)
+    kl_ref[...] = side[heads, :].astype(BF16)
+    for copy in copies:
+        copy.wait()
+
+
+def fast_local(n_seq, n_head, query_mla, key_mla, lse, query_index, key_index, head_weight, query_pos, key_block):
+    rows, keys = query_mla.shape[0], key_mla.shape[0]
+    mla_heads = lse.shape[1]
+    mla_width = query_mla.shape[1] // mla_heads
+    heads, width = head_weight.shape[1], key_index.shape[1]
+    own = rows // (n_seq * n_head)
+    group = n_head * own
+    heads_all = heads * n_head
+    half = n_seq // 2
+    wide_cols = heads * width + LANES
+    me = jnp.stack([lax.axis_index("seq"), lax.axis_index("head")]).astype(jnp.int32)
+
+    def swap(x, axis, n, mask):
+        return lax.ppermute(x, axis, [(i, i ^ mask) for i in range(n)])
+
+    def limit(mib):
+        return pltpu.CompilerParams(vmem_limit_bytes=mib * 2**20)
+
+    cols = query_index.shape[1] // n_seq
+    parts = head_parts(mla_heads, mla_width)
+    hbm = pl.BlockSpec(memory_space=pltpu.HBM)
+    sent = pl.pallas_call(
+        functools.partial(attention_kernel, parts),
+        in_specs=[smem_spec()] * 2 + [hbm] * 6,
+        out_specs=vmem_spec(),
+        out_shape=jax.ShapeDtypeStruct((rows, keys + cols + LANES), BF16),
+        scratch_shapes=[
+            pltpu.VMEM((1, rows), jnp.int32),
+            pltpu.VMEM(query_mla.shape, BF16),
+            pltpu.VMEM(key_mla.shape, BF16),
+            pltpu.VMEM((mla_heads, rows), F32),
+            pltpu.VMEM((heads, rows), F32),
+            pltpu.VMEM((keys, rows), F32),
+            pltpu.SemaphoreType.DMA((4,)),
+            pltpu.SemaphoreType.DMA((2, len(parts))),
+        ],
+        compiler_params=limit(56),
+        cost_estimate=pl.CostEstimate(
+            flops=4 * rows * keys * mla_heads * mla_width,
+            bytes_accessed=2 * (rows + keys) * mla_heads * mla_width,
+            transcendentals=rows * keys * mla_heads,
+        ),
+        name="attention",
+    )(me, key_block, query_pos.reshape(1, rows), query_mla, key_mla, lse.T, query_index, head_weight.T)
+
+    near_keys = [key_index] + [swap(key_index, "seq", n_seq, k) for k in range(2, n_seq, 2)]
+    sent, *near_keys = lax.optimization_barrier((sent, *near_keys))
+    got = lax.all_to_all(sent, ("seq", "head"), 0, 0, tiled=True)
+    all_keys = []
+    for piece in near_keys:
+        all_keys += [piece, swap(piece, "seq", n_seq, 1)]
+
+    product = pl.CostEstimate(
+        flops=4 * own * heads_all * n_seq * keys * width, bytes_accessed=2**21, transcendentals=0
+    )
+    near, far, gated, queries, wide, kl_rows = pl.pallas_call(
+        functools.partial(keys_kernel, n_seq, n_head, own),
+        in_specs=[smem_spec()] + [vmem_spec()] * (1 + n_seq),
+        out_specs=[vmem_spec()] * 6,
+        out_shape=[
+            jax.ShapeDtypeStruct((half, keys, width), F32),
+            jax.ShapeDtypeStruct((half, keys, width), BF16),
+            jax.ShapeDtypeStruct((n_seq, heads_all * own, keys), BF16),
+            jax.ShapeDtypeStruct((heads_all * own, width), BF16),
+            jax.ShapeDtypeStruct((heads_all, own, LANES), F32),
+            jax.ShapeDtypeStruct((own, LANES), F32),
+        ],
+        scratch_shapes=[
+            pltpu.VMEM((n_seq, heads_all * own, keys), BF16),
+            pltpu.VMEM((n_seq, own, keys), F32),
+        ],
+        compiler_params=limit(20),
+        cost_estimate=product,
+        name="key_grad",
+    )(me, got, *all_keys)
+
+    far = swap(far, "seq", n_seq, 1)
+    paired = [near[e] + far[e].astype(F32) for e in range(half)]
+    sides = [x.astype(BF16) for x in paired[1:]]
+    gated, *sides = lax.optimization_barrier((gated, *sides))
+    mine = paired[0]
+    for e in range(1, half):
+        mine = mine + swap(sides[e - 1], "seq", n_seq, 2 * e).astype(F32)
+
+    rows_out = pl.pallas_call(
+        functools.partial(queries_kernel, n_seq, n_head, own),
+        in_specs=[vmem_spec()] * (4 + n_seq),
+        out_specs=vmem_spec(),
+        out_shape=jax.ShapeDtypeStruct((group, wide_cols), BF16),
+        compiler_params=limit(16),
+        cost_estimate=product,
+        name="query_grad",
+    )(gated, queries, wide, kl_rows, *all_keys)
+    own_rows = lax.all_to_all(rows_out, "head", 0, 0, tiled=True)
+    own_rows, _ = lax.optimization_barrier((own_rows, mine))
+    steps = bits(n_head)
+    for mask in steps[:-1]:
+        mine = mine + swap(mine.astype(BF16), "head", n_head, mask).astype(F32)
+    last = swap(mine.astype(BF16), "head", n_head, steps[-1])
+
+    all_rows = {0: own_rows}
+    for k in range(2, n_seq, 2):
+        all_rows[k] = swap(all_rows[0], "seq", n_seq, k)
+    for k in range(0, n_seq, 2):
+        all_rows[k + 1] = swap(all_rows[k], "seq", n_seq, 1)
+    grad_query_index, hw, kl = pl.pallas_call(
+        functools.partial(place_kernel, n_seq),
+        in_specs=[smem_spec()] + [vmem_spec()] * n_seq,
+        out_specs=[pl.BlockSpec(memory_space=pl.ANY), vmem_spec(), vmem_spec()],
+        out_shape=[
+            jax.ShapeDtypeStruct((rows, heads * width), BF16),
+            jax.ShapeDtypeStruct((heads, rows), BF16),
+            jax.ShapeDtypeStruct((rows,), BF16),
+        ],
+        scratch_shapes=[pltpu.VMEM((rows, LANES), F32), pltpu.SemaphoreType.DMA((n_seq,))],
+        compiler_params=limit(4),
+        cost_estimate=pl.CostEstimate(flops=0, bytes_accessed=8 * rows * wide_cols, transcendentals=0),
+        name="place",
+    )(me, *[all_rows[k] for k in range(n_seq)])
+    grad_key_index = (mine + last.astype(F32)).astype(BF16)
+    return kl, grad_query_index, hw.T, grad_key_index
+
+
+def plain_local(query_mla, key_mla, lse, query_index, key_index, head_weight, query_pos, key_block):
     row_count = query_mla.shape[0]
     key_count = key_mla.shape[0]
     mla_heads = lse.shape[1]
@@ -68,6 +401,14 @@
         P(),
         P("seq"),
     )
+    n_seq, n_head = mesh.shape["seq"], mesh.shape["head"]
+
+    def local(*args):
+        rows, heads = args[0].shape[0], args[5].shape[1]
+        if rows == 8 * n_seq * n_head and heads % n_seq == 0:
+            return fast_local(n_seq, n_head, *args)
+        return plain_local(*args)
+
     return jax.shard_map(
         local,
         mesh=mesh,

time: 197 us -> 67.7 us (0.34)
  blocking collectives: 71.2 us -> 0 us
  waiting for transfers between devices: 57.3 us -> 23.2 us
  starting transfers between devices: 0.08 us -> 26 us
  matrix products: 17.6 us -> 0 us
  local copies, waits for them, and re-layouts: 17 us -> 0.01 us
  other arithmetic: 18 us -> 1.48 us
  Pallas kernels: 0 us -> 15.3 us
  between operations: 14.9 us -> 1.4 us
    psum x3 -> x0, blocking collectives: 57.4 us -> none  [the longest x1 23.2 us: local(): lax.psum((query_part, weight_part, kl_part), 'seq')]
    psum x2 -> x0, waiting for transfers between devices: 57.2 us -> none  [the longest x1 50.4 us: local(): attention, logit = lax.psum((attention_part, logit_part), 'head')]
    dot_general x4 -> x0, matrix products: 17.6 us -> none  [the longest x1 7.19 us: local(): jnp.einsum('thd,jhd->htj', queries, mla_keys, preferred_element_type=jnp....]
    ppermute x0 -> x20, starting transfers between devices: none -> 16.4 us  [swap(): return lax.ppermute(x, axis, [(i, i ^ mask) for i in range(n)])]
    pallas_call x0 -> x4, Pallas kernels: none -> 15.3 us  [the longest x1 7.22 us: fast_local(): pl.pallas_call(functools.partial(attention_kernel, parts), in_specs=[smem...]
    all_to_all x0 -> x2, waiting for transfers between devices: none -> 15.1 us  [the longest x1 10.9 us: fast_local(): got = lax.all_to_all(sent, ('seq', 'head'), 0, 0, tiled=True)]
    pmax x1 -> x0, blocking collectives: 13.8 us -> none  [local(): peak = lax.pmax(local_peak, 'seq')]
    unnamed x17 -> x4, local copies, waits for them, and re-layouts: 13.5 us -> 0.01 us
  transfers between devices with their start and end apart: 2 -> 22, of which waited for: 2 -> 12; matrix products, arithmetic and copies ran while one was open for 6% -> 2% of each run, Pallas kernels for 0% -> 14%
where the time goes in v2:
time: 67.7 us; the launch traced here: 67.4 us
  starting transfers between devices  26 us (38%)
  waiting for transfers between devices  23.2 us (34%)
  Pallas kernels  15.3 us (23%)
  other arithmetic  1.48 us (2%)
  between operations  1.4 us (2%)
    ppermute x20, starting transfers between devices, swap(): return lax.ppermute(x, axis, [(i, i ^ mask) for i in range(n)])  16.4 us
    all_to_all x1, waiting for transfers between devices, fast_local(): got = lax.all_to_all(sent, ('seq', 'head'), 0, 0, tiled=True)  10.9 us
    ppermute x20, waiting for transfers between devices, swap(): return lax.ppermute(x, axis, [(i, i ^ mask) for i in range(n)])  8.13 us
    pallas_call x1, Pallas kernels, fast_local(): pl.pallas_call(functools.partial(attention_kernel, parts), in_specs=[smem...  7.22 us
    all_to_all x1, starting transfers between devices, fast_local(): got = lax.all_to_all(sent, ('seq', 'head'), 0, 0, tiled=True)  6.29 us
    all_to_all x1, waiting for transfers between devices, fast_local(): own_rows = lax.all_to_all(rows_out, 'head', 0, 0, tiled=True)  4.19 us
    pallas_call x1, Pallas kernels, fast_local(): pl.pallas_call(functools.partial(keys_kernel, n_seq, n_head, own), in_spe...  3.91 us
    all_to_all x1, starting transfers between devices, fast_local(): own_rows = lax.all_to_all(rows_out, 'head', 0, 0, tiled=True)  3.33 us
  transfers between devices with their start and end apart: 22, of which 12 were waited for; matrix products, arithmetic and copies ran while one was open for 2% of the time, Pallas kernels for 14%

profile of v2, /device:TPU:0, one launch (start us, length us, event | category | flops | bytes accessed | tf_op | source)
XLA Modules:
  0.0 67.4 jit_solution(5769813018230454085)
XLA Ops:
  0.6 3.0 %collective-permute-start.1 = (bf16[512,128]{1,0:T(8,128)(2,1)}, bf16[512,128]{1,0:T(8,128)(2,1)S(1)}, u32[]{:S(2)}, u32[]{:S(2)}) collective-permute-start(bf16[512,128]{1,0:T(8,128)(2,1)} %refs_0_.1), channel_id=1, source_target_pairs={{0,4},{1,5},{2,6},{3,7},{4,0},{5,1},{6,2},{7,3},{8,12},{9,13},{10,... | collective-permute-start | bytes 393224 | tf_op jit(solution)/shard_map/ppermute | solution.py:230
  3.7 1.5 %collective-permute-start = (bf16[512,128]{1,0:T(8,128)(2,1)}, bf16[512,128]{1,0:T(8,128)(2,1)S(1)}, u32[]{:S(2)}, u32[]{:S(2)}) collective-permute-start(bf16[512,128]{1,0:T(8,128)(2,1)} %refs_0_.1), channel_id=1, source_target_pairs={{0,2},{1,3},{2,0},{3,1},{4,6},{5,7},{6,4},{7,5},{8,10},{9,11},{10,... | collective-permute-start | bytes 393224 | tf_op jit(solution)/shard_map/ppermute | solution.py:230
  5.2 0.1 collective-permute-start.2
  5.9 0.6 pad_add_fusion.me_ref
  6.4 7.2 %attention.1 = bf16[256,896]{1,0:T(8,128)(2,1)} custom-call(s32[2]{0:T(128)} %pad_add_fusion.me_ref, s32[1]{0:T(128)S(6)} %copy.12.block_ref, s32[1,256]{1,0:T(1,128)} %bitcast.33, bf16[256,6144]{1,0:T(8,128)(2,1)} %q_hbm.1, bf16[512,6144]{1,0:T(8,128)(2,1)} %k_hbm.1, f32[32,256]{1,0:T(8,128)} %bitcast.30, bf16[256,2048]{1,0:T(8,128)(2,1)} %qi_hbm.1, ...), custom_call_target="tpu_custom_call" | custom-call | flops 3221225472 | bytes 9437184 | tf_op jit(solution)/shard_map/attention/pallas_call | solution.py:238
  13.7 0.0 collective-permute-done.1.refs_4_
  13.7 0.0 collective-permute-done.refs_2_
  13.7 0.0 collective-permute-done.2.refs_6_
  13.7 6.3 %all-to-all-start = ((bf16[32,8,896]{2,1,0:T(8,128)(2,1)}), bf16[32,8,896]{2,1,0:T(8,128)(2,1)S(1)}, u32[]{:S(2)}, u32[]{:S(2)}) async-start(bf16[32,8,896]{2,1,0:T(8,128)(2,1)} %bitcast.29), calls=%async_computation | async-start | bytes 917504 | tf_op jit(solution)/shard_map/all_to_all | solution.py:264
  20.0 0.3 collective-permute-start.3
  20.3 0.3 collective-permute-start.4
  20.6 0.3 collective-permute-start.5
  20.8 0.3 collective-permute-start.6
  21.1 0.3 collective-permute-done.3.refs_1_
  21.4 0.3 collective-permute-done.4.refs_3_
  21.7 0.3 collective-permute-done.5.refs_5_
  21.9 0.3 collective-permute-done.6.refs_7_
  22.2 10.9 %all-to-all-done = bf16[32,8,896]{2,1,0:T(8,128)(2,1)S(1)} async-done(((bf16[32,8,896]{2,1,0:T(8,128)(2,1)}), bf16[32,8,896]{2,1,0:T(8,128)(2,1)S(1)}, u32[]{:S(2)}, u32[]{:S(2)}) %all-to-all-start) | async-done | bytes 458784 | tf_op jit(solution)/shard_map/all_to_all | solution.py:264
  33.1 3.9 %key_grad.1 = (f32[4,512,128]{2,1,0:T(8,128)S(1)}, bf16[4,512,128]{2,1,0:T(8,128)(2,1)S(1)}, bf16[8,512,512]{2,1,0:T(8,128)(2,1)S(1)}, bf16[512,128]{1,0:T(8,128...) custom-call(s32[2]{0:T(128)S(1)} %copy-done.1, bf16[256,896]{1,0:T(8,128)(2,1)S(1)} %bitcast.28, ...), custom_call_target="tpu_custom_call" | custom-call | flops 1073741824 | bytes 2097152 | tf_op jit(solution)/shard_map/key_grad/pallas_call | solution.py:272
  37.0 1.1 %collective-permute-start.7 = (bf16[4,512,128]{2,1,0:T(8,128)(2,1)S(1)}, bf16[4,512,128]{2,1,0:T(8,128)(2,1)S(1)}, u32[]{:S(2)}, u32[]{:S(2)}) collective-permute-start(bf16[4,512,128]{2,1,0:T(8,128)(2,1)S(1)} %get-tuple-element.30), channel_id=1, source_target_pairs={{0,1},{1,0},{2,3},{3,2},{4,5},{5,4},{6,7},{7,6},{8,9},{9,8},{10,11... | collective-permute-start | bytes 1572872 | tf_op jit(solution)/shard_map/ppermute | solution.py:230
  38.2 1.5 %collective-permute-done.7 = bf16[4,512,128]{2,1,0:T(8,128)(2,1)S(1)} collective-permute-done((bf16[4,512,128]{2,1,0:T(8,128)(2,1)S(1)}, bf16[4,512,128]{2,1,0:T(8,128)(2,1)S(1)}, u32[]{:S(2)}, u32[]{:S(2)}) %collective-permute-start.7) | collective-permute-done | bytes 524320 | tf_op jit(solution)/shard_map/ppermute | solution.py:230
  39.7 0.1 fusion.5
  39.8 1.5 %collective-permute-start.8 = (bf16[512,128]{1,0:T(8,128)(2,1)S(1)}, bf16[512,128]{1,0:T(8,128)(2,1)S(1)}, u32[]{:S(2)}, u32[]{:S(2)}) collective-permute-start(bf16[512,128]{1,0:T(8,128)(2,1)S(1)} %get-tuple-element.35), channel_id=1, source_target_pairs={{0,2},{1,3},{2,0},{3,1},{4,6},{5,7},{6,4},{7,5},{8,10},{9,11},{10,... | collective-permute-start | bytes 393224 | tf_op jit(solution)/shard_map/ppermute | solution.py:230
  41.3 0.6 collective-permute-start.9
  41.9 1.5 %collective-permute-start.10 = (bf16[512,128]{1,0:T(8,128)(2,1)S(1)}, bf16[512,128]{1,0:T(8,128)(2,1)S(1)}, u32[]{:S(2)}, u32[]{:S(2)}) collective-permute-start(bf16[512,128]{1,0:T(8,128)(2,1)S(1)} %get-tuple-element.37), channel_id=1, source_target_pairs={{0,6},{1,7},{2,4},{3,5},{4,2},{5,3},{6,0},{7,1},{8,14},{9,15},{10,... | collective-permute-start | bytes 393224 | tf_op jit(solution)/shard_map/ppermute | solution.py:230
  43.4 2.0 %query_grad.1 = bf16[32,2176]{1,0:T(8,128)(2,1)} custom-call(bf16[8,512,512]{2,1,0:T(8,128)(2,1)S(1)} %get-tuple-element.31.gated_ref, bf16[512,128]{1,0:T(8,128)(2,1)S(1)} %get-tuple-element.32.q_ref, f32[64,8,128]{2,1,0:T(8,128)S(1)} %get-tuple-element.33.wide_ref, f32[8,128]{1,0:T(8,128)S(1)} %get-tuple-element.34.kl_ref, bf16[512,128]{1,0:T(8,128)(2,1)S(1)} %copy-done, ...), custom_call_target="tpu_custom_call" | custom-call | flops 1073741824 | bytes 2097152 | tf_op jit(solution)/shard_map/query_grad/pallas_call | solution.py:301
  45.3 3.3 %all-to-all-start.1 = ((bf16[4,8,2176]{2,1,0:T(8,128)(2,1)}), bf16[4,8,2176]{2,1,0:T(8,128)(2,1)S(1)}, u32[]{:S(2)}, u32[]{:S(2)}) async-start(bf16[4,8,2176]{2,1,0:T(8,128)(2,1)} %bitcast.10), calls=%async_computation.1 | async-start | bytes 278528 | tf_op jit(solution)/shard_map/all_to_all | solution.py:310
  48.7 0.0 collective-permute-done.8
  48.7 0.9 %collective-permute-done.9 = bf16[512,128]{1,0:T(8,128)(2,1)S(1)} collective-permute-done((bf16[512,128]{1,0:T(8,128)(2,1)S(1)}, bf16[512,128]{1,0:T(8,128)(2,1)S(1)}, u32[]{:S(2)}, u32[]{:S(2)}) %collective-permute-start.9) | collective-permute-done | bytes 131104 | tf_op jit(solution)/shard_map/ppermute | solution.py:230
  49.6 0.0 collective-permute-done.10
  49.6 0.1 fusion.6
  49.7 1.1 %collective-permute-start.18 = (bf16[512,128]{1,0:T(8,128)(2,1)S(1)}, bf16[512,128]{1,0:T(8,128)(2,1)S(1)}, u32[]{:S(2)}, u32[]{:S(2)}) collective-permute-start(bf16[512,128]{1,0:T(8,128)(2,1)S(1)} %get-tuple-element.42), channel_id=1, source_target_pairs={{0,8},{8,0},{16,24},{24,16},{1,9},{9,1},{17,25},{25,17},{2,10},{10... | collective-permute-start | bytes 393224 | tf_op jit(solution)/shard_map/ppermute | solution.py:230
  50.8 4.2 %all-to-all-done.1 = bf16[4,8,2176]{2,1,0:T(8,128)(2,1)S(1)} async-done(((bf16[4,8,2176]{2,1,0:T(8,128)(2,1)}), bf16[4,8,2176]{2,1,0:T(8,128)(2,1)S(1)}, u32[]{:S(2)}, u32[]{:S(2)}) %all-to-all-start.1) | async-done | bytes 139296 | tf_op jit(solution)/shard_map/all_to_all | solution.py:310
  55.0 1.5 %collective-permute-start.16 = (bf16[32,2176]{1,0:T(8,128)(2,1)S(1)}, bf16[32,2176]{1,0:T(8,128)(2,1)S(1)}, u32[]{:S(2)}, u32[]{:S(2)}) collective-permute-start(bf16[32,2176]{1,0:T(8,128)(2,1)S(1)} %bitcast.23), channel_id=1, source_target_pairs={{0,6},{1,7},{2,4},{3,5},{4,2},{5,3},{6,0},{7,1},{8,14},{9,15},{10,... | collective-permute-start | bytes 417800 | tf_op jit(solution)/shard_map/ppermute | solution.py:230
  56.5 1.5 %collective-permute-start.14 = (bf16[32,2176]{1,0:T(8,128)(2,1)S(1)}, bf16[32,2176]{1,0:T(8,128)(2,1)S(1)}, u32[]{:S(2)}, u32[]{:S(2)}) collective-permute-start(bf16[32,2176]{1,0:T(8,128)(2,1)S(1)} %bitcast.24), channel_id=1, source_target_pairs={{0,4},{1,5},{2,6},{3,7},{4,0},{5,1},{6,2},{7,3},{8,12},{9,13},{10,... | collective-permute-start | bytes 417800 | tf_op jit(solution)/shard_map/ppermute | solution.py:230
  57.9 0.6 collective-permute-start.12
  58.5 0.0 collective-permute-done.18
  58.5 1.4 %collective-permute-start.19 = (bf16[512,128]{1,0:T(8,128)(2,1)S(1)}, bf16[512,128]{1,0:T(8,128)(2,1)S(1)}, u32[]{:S(2)}, u32[]{:S(2)}) collective-permute-start(bf16[512,128]{1,0:T(8,128)(2,1)S(1)} %fusion.2), channel_id=1, source_target_pairs={{0,16},{8,24},{16,0},{24,8},{1,17},{9,25},{17,1},{25,9},{2,18},{10... | collective-permute-start | bytes 393224 | tf_op jit(solution)/shard_map/ppermute | solution.py:230
  59.9 0.0 collective-permute-start.11
  59.9 1.2 %collective-permute-done.16.refs_6_ = bf16[32,2176]{1,0:T(8,128)(2,1)S(1)} collective-permute-done((bf16[32,2176]{1,0:T(8,128)(2,1)S(1)}, bf16[32,2176]{1,0:T(8,128)(2,1)S(1)}, u32[]{:S(2)}, u32[]{:S(2)}) %collective-permute-start.16) | collective-permute-done | bytes 139296 | tf_op jit(solution)/shard_map/ppermute | solution.py:230
  61.1 0.0 collective-permute-start.17
  61.1 1.4 %collective-permute-done.14.refs_4_ = bf16[32,2176]{1,0:T(8,128)(2,1)S(1)} collective-permute-done((bf16[32,2176]{1,0:T(8,128)(2,1)S(1)}, bf16[32,2176]{1,0:T(8,128)(2,1)S(1)}, u32[]{:S(2)}, u32[]{:S(2)}) %collective-permute-start.14) | collective-permute-done | bytes 139296 | tf_op jit(solution)/shard_map/ppermute | solution.py:230
  62.5 0.0 collective-permute-start.15
  62.5 0.5 collective-permute-done.12.refs_2_
  63.0 1.5 %collective-permute-done.19 = bf16[512,128]{1,0:T(8,128)(2,1)S(1)} collective-permute-done((bf16[512,128]{1,0:T(8,128)(2,1)S(1)}, bf16[512,128]{1,0:T(8,128)(2,1)S(1)}, u32[]{:S(2)}, u32[]{:S(2)}) %collective-permute-start.19) | collective-permute-done | bytes 131104 | tf_op jit(solution)/shard_map/ppermute | solution.py:230
  64.5 0.7 %add_convert_fusion = bf16[512,128]{1,0:T(8,128)(2,1)} fusion(bf16[512,128]{1,0:T(8,128)(2,1)S(1)} %collective-permute-done.19, f32[512,128]{1,0:T(8,128)S(1)} %get-tuple-element.43, bf16[512,128]{1,0:T(8,128)(2,1)S(1)} %collective-permute-done.18), kind=kLoop, calls=%fused_computation.3 | loop fusion | flops 327680 | bytes 655360 | tf_op jit(solution)/shard_map/convert_element_type | solution.py:336
  65.2 0.0 collective-permute-done.13.refs_3_
  65.2 2.2 %place.1 = (bf16[256,2048]{1,0:T(8,128)(2,1)}, bf16[16,256]{1,0:T(8,128)(2,1)}, bf16[256]{0:T(256)(128)(2,1)}) custom-call(s32[2]{0:T(128)S(1)} %copy-done.1, bf16[32,2176]{1,0:T(8,128)(2,1)S(1)} %bitcast.27, bf16[32,2176]{1,0:T(8,128)(2,1)S(1)} %collective-permute-done.11.refs_1_, bf16[32,2176]{1,0:T(8,128)(2,1)S(1)} %collective-permute-done.12.refs_2_, ...), custom_call_target="tpu_custom_call" | custom-call | bytes 4456448 | tf_op jit(solution)/shard_map/place/pallas_call | solution.py:322
  (9 shorter events, 0.0 us)
Async XLA Ops:
  0.6 13.0 %collective-permute-start.1 = (bf16[512,128]{1,0:T(8,128)(2,1)}, bf16[512,128]{1,0:T(8,128)(2,1)S(1)}, u32[]{:S(2)}, u32[]{:S(2)}) collective-permute-start(bf16[512,128]{1,0:T(8,128)(2,1)} %refs_0_.1), channel_id=1, source_target_pairs={{0,4},{1,5},{2,6},{3,7},{4,0},{5,1},{6,2},{7,3},{8,12},{9,13},{10,... | collective-permute-start | bytes 393224 | tf_op jit(solution)/shard_map/ppermute | solution.py:230
  3.7 10.0 %collective-permute-start = (bf16[512,128]{1,0:T(8,128)(2,1)}, bf16[512,128]{1,0:T(8,128)(2,1)S(1)}, u32[]{:S(2)}, u32[]{:S(2)}) collective-permute-start(bf16[512,128]{1,0:T(8,128)(2,1)} %refs_0_.1), channel_id=1, source_target_pairs={{0,2},{1,3},{2,0},{3,1},{4,6},{5,7},{6,4},{7,5},{8,10},{9,11},{10,... | collective-permute-start | bytes 393224 | tf_op jit(solution)/shard_map/ppermute | solution.py:230
  5.2 8.5 %collective-permute-start.2 = (bf16[512,128]{1,0:T(8,128)(2,1)}, bf16[512,128]{1,0:T(8,128)(2,1)S(1)}, u32[]{:S(2)}, u32[]{:S(2)}) collective-permute-start(bf16[512,128]{1,0:T(8,128)(2,1)} %refs_0_.1), channel_id=1, source_target_pairs={{0,6},{1,7},{2,4},{3,5},{4,2},{5,3},{6,0},{7,1},{8,14},{9,15},{10,... | collective-permute-start | bytes 393224 | tf_op jit(solution)/shard_map/ppermute | solution.py:230
  6.4 13.6 %copy-start = (bf16[512,128]{1,0:T(8,128)(2,1)S(1)}, bf16[512,128]{1,0:T(8,128)(2,1)}, u32[]{:S(2)}) copy-start(bf16[512,128]{1,0:T(8,128)(2,1)} %refs_0_.1) | copy-start | bytes 393220
  6.4 26.7 %copy-start.1 = (s32[2]{0:T(128)S(1)}, s32[2]{0:T(128)}, u32[]{:S(2)}) copy-start(s32[2]{0:T(128)} %pad_add_fusion.me_ref) | copy-start | bytes 28
  13.7 19.4 %all-to-all-start = ((bf16[32,8,896]{2,1,0:T(8,128)(2,1)}), bf16[32,8,896]{2,1,0:T(8,128)(2,1)S(1)}, u32[]{:S(2)}, u32[]{:S(2)}) async-start(bf16[32,8,896]{2,1,0:T(8,128)(2,1)} %bitcast.29), calls=%async_computation | async-start | bytes 917504 | tf_op jit(solution)/shard_map/all_to_all | solution.py:264
  20.0 1.4 %collective-permute-start.3 = (bf16[512,128]{1,0:T(8,128)(2,1)S(1)}, bf16[512,128]{1,0:T(8,128)(2,1)S(1)}, u32[]{:S(2)}, u32[]{:S(2)}) collective-permute-start(bf16[512,128]{1,0:T(8,128)(2,1)S(1)} %copy-done), channel_id=1, source_target_pairs={{0,1},{1,0},{2,3},{3,2},{4,5},{5,4},{6,7},{7,6},{8,9},{9,8},{10,11... | collective-permute-start | bytes 393224 | tf_op jit(solution)/shard_map/ppermute | solution.py:230
  20.3 1.3 %collective-permute-start.4 = (bf16[512,128]{1,0:T(8,128)(2,1)S(1)}, bf16[512,128]{1,0:T(8,128)(2,1)S(1)}, u32[]{:S(2)}, u32[]{:S(2)}) collective-permute-start(bf16[512,128]{1,0:T(8,128)(2,1)S(1)} %collective-permute-done.refs_2_), channel_id=1, source_target_pairs={{0,1},{1,0},{2,3},{3,2},{4,5},{5,4},{6,7},{7,6},{8,9},{9,8},{10,11... | collective-permute-start | bytes 393224 | tf_op jit(solution)/shard_map/ppermute | solution.py:230
  20.6 1.3 %collective-permute-start.5 = (bf16[512,128]{1,0:T(8,128)(2,1)S(1)}, bf16[512,128]{1,0:T(8,128)(2,1)S(1)}, u32[]{:S(2)}, u32[]{:S(2)}) collective-permute-start(bf16[512,128]{1,0:T(8,128)(2,1)S(1)} %collective-permute-done.1.refs_4_), channel_id=1, source_target_pairs={{0,1},{1,0},{2,3},{3,2},{4,5},{5,4},{6,7},{7,6},{8,9},{9,8},{10,11... | collective-permute-start | bytes 393224 | tf_op jit(solution)/shard_map/ppermute | solution.py:230
  20.8 1.3 %collective-permute-start.6 = (bf16[512,128]{1,0:T(8,128)(2,1)S(1)}, bf16[512,128]{1,0:T(8,128)(2,1)S(1)}, u32[]{:S(2)}, u32[]{:S(2)}) collective-permute-start(bf16[512,128]{1,0:T(8,128)(2,1)S(1)} %collective-permute-done.2.refs_6_), channel_id=1, source_target_pairs={{0,1},{1,0},{2,3},{3,2},{4,5},{5,4},{6,7},{7,6},{8,9},{9,8},{10,11... | collective-permute-start | bytes 393224 | tf_op jit(solution)/shard_map/ppermute | solution.py:230
  37.0 2.7 %collective-permute-start.7 = (bf16[4,512,128]{2,1,0:T(8,128)(2,1)S(1)}, bf16[4,512,128]{2,1,0:T(8,128)(2,1)S(1)}, u32[]{:S(2)}, u32[]{:S(2)}) collective-permute-start(bf16[4,512,128]{2,1,0:T(8,128)(2,1)S(1)} %get-tuple-element.30), channel_id=1, source_target_pairs={{0,1},{1,0},{2,3},{3,2},{4,5},{5,4},{6,7},{7,6},{8,9},{9,8},{10,11... | collective-permute-start | bytes 1572872 | tf_op jit(solution)/shard_map/ppermute | solution.py:230
  39.8 8.9 %collective-permute-start.8 = (bf16[512,128]{1,0:T(8,128)(2,1)S(1)}, bf16[512,128]{1,0:T(8,128)(2,1)S(1)}, u32[]{:S(2)}, u32[]{:S(2)}) collective-permute-start(bf16[512,128]{1,0:T(8,128)(2,1)S(1)} %get-tuple-element.35), channel_id=1, source_target_pairs={{0,2},{1,3},{2,0},{3,1},{4,6},{5,7},{6,4},{7,5},{8,10},{9,11},{10,... | collective-permute-start | bytes 393224 | tf_op jit(solution)/shard_map/ppermute | solution.py:230
  41.3 8.3 %collective-permute-start.9 = (bf16[512,128]{1,0:T(8,128)(2,1)S(1)}, bf16[512,128]{1,0:T(8,128)(2,1)S(1)}, u32[]{:S(2)}, u32[]{:S(2)}) collective-permute-start(bf16[512,128]{1,0:T(8,128)(2,1)S(1)} %get-tuple-element.36), channel_id=1, source_target_pairs={{0,4},{1,5},{2,6},{3,7},{4,0},{5,1},{6,2},{7,3},{8,12},{9,13},{10,... | collective-permute-start | bytes 393224 | tf_op jit(solution)/shard_map/ppermute | solution.py:230
  41.9 7.7 %collective-permute-start.10 = (bf16[512,128]{1,0:T(8,128)(2,1)S(1)}, bf16[512,128]{1,0:T(8,128)(2,1)S(1)}, u32[]{:S(2)}, u32[]{:S(2)}) collective-permute-start(bf16[512,128]{1,0:T(8,128)(2,1)S(1)} %get-tuple-element.37), channel_id=1, source_target_pairs={{0,6},{1,7},{2,4},{3,5},{4,2},{5,3},{6,0},{7,1},{8,14},{9,15},{10,... | collective-permute-start | bytes 393224 | tf_op jit(solution)/shard_map/ppermute | solution.py:230
  45.3 9.7 %all-to-all-start.1 = ((bf16[4,8,2176]{2,1,0:T(8,128)(2,1)}), bf16[4,8,2176]{2,1,0:T(8,128)(2,1)S(1)}, u32[]{:S(2)}, u32[]{:S(2)}) async-start(bf16[4,8,2176]{2,1,0:T(8,128)(2,1)} %bitcast.10), calls=%async_computation.1 | async-start | bytes 278528 | tf_op jit(solution)/shard_map/all_to_all | solution.py:310
  49.7 8.8 %collective-permute-start.18 = (bf16[512,128]{1,0:T(8,128)(2,1)S(1)}, bf16[512,128]{1,0:T(8,128)(2,1)S(1)}, u32[]{:S(2)}, u32[]{:S(2)}) collective-permute-start(bf16[512,128]{1,0:T(8,128)(2,1)S(1)} %get-tuple-element.42), channel_id=1, source_target_pairs={{0,8},{8,0},{16,24},{24,16},{1,9},{9,1},{17,25},{25,17},{2,10},{10... | collective-permute-start | bytes 393224 | tf_op jit(solution)/shard_map/ppermute | solution.py:230
  55.0 6.1 %collective-permute-start.16 = (bf16[32,2176]{1,0:T(8,128)(2,1)S(1)}, bf16[32,2176]{1,0:T(8,128)(2,1)S(1)}, u32[]{:S(2)}, u32[]{:S(2)}) collective-permute-start(bf16[32,2176]{1,0:T(8,128)(2,1)S(1)} %bitcast.23), channel_id=1, source_target_pairs={{0,6},{1,7},{2,4},{3,5},{4,2},{5,3},{6,0},{7,1},{8,14},{9,15},{10,... | collective-permute-start | bytes 417800 | tf_op jit(solution)/shard_map/ppermute | solution.py:230
  56.5 6.0 %collective-permute-start.14 = (bf16[32,2176]{1,0:T(8,128)(2,1)S(1)}, bf16[32,2176]{1,0:T(8,128)(2,1)S(1)}, u32[]{:S(2)}, u32[]{:S(2)}) collective-permute-start(bf16[32,2176]{1,0:T(8,128)(2,1)S(1)} %bitcast.24), channel_id=1, source_target_pairs={{0,4},{1,5},{2,6},{3,7},{4,0},{5,1},{6,2},{7,3},{8,12},{9,13},{10,... | collective-permute-start | bytes 417800 | tf_op jit(solution)/shard_map/ppermute | solution.py:230
  57.9 5.1 %collective-permute-start.12 = (bf16[32,2176]{1,0:T(8,128)(2,1)S(1)}, bf16[32,2176]{1,0:T(8,128)(2,1)S(1)}, u32[]{:S(2)}, u32[]{:S(2)}) collective-permute-start(bf16[32,2176]{1,0:T(8,128)(2,1)S(1)} %bitcast.25), channel_id=1, source_target_pairs={{0,2},{1,3},{2,0},{3,1},{4,6},{5,7},{6,4},{7,5},{8,10},{9,11},{10,... | collective-permute-start | bytes 417800 | tf_op jit(solution)/shard_map/ppermute | solution.py:230
  58.5 5.9 %collective-permute-start.19 = (bf16[512,128]{1,0:T(8,128)(2,1)S(1)}, bf16[512,128]{1,0:T(8,128)(2,1)S(1)}, u32[]{:S(2)}, u32[]{:S(2)}) collective-permute-start(bf16[512,128]{1,0:T(8,128)(2,1)S(1)} %fusion.2), channel_id=1, source_target_pairs={{0,16},{8,24},{16,0},{24,8},{1,17},{9,25},{17,1},{25,9},{2,18},{10... | collective-permute-start | bytes 393224 | tf_op jit(solution)/shard_map/ppermute | solution.py:230
  59.9 5.3 %collective-permute-start.11 = (bf16[32,2176]{1,0:T(8,128)(2,1)S(1)}, bf16[32,2176]{1,0:T(8,128)(2,1)S(1)}, u32[]{:S(2)}, u32[]{:S(2)}) collective-permute-start(bf16[32,2176]{1,0:T(8,128)(2,1)S(1)} %bitcast.26), channel_id=1, source_target_pairs={{0,1},{1,0},{2,3},{3,2},{4,5},{5,4},{6,7},{7,6},{8,9},{9,8},{10,11... | collective-permute-start | bytes 417800 | tf_op jit(solution)/shard_map/ppermute | solution.py:230
  61.1 4.1 %collective-permute-start.17 = (bf16[32,2176]{1,0:T(8,128)(2,1)S(1)}, bf16[32,2176]{1,0:T(8,128)(2,1)S(1)}, u32[]{:S(2)}, u32[]{:S(2)}) collective-permute-start(bf16[32,2176]{1,0:T(8,128)(2,1)S(1)} %collective-permute-done.16.refs_6_), channel_id=1, source_target_pairs={{0,1},{1,0},{2,3},{3,2},{4,5},{5,4},{6,7},{7,6},{8,9},{9,8},{10,11... | collective-permute-start | bytes 417800 | tf_op jit(solution)/shard_map/ppermute | solution.py:230
  62.5 2.7 %collective-permute-start.15 = (bf16[32,2176]{1,0:T(8,128)(2,1)S(1)}, bf16[32,2176]{1,0:T(8,128)(2,1)S(1)}, u32[]{:S(2)}, u32[]{:S(2)}) collective-permute-start(bf16[32,2176]{1,0:T(8,128)(2,1)S(1)} %collective-permute-done.14.refs_4_), channel_id=1, source_target_pairs={{0,1},{1,0},{2,3},{3,2},{4,5},{5,4},{6,7},{7,6},{8,9},{9,8},{10,11... | collective-permute-start | bytes 417800 | tf_op jit(solution)/shard_map/ppermute | solution.py:230
  63.0 2.2 %collective-permute-start.13 = (bf16[32,2176]{1,0:T(8,128)(2,1)S(1)}, bf16[32,2176]{1,0:T(8,128)(2,1)S(1)}, u32[]{:S(2)}, u32[]{:S(2)}) collective-permute-start(bf16[32,2176]{1,0:T(8,128)(2,1)S(1)} %collective-permute-done.12.refs_2_), channel_id=1, source_target_pairs={{0,1},{1,0},{2,3},{3,2},{4,5},{5,4},{6,7},{7,6},{8,9},{9,8},{10,11... | collective-permute-start | bytes 417800 | tf_op jit(solution)/shard_map/ppermute | solution.py:230

commit v3 on v2

--- a/solution.py
+++ b/solution.py
@@ -33,7 +33,7 @@
 
 
 def attention_kernel(
-    parts, me_ref, block_ref, pos_hbm, q_hbm, k_hbm, lse_hbm, qi_hbm, hw_hbm, out_ref,
+    parts, block_ref, pos_hbm, q_hbm, k_hbm, lse_hbm, qi_hbm, hw_hbm, out_ref,
     pos_ref, q_ref, k_ref, lse_ref, hw_ref, acc_ref, sems, part_sems
 ):
     rows, keys = q_ref.shape[0], k_ref.shape[0]
@@ -46,7 +46,7 @@
         pltpu.make_async_copy(source, target, sems.at[i])
         for i, (source, target) in enumerate(((lse_hbm, lse_ref), (hw_hbm, hw_ref), (pos_hbm, pos_ref)))
     ]
-    share_at = pl.ds(pl.multiple_of(me_ref[0] * cols, LANES), cols)
+    share_at = pl.ds(pl.multiple_of(lax.axis_index("seq") * cols, LANES), cols)
     share_copy = pltpu.make_async_copy(qi_hbm.at[:, share_at], out_ref.at[:, keys : keys + cols], sems.at[3])
     large = []
     first = 0
@@ -102,10 +102,10 @@
     share_copy.wait()
 
 
-def keys_kernel(n_seq, n_head, own, me_ref, got_ref, *refs):
+def keys_kernel(n_seq, n_head, own, got_ref, *refs):
     key_refs = refs[:n_seq]
-    near_ref, far_ref, gated_ref, q_ref, wide_ref, kl_ref, dots_ref, logit_ref = refs[n_seq:]
-    s = me_ref[0]
+    far_ref, gated_ref, q_ref, wide_ref, kl_ref, weighted_ref, dots_ref, logit_ref = refs[n_seq:]
+    s = lax.axis_index("seq")
     keys, width = key_refs[0].shape
     heads_all = wide_ref.shape[0]
     heads = heads_all // n_head
@@ -152,6 +152,7 @@
     norm = row_sum([jnp.where(v, jnp.exp(x - peak), 0.0) for v, x in zip(valids, logits)])
     log_norm, log_total, inverse = jnp.log(norm), jnp.log(total), 1.0 / total
     weighted = jnp.transpose(q_ref[...].astype(F32) * wide_ref[...].reshape(q_ref.shape)).astype(BF16)
+    weighted_ref[...] = weighted
     kls = []
     for k in range(n_seq):
         target = shares[k] * inverse
@@ -163,23 +164,29 @@
         cube = dots_ref[k].astype(F32).reshape(heads_all, own, keys)
         gated = jnp.where(cube > 0.0, dlogit[None], 0.0).reshape(heads_all * own, keys).astype(BF16)
         gated_ref[k] = gated
-        side = jnp.transpose(jnp.dot(weighted, gated, preferred_element_type=F32))
+        if k % 2 == 1:
+            side = jnp.dot(weighted, gated, preferred_element_type=F32)
+            far_ref[k // 2] = jnp.transpose(side).astype(BF16)
+    kl_ref[...] = jnp.broadcast_to(row_sum(kls), kl_ref.shape)
+
+
+def products_kernel(n_seq, gated_ref, weighted_ref, *refs):
+    key_refs, near_ref, term_ref = refs[:n_seq], refs[n_seq], refs[n_seq + 1]
+    term = None
+    for k in range(n_seq):
         if k % 2 == 0:
-            near_ref[k // 2] = side
-        else:
-            far_ref[k // 2] = side.astype(BF16)
-    kl_ref[...] = jnp.broadcast_to(row_sum(kls), kl_ref.shape)
-
-
-def queries_kernel(n_seq, n_head, own, gated_ref, q_ref, wide_ref, kl_ref, *refs):
-    key_refs, out_ref = refs[:n_seq], refs[n_seq]
-    keys, width = key_refs[0].shape
+            side = jnp.dot(weighted_ref[...], gated_ref[k], preferred_element_type=F32)
+            near_ref[k // 2] = jnp.transpose(side)
+        part = jnp.dot(gated_ref[k], key_refs[k][...], preferred_element_type=F32)
+        term = part if term is None else term + part
+    term_ref[...] = term
+
+
+def queries_kernel(n_head, own, term_ref, q_ref, wide_ref, kl_ref, out_ref):
+    width = q_ref.shape[1]
     heads_all = wide_ref.shape[0]
     heads = heads_all // n_head
-    term = None
-    for k in range(n_seq):
-        part = jnp.dot(gated_ref[k], key_refs[k][...], preferred_element_type=F32)
-        term = part if term is None else term + part
+    term = term_ref[...]
     per_head = jnp.sum((term * q_ref[...].astype(F32)).reshape(heads_all, own, width), axis=2, keepdims=True)
     scaled = term.reshape(heads_all, own, width) * wide_ref[...]
     lane = lax.broadcasted_iota(jnp.int32, (own, LANES), 1)
@@ -195,10 +202,10 @@
         out_ref[rows, heads * width :] = jnp.concatenate([first, second], axis=0).astype(BF16)
 
 
-def place_kernel(n_seq, me_ref, *refs):
+def place_kernel(n_seq, *refs):
     pieces = refs[:n_seq]
     gq_ref, hw_ref, kl_ref, side_ref, sems = refs[n_seq:]
-    s = me_ref[0]
+    s = lax.axis_index("seq")
     rows, cols = pieces[0].shape[0], gq_ref.shape[1]
     heads = hw_ref.shape[0]
     copies = []
@@ -224,7 +231,6 @@
     heads_all = heads * n_head
     half = n_seq // 2
     wide_cols = heads * width + LANES
-    me = jnp.stack([lax.axis_index("seq"), lax.axis_index("head")]).astype(jnp.int32)
 
     def swap(x, axis, n, mask):
         return lax.ppermute(x, axis, [(i, i ^ mask) for i in range(n)])
@@ -237,7 +243,7 @@
     hbm = pl.BlockSpec(memory_space=pltpu.HBM)
     sent = pl.pallas_call(
         functools.partial(attention_kernel, parts),
-        in_specs=[smem_spec()] * 2 + [hbm] * 6,
+        in_specs=[smem_spec()] + [hbm] * 6,
         out_specs=vmem_spec(),
         out_shape=jax.ShapeDtypeStruct((rows, keys + cols + LANES), BF16),
         scratch_shapes=[
@@ -257,10 +263,11 @@
             transcendentals=rows * keys * mla_heads,
         ),
         name="attention",
-    )(me, key_block, query_pos.reshape(1, rows), query_mla, key_mla, lse.T, query_index, head_weight.T)
+    )(key_block, query_pos.reshape(1, rows), query_mla, key_mla, lse.T, query_index, head_weight.T)
 
     near_keys = [key_index] + [swap(key_index, "seq", n_seq, k) for k in range(2, n_seq, 2)]
-    sent, *near_keys = lax.optimization_barrier((sent, *near_keys))
+    sent, *held = lax.optimization_barrier((sent, *near_keys[:-1]))
+    near_keys = held + near_keys[-1:]
     got = lax.all_to_all(sent, ("seq", "head"), 0, 0, tiled=True)
     all_keys = []
     for piece in near_keys:
@@ -269,17 +276,17 @@
     product = pl.CostEstimate(
         flops=4 * own * heads_all * n_seq * keys * width, bytes_accessed=2**21, transcendentals=0
     )
-    near, far, gated, queries, wide, kl_rows = pl.pallas_call(
+    far, gated, queries, wide, kl_rows, weighted = pl.pallas_call(
         functools.partial(keys_kernel, n_seq, n_head, own),
-        in_specs=[smem_spec()] + [vmem_spec()] * (1 + n_seq),
+        in_specs=[vmem_spec()] * (1 + n_seq),
         out_specs=[vmem_spec()] * 6,
         out_shape=[
-            jax.ShapeDtypeStruct((half, keys, width), F32),
             jax.ShapeDtypeStruct((half, keys, width), BF16),
             jax.ShapeDtypeStruct((n_seq, heads_all * own, keys), BF16),
             jax.ShapeDtypeStruct((heads_all * own, width), BF16),
             jax.ShapeDtypeStruct((heads_all, own, LANES), F32),
             jax.ShapeDtypeStruct((own, LANES), F32),
+            jax.ShapeDtypeStruct((width, heads_all * own), BF16),
         ],
         scratch_shapes=[
             pltpu.VMEM((n_seq, heads_all * own, keys), BF16),
@@ -288,25 +295,37 @@
         compiler_params=limit(20),
         cost_estimate=product,
         name="key_grad",
-    )(me, got, *all_keys)
+    )(got, *all_keys)
 
     far = swap(far, "seq", n_seq, 1)
+    near, term = pl.pallas_call(
+        functools.partial(products_kernel, n_seq),
+        in_specs=[vmem_spec()] * (2 + n_seq),
+        out_specs=[vmem_spec()] * 2,
+        out_shape=[
+            jax.ShapeDtypeStruct((half, keys, width), F32),
+            jax.ShapeDtypeStruct((heads_all * own, width), F32),
+        ],
+        compiler_params=limit(16),
+        cost_estimate=product,
+        name="products",
+    )(gated, weighted, *all_keys)
     paired = [near[e] + far[e].astype(F32) for e in range(half)]
     sides = [x.astype(BF16) for x in paired[1:]]
-    gated, *sides = lax.optimization_barrier((gated, *sides))
+    term, *sides = lax.optimization_barrier((term, *sides))
     mine = paired[0]
     for e in range(1, half):
         mine = mine + swap(sides[e - 1], "seq", n_seq, 2 * e).astype(F32)
 
     rows_out = pl.pallas_call(
-        functools.partial(queries_kernel, n_seq, n_head, own),
-        in_specs=[vmem_spec()] * (4 + n_seq),
+        functools.partial(queries_kernel, n_head, own),
+        in_specs=[vmem_spec()] * 4,
         out_specs=vmem_spec(),
         out_shape=jax.ShapeDtypeStruct((group, wide_cols), BF16),
         compiler_params=limit(16),
-        cost_estimate=product,
+        cost_estimate=pl.CostEstimate(flops=0, bytes_accessed=2**21, transcendentals=0),
         name="query_grad",
-    )(gated, queries, wide, kl_rows, *all_keys)
+    )(term, queries, wide, kl_rows)
     own_rows = lax.all_to_all(rows_out, "head", 0, 0, tiled=True)
     own_rows, _ = lax.optimization_barrier((own_rows, mine))
     steps = bits(n_head)
@@ -321,7 +340,7 @@
         all_rows[k + 1] = swap(all_rows[k], "seq", n_seq, 1)
     grad_query_index, hw, kl = pl.pallas_call(
         functools.partial(place_kernel, n_seq),
-        in_specs=[smem_spec()] + [vmem_spec()] * n_seq,
+        in_specs=[vmem_spec()] * n_seq,
         out_specs=[pl.BlockSpec(memory_space=pl.ANY), vmem_spec(), vmem_spec()],
         out_shape=[
             jax.ShapeDtypeStruct((rows, heads * width), BF16),
@@ -332,7 +351,7 @@
         compiler_params=limit(4),
         cost_estimate=pl.CostEstimate(flops=0, bytes_accessed=8 * rows * wide_cols, transcendentals=0),
         name="place",
-    )(me, *[all_rows[k] for k in range(n_seq)])
+    )(*[all_rows[k] for k in range(n_seq)])
     grad_key_index = (mine + last.astype(F32)).astype(BF16)
     return kl, grad_query_index, hw.T, grad_key_index
 

time: 67.7 us -> 63.5 us (0.938)
  waiting for transfers between devices: 23.2 us -> 21.5 us
  Pallas kernels: 15.3 us -> 14.2 us
  starting transfers between devices: 26 us -> 25.2 us
    all_to_all x1, waiting for transfers between devices: 10.9 us -> 1.15 us  [fast_local(): got = lax.all_to_all(sent, ('seq', 'head'), 0, 0, tiled=True)]
    ppermute x20, waiting for transfers between devices: 8.13 us -> 16.6 us  [swap(): return lax.ppermute(x, axis, [(i, i ^ mask) for i in range(n)])]
    all_to_all x1, starting transfers between devices: 6.29 us -> 3.97 us  [fast_local(): got = lax.all_to_all(sent, ('seq', 'head'), 0, 0, tiled=True)]
    ppermute x20, starting transfers between devices: 16.4 us -> 17.9 us  [swap(): return lax.ppermute(x, axis, [(i, i ^ mask) for i in range(n)])]
    pallas_call x1, Pallas kernels: 7.22 us -> 6.46 us  [fast_local(): pl.pallas_call(functools.partial(attention_kernel, parts), in_specs=[smem...]
    pallas_call x2 -> x3, Pallas kernels: 4.16 us -> 4.07 us  [the longest x1 1.64 us: fast_local(): pl.pallas_call(functools.partial(place_kernel, n_seq), in_specs=[vmem_spe...]
  transfers between devices with their start and end apart: 22 -> 22, of which waited for: 12 -> 11; matrix products, arithmetic and copies ran while one was open for 2% -> 1% of each run, Pallas kernels for 14% -> 14%
where the time goes in v3:
time: 63.5 us; the launch traced here: 63.2 us
  starting transfers between devices  25.2 us (40%)
  waiting for transfers between devices  21.5 us (34%)
  Pallas kernels  14.2 us (22%)
  between operations  1.4 us (2%)
  other arithmetic  0.9 us (1%)
    ppermute x20, starting transfers between devices, swap(): return lax.ppermute(x, axis, [(i, i ^ mask) for i in range(n)])  17.9 us
    ppermute x20, waiting for transfers between devices, swap(): return lax.ppermute(x, axis, [(i, i ^ mask) for i in range(n)])  16.6 us
    pallas_call x1, Pallas kernels, fast_local(): pl.pallas_call(functools.partial(attention_kernel, parts), in_specs=[smem...  6.46 us
    all_to_all x1, starting transfers between devices, fast_local(): got = lax.all_to_all(sent, ('seq', 'head'), 0, 0, tiled=True)  3.97 us
    all_to_all x1, waiting for transfers between devices, fast_local(): own_rows = lax.all_to_all(rows_out, 'head', 0, 0, tiled=True)  3.75 us
    pallas_call x1, Pallas kernels, fast_local(): pl.pallas_call(functools.partial(keys_kernel, n_seq, n_head, own), in_spe...  3.64 us
    all_to_all x1, starting transfers between devices, fast_local(): own_rows = lax.all_to_all(rows_out, 'head', 0, 0, tiled=True)  3.34 us
    pallas_call x1, Pallas kernels, fast_local(): pl.pallas_call(functools.partial(place_kernel, n_seq), in_specs=[vmem_spe...  1.64 us
  transfers between devices with their start and end apart: 22, of which 11 were waited for; matrix products, arithmetic and copies ran while one was open for 1% of the time, Pallas kernels for 14%

profile of v3, /device:TPU:0, one launch (start us, length us, event | category | flops | bytes accessed | tf_op | source)
XLA Modules:
  0.0 63.2 jit_solution(5981704764774374726)
XLA Ops:
  0.6 3.0 %collective-permute-start.1 = (bf16[512,128]{1,0:T(8,128)(2,1)}, bf16[512,128]{1,0:T(8,128)(2,1)S(1)}, u32[]{:S(2)}, u32[]{:S(2)}) collective-permute-start(bf16[512,128]{1,0:T(8,128)(2,1)} %refs_0_.1), channel_id=1, source_target_pairs={{0,4},{1,5},{2,6},{3,7},{4,0},{5,1},{6,2},{7,3},{8,12},{9,13},{10,... | collective-permute-start | bytes 393224 | tf_op jit(solution)/shard_map/ppermute | solution.py:236
  3.7 1.5 %collective-permute-start = (bf16[512,128]{1,0:T(8,128)(2,1)}, bf16[512,128]{1,0:T(8,128)(2,1)S(1)}, u32[]{:S(2)}, u32[]{:S(2)}) collective-permute-start(bf16[512,128]{1,0:T(8,128)(2,1)} %refs_0_.1), channel_id=1, source_target_pairs={{0,2},{1,3},{2,0},{3,1},{4,6},{5,7},{6,4},{7,5},{8,10},{9,11},{10,... | collective-permute-start | bytes 393224 | tf_op jit(solution)/shard_map/ppermute | solution.py:236
  5.8 6.5 %attention.1 = bf16[256,896]{1,0:T(8,128)(2,1)} custom-call(s32[1]{0:T(128)S(6)} %copy.12.block_ref, s32[1,256]{1,0:T(1,128)} %bitcast.31, bf16[256,6144]{1,0:T(8,128)(2,1)} %q_hbm.1, bf16[512,6144]{1,0:T(8,128)(2,1)} %k_hbm.1, f32[32,256]{1,0:T(8,128)} %bitcast.28, bf16[256,2048]{1,0:T(8,128)(2,1)} %qi_hbm.1, f32[16,256]{1,0:T(8,128)} %bitcast.29), custom_call_target="tpu_custom_call" | custom-call | flops 3221225472 | bytes 9437184 | tf_op jit(solution)/shard_map/attention/pallas_call | solution.py:244
  12.3 0.0 collective-permute-done.1.refs_4_
  12.3 0.0 collective-permute-done.refs_2_
  12.3 4.0 %all-to-all-start = ((bf16[32,8,896]{2,1,0:T(8,128)(2,1)}), bf16[32,8,896]{2,1,0:T(8,128)(2,1)S(1)}, u32[]{:S(2)}, u32[]{:S(2)}) async-start(bf16[32,8,896]{2,1,0:T(8,128)(2,1)} %bitcast.27), calls=%async_computation | async-start | bytes 917504 | tf_op jit(solution)/shard_map/all_to_all | solution.py:271
  16.3 2.7 %collective-permute-start.5 = (bf16[512,128]{1,0:T(8,128)(2,1)S(1)}, bf16[512,128]{1,0:T(8,128)(2,1)S(1)}, u32[]{:S(2)}, u32[]{:S(2)}) collective-permute-start(bf16[512,128]{1,0:T(8,128)(2,1)S(1)} %copy-done), channel_id=1, source_target_pairs={{0,6},{1,7},{2,4},{3,5},{4,2},{5,3},{6,0},{7,1},{8,14},{9,15},{10,... | collective-permute-start | bytes 393224 | tf_op jit(solution)/shard_map/ppermute | solution.py:236
  19.0 0.0 collective-permute-start.2
  19.0 7.3 %collective-permute-done.5.refs_6_ = bf16[512,128]{1,0:T(8,128)(2,1)S(1)} collective-permute-done((bf16[512,128]{1,0:T(8,128)(2,1)S(1)}, bf16[512,128]{1,0:T(8,128)(2,1)S(1)}, u32[]{:S(2)}, u32[]{:S(2)}) %collective-permute-start.5) | collective-permute-done | bytes 131104 | tf_op jit(solution)/shard_map/ppermute | solution.py:236
  26.4 0.0 collective-permute-start.6
  26.4 0.5 collective-permute-start.3
  26.9 0.0 collective-permute-start.4
  26.9 0.8 %collective-permute-done.6.refs_7_ = bf16[512,128]{1,0:T(8,128)(2,1)S(1)} collective-permute-done((bf16[512,128]{1,0:T(8,128)(2,1)S(1)}, bf16[512,128]{1,0:T(8,128)(2,1)S(1)}, u32[]{:S(2)}, u32[]{:S(2)}) %collective-permute-start.6) | collective-permute-done | bytes 131104 | tf_op jit(solution)/shard_map/ppermute | solution.py:236
  27.7 0.0 collective-permute-done.2.refs_1_
  27.7 0.2 collective-permute-done.3.refs_3_
  27.9 0.3 collective-permute-done.4.refs_5_
  28.2 1.2 %all-to-all-done = bf16[32,8,896]{2,1,0:T(8,128)(2,1)S(1)} async-done(((bf16[32,8,896]{2,1,0:T(8,128)(2,1)}), bf16[32,8,896]{2,1,0:T(8,128)(2,1)S(1)}, u32[]{:S(2)}, u32[]{:S(2)}) %all-to-all-start) | async-done | bytes 458784 | tf_op jit(solution)/shard_map/all_to_all | solution.py:271
  29.4 3.6 %key_grad.1 = (bf16[4,512,128]{2,1,0:T(8,128)(2,1)S(1)}, bf16[8,512,512]{2,1,0:T(8,128)(2,1)S(1)}, bf16[512,128]{1,0:T(8,128)(2,1)S(1)}, f32[64,8,128]{2,1,0:T(8...) custom-call(bf16[256,896]{1,0:T(8,128)(2,1)S(1)} %bitcast.26, bf16[512,128]{1,0:T(8,128)(2,1)S(1)} %copy-done, ...), custom_call_target="tpu_custom_call" | custom-call | flops 1073741824 | bytes 2097152 | tf_op jit(solution)/shard_map/key_grad/pallas_call | solution.py:279
  33.0 1.1 %collective-permute-start.7 = (bf16[4,512,128]{2,1,0:T(8,128)(2,1)S(1)}, bf16[4,512,128]{2,1,0:T(8,128)(2,1)S(1)}, u32[]{:S(2)}, u32[]{:S(2)}) collective-permute-start(bf16[4,512,128]{2,1,0:T(8,128)(2,1)S(1)} %get-tuple-element.32), channel_id=1, source_target_pairs={{0,1},{1,0},{2,3},{3,2},{4,5},{5,4},{6,7},{7,6},{8,9},{9,8},{10,11... | collective-permute-start | bytes 1572872 | tf_op jit(solution)/shard_map/ppermute | solution.py:236
  34.2 1.6 %products.1 = (f32[4,512,128]{2,1,0:T(8,128)S(1)}, f32[512,128]{1,0:T(8,128)S(1)}) custom-call(bf16[8,512,512]{2,1,0:T(8,128)(2,1)S(1)} %get-tuple-element.28.gated_ref, bf16[128,512]{1,0:T(8,128)(2,1)S(1)} %get-tuple-element.29.weighted_ref, bf16[512,128]{1,0:T(8,128)(2,1)S(1)} %copy-done, bf16[512,128]{1,0:T(8,128)(2,1)S(1)} %collective-permute-done.2.refs_1_, ...), custom_call_target="tpu_custom_call" | custom-call | flops 1073741824 | bytes 2097152 | tf_op jit(solution)/shard_map/products/pallas_call | solution.py:301
  35.8 0.0 collective-permute-done.7
  35.8 0.1 fusion.5
  35.9 1.5 %collective-permute-start.8 = (bf16[512,128]{1,0:T(8,128)(2,1)S(1)}, bf16[512,128]{1,0:T(8,128)(2,1)S(1)}, u32[]{:S(2)}, u32[]{:S(2)}) collective-permute-start(bf16[512,128]{1,0:T(8,128)(2,1)S(1)} %get-tuple-element.37), channel_id=1, source_target_pairs={{0,2},{1,3},{2,0},{3,1},{4,6},{5,7},{6,4},{7,5},{8,10},{9,11},{10,... | collective-permute-start | bytes 393224 | tf_op jit(solution)/shard_map/ppermute | solution.py:236
  37.4 0.5 collective-permute-start.9
  38.0 1.5 %collective-permute-start.10 = (bf16[512,128]{1,0:T(8,128)(2,1)S(1)}, bf16[512,128]{1,0:T(8,128)(2,1)S(1)}, u32[]{:S(2)}, u32[]{:S(2)}) collective-permute-start(bf16[512,128]{1,0:T(8,128)(2,1)S(1)} %get-tuple-element.39), channel_id=1, source_target_pairs={{0,6},{1,7},{2,4},{3,5},{4,2},{5,3},{6,0},{7,1},{8,14},{9,15},{10,... | collective-permute-start | bytes 393224 | tf_op jit(solution)/shard_map/ppermute | solution.py:236
  39.5 0.8 %query_grad.1 = bf16[32,2176]{1,0:T(8,128)(2,1)} custom-call(f32[512,128]{1,0:T(8,128)S(1)} %get-tuple-element.33.term_ref, bf16[512,128]{1,0:T(8,128)(2,1)S(1)} %get-tuple-element.34.q_ref, f32[64,8,128]{2,1,0:T(8,128)S(1)} %get-tuple-element.35.wide_ref, f32[8,128]{1,0:T(8,128)S(1)} %get-tuple-element.36.kl_ref), custom_call_target="tpu_custom_call" | custom-call | bytes 2097152 | tf_op jit(solution)/shard_map/query_grad/pallas_call | solution.py:320
  40.3 3.3 %all-to-all-start.1 = ((bf16[4,8,2176]{2,1,0:T(8,128)(2,1)}), bf16[4,8,2176]{2,1,0:T(8,128)(2,1)S(1)}, u32[]{:S(2)}, u32[]{:S(2)}) async-start(bf16[4,8,2176]{2,1,0:T(8,128)(2,1)} %bitcast.8), calls=%async_computation.1 | async-start | bytes 278528 | tf_op jit(solution)/shard_map/all_to_all | solution.py:329
  43.6 0.0 collective-permute-done.8
  43.6 2.0 %collective-permute-done.9 = bf16[512,128]{1,0:T(8,128)(2,1)S(1)} collective-permute-done((bf16[512,128]{1,0:T(8,128)(2,1)S(1)}, bf16[512,128]{1,0:T(8,128)(2,1)S(1)}, u32[]{:S(2)}, u32[]{:S(2)}) %collective-permute-start.9) | collective-permute-done | bytes 131104 | tf_op jit(solution)/shard_map/ppermute | solution.py:236
  45.6 0.1 fusion.6
  45.7 0.5 collective-permute-start.18
  46.2 3.7 %all-to-all-done.1 = bf16[4,8,2176]{2,1,0:T(8,128)(2,1)S(1)} async-done(((bf16[4,8,2176]{2,1,0:T(8,128)(2,1)}), bf16[4,8,2176]{2,1,0:T(8,128)(2,1)S(1)}, u32[]{:S(2)}, u32[]{:S(2)}) %all-to-all-start.1) | async-done | bytes 139296 | tf_op jit(solution)/shard_map/all_to_all | solution.py:329
  50.0 1.4 %collective-permute-start.16 = (bf16[32,2176]{1,0:T(8,128)(2,1)S(1)}, bf16[32,2176]{1,0:T(8,128)(2,1)S(1)}, u32[]{:S(2)}, u32[]{:S(2)}) collective-permute-start(bf16[32,2176]{1,0:T(8,128)(2,1)S(1)} %bitcast.21), channel_id=1, source_target_pairs={{0,6},{1,7},{2,4},{3,5},{4,2},{5,3},{6,0},{7,1},{8,14},{9,15},{10,... | collective-permute-start | bytes 417800 | tf_op jit(solution)/shard_map/ppermute | solution.py:236
  51.4 1.5 %collective-permute-start.14 = (bf16[32,2176]{1,0:T(8,128)(2,1)S(1)}, bf16[32,2176]{1,0:T(8,128)(2,1)S(1)}, u32[]{:S(2)}, u32[]{:S(2)}) collective-permute-start(bf16[32,2176]{1,0:T(8,128)(2,1)S(1)} %bitcast.22), channel_id=1, source_target_pairs={{0,4},{1,5},{2,6},{3,7},{4,0},{5,1},{6,2},{7,3},{8,12},{9,13},{10,... | collective-permute-start | bytes 417800 | tf_op jit(solution)/shard_map/ppermute | solution.py:236
  52.9 0.6 collective-permute-start.12
  53.5 0.0 collective-permute-done.18
  53.5 1.4 %collective-permute-start.19 = (bf16[512,128]{1,0:T(8,128)(2,1)S(1)}, bf16[512,128]{1,0:T(8,128)(2,1)S(1)}, u32[]{:S(2)}, u32[]{:S(2)}) collective-permute-start(bf16[512,128]{1,0:T(8,128)(2,1)S(1)} %fusion.2), channel_id=1, source_target_pairs={{0,16},{8,24},{16,0},{24,8},{1,17},{9,25},{17,1},{25,9},{2,18},{10... | collective-permute-start | bytes 393224 | tf_op jit(solution)/shard_map/ppermute | solution.py:236
  54.9 0.0 collective-permute-start.11
  54.9 1.2 %collective-permute-done.16.refs_6_ = bf16[32,2176]{1,0:T(8,128)(2,1)S(1)} collective-permute-done((bf16[32,2176]{1,0:T(8,128)(2,1)S(1)}, bf16[32,2176]{1,0:T(8,128)(2,1)S(1)}, u32[]{:S(2)}, u32[]{:S(2)}) %collective-permute-start.16) | collective-permute-done | bytes 139296 | tf_op jit(solution)/shard_map/ppermute | solution.py:236
  56.0 0.0 collective-permute-start.17
  56.0 1.4 %collective-permute-done.14.refs_4_ = bf16[32,2176]{1,0:T(8,128)(2,1)S(1)} collective-permute-done((bf16[32,2176]{1,0:T(8,128)(2,1)S(1)}, bf16[32,2176]{1,0:T(8,128)(2,1)S(1)}, u32[]{:S(2)}, u32[]{:S(2)}) %collective-permute-start.14) | collective-permute-done | bytes 139296 | tf_op jit(solution)/shard_map/ppermute | solution.py:236
  57.4 0.5 collective-permute-done.12.refs_2_
  57.9 0.0 collective-permute-start.13
  57.9 2.9 %collective-permute-done.19 = bf16[512,128]{1,0:T(8,128)(2,1)S(1)} collective-permute-done((bf16[512,128]{1,0:T(8,128)(2,1)S(1)}, bf16[512,128]{1,0:T(8,128)(2,1)S(1)}, u32[]{:S(2)}, u32[]{:S(2)}) %collective-permute-start.19) | collective-permute-done | bytes 131104 | tf_op jit(solution)/shard_map/ppermute | solution.py:236
  60.8 0.7 %add_convert_fusion = bf16[512,128]{1,0:T(8,128)(2,1)} fusion(bf16[512,128]{1,0:T(8,128)(2,1)S(1)} %collective-permute-done.19, f32[512,128]{1,0:T(8,128)S(1)} %get-tuple-element.45, bf16[512,128]{1,0:T(8,128)(2,1)S(1)} %collective-permute-done.18), kind=kLoop, calls=%fused_computation.3 | loop fusion | flops 327680 | bytes 655360 | tf_op jit(solution)/shard_map/convert_element_type | solution.py:355
  61.6 0.0 collective-permute-done.17.refs_7_
  61.6 0.0 collective-permute-done.15.refs_5_
  61.6 1.6 %place.1 = (bf16[256,2048]{1,0:T(8,128)(2,1)}, bf16[16,256]{1,0:T(8,128)(2,1)}, bf16[256]{0:T(256)(128)(2,1)}) custom-call(bf16[32,2176]{1,0:T(8,128)(2,1)S(1)} %bitcast.25, bf16[32,2176]{1,0:T(8,128)(2,1)S(1)} %collective-permute-done.11.refs_1_, bf16[32,2176]{1,0:T(8,128)(2,1)S(1)} %collective-permute-done.12.refs_2_, ...), custom_call_target="tpu_custom_call" | custom-call | bytes 4456448 | tf_op jit(solution)/shard_map/place/pallas_call | solution.py:341
  (7 shorter events, 0.0 us)
Async XLA Ops:
  0.6 11.7 %collective-permute-start.1 = (bf16[512,128]{1,0:T(8,128)(2,1)}, bf16[512,128]{1,0:T(8,128)(2,1)S(1)}, u32[]{:S(2)}, u32[]{:S(2)}) collective-permute-start(bf16[512,128]{1,0:T(8,128)(2,1)} %refs_0_.1), channel_id=1, source_target_pairs={{0,4},{1,5},{2,6},{3,7},{4,0},{5,1},{6,2},{7,3},{8,12},{9,13},{10,... | collective-permute-start | bytes 393224 | tf_op jit(solution)/shard_map/ppermute | solution.py:236
  3.7 8.6 %collective-permute-start = (bf16[512,128]{1,0:T(8,128)(2,1)}, bf16[512,128]{1,0:T(8,128)(2,1)S(1)}, u32[]{:S(2)}, u32[]{:S(2)}) collective-permute-start(bf16[512,128]{1,0:T(8,128)(2,1)} %refs_0_.1), channel_id=1, source_target_pairs={{0,2},{1,3},{2,0},{3,1},{4,6},{5,7},{6,4},{7,5},{8,10},{9,11},{10,... | collective-permute-start | bytes 393224 | tf_op jit(solution)/shard_map/ppermute | solution.py:236
  5.8 10.5 %copy-start = (bf16[512,128]{1,0:T(8,128)(2,1)S(1)}, bf16[512,128]{1,0:T(8,128)(2,1)}, u32[]{:S(2)}) copy-start(bf16[512,128]{1,0:T(8,128)(2,1)} %refs_0_.1) | copy-start | bytes 393220
  12.3 17.1 %all-to-all-start = ((bf16[32,8,896]{2,1,0:T(8,128)(2,1)}), bf16[32,8,896]{2,1,0:T(8,128)(2,1)S(1)}, u32[]{:S(2)}, u32[]{:S(2)}) async-start(bf16[32,8,896]{2,1,0:T(8,128)(2,1)} %bitcast.27), calls=%async_computation | async-start | bytes 917504 | tf_op jit(solution)/shard_map/all_to_all | solution.py:271
  16.3 10.1 %collective-permute-start.5 = (bf16[512,128]{1,0:T(8,128)(2,1)S(1)}, bf16[512,128]{1,0:T(8,128)(2,1)S(1)}, u32[]{:S(2)}, u32[]{:S(2)}) collective-permute-start(bf16[512,128]{1,0:T(8,128)(2,1)S(1)} %copy-done), channel_id=1, source_target_pairs={{0,6},{1,7},{2,4},{3,5},{4,2},{5,3},{6,0},{7,1},{8,14},{9,15},{10,... | collective-permute-start | bytes 393224 | tf_op jit(solution)/shard_map/ppermute | solution.py:236
  19.0 8.7 %collective-permute-start.2 = (bf16[512,128]{1,0:T(8,128)(2,1)S(1)}, bf16[512,128]{1,0:T(8,128)(2,1)S(1)}, u32[]{:S(2)}, u32[]{:S(2)}) collective-permute-start(bf16[512,128]{1,0:T(8,128)(2,1)S(1)} %copy-done), channel_id=1, source_target_pairs={{0,1},{1,0},{2,3},{3,2},{4,5},{5,4},{6,7},{7,6},{8,9},{9,8},{10,11... | collective-permute-start | bytes 393224 | tf_op jit(solution)/shard_map/ppermute | solution.py:236
  26.4 1.3 %collective-permute-start.6 = (bf16[512,128]{1,0:T(8,128)(2,1)S(1)}, bf16[512,128]{1,0:T(8,128)(2,1)S(1)}, u32[]{:S(2)}, u32[]{:S(2)}) collective-permute-start(bf16[512,128]{1,0:T(8,128)(2,1)S(1)} %collective-permute-done.5.refs_6_), channel_id=1, source_target_pairs={{0,1},{1,0},{2,3},{3,2},{4,5},{5,4},{6,7},{7,6},{8,9},{9,8},{10,11... | collective-permute-start | bytes 393224 | tf_op jit(solution)/shard_map/ppermute | solution.py:236
  26.4 1.5 %collective-permute-start.3 = (bf16[512,128]{1,0:T(8,128)(2,1)S(1)}, bf16[512,128]{1,0:T(8,128)(2,1)S(1)}, u32[]{:S(2)}, u32[]{:S(2)}) collective-permute-start(bf16[512,128]{1,0:T(8,128)(2,1)S(1)} %collective-permute-done.refs_2_), channel_id=1, source_target_pairs={{0,1},{1,0},{2,3},{3,2},{4,5},{5,4},{6,7},{7,6},{8,9},{9,8},{10,11... | collective-permute-start | bytes 393224 | tf_op jit(solution)/shard_map/ppermute | solution.py:236
  26.9 1.3 %collective-permute-start.4 = (bf16[512,128]{1,0:T(8,128)(2,1)S(1)}, bf16[512,128]{1,0:T(8,128)(2,1)S(1)}, u32[]{:S(2)}, u32[]{:S(2)}) collective-permute-start(bf16[512,128]{1,0:T(8,128)(2,1)S(1)} %collective-permute-done.1.refs_4_), channel_id=1, source_target_pairs={{0,1},{1,0},{2,3},{3,2},{4,5},{5,4},{6,7},{7,6},{8,9},{9,8},{10,11... | collective-permute-start | bytes 393224 | tf_op jit(solution)/shard_map/ppermute | solution.py:236
  33.0 2.8 %collective-permute-start.7 = (bf16[4,512,128]{2,1,0:T(8,128)(2,1)S(1)}, bf16[4,512,128]{2,1,0:T(8,128)(2,1)S(1)}, u32[]{:S(2)}, u32[]{:S(2)}) collective-permute-start(bf16[4,512,128]{2,1,0:T(8,128)(2,1)S(1)} %get-tuple-element.32), channel_id=1, source_target_pairs={{0,1},{1,0},{2,3},{3,2},{4,5},{5,4},{6,7},{7,6},{8,9},{9,8},{10,11... | collective-permute-start | bytes 1572872 | tf_op jit(solution)/shard_map/ppermute | solution.py:236
  35.9 7.7 %collective-permute-start.8 = (bf16[512,128]{1,0:T(8,128)(2,1)S(1)}, bf16[512,128]{1,0:T(8,128)(2,1)S(1)}, u32[]{:S(2)}, u32[]{:S(2)}) collective-permute-start(bf16[512,128]{1,0:T(8,128)(2,1)S(1)} %get-tuple-element.37), channel_id=1, source_target_pairs={{0,2},{1,3},{2,0},{3,1},{4,6},{5,7},{6,4},{7,5},{8,10},{9,11},{10,... | collective-permute-start | bytes 393224 | tf_op jit(solution)/shard_map/ppermute | solution.py:236
  37.4 8.2 %collective-permute-start.9 = (bf16[512,128]{1,0:T(8,128)(2,1)S(1)}, bf16[512,128]{1,0:T(8,128)(2,1)S(1)}, u32[]{:S(2)}, u32[]{:S(2)}) collective-permute-start(bf16[512,128]{1,0:T(8,128)(2,1)S(1)} %get-tuple-element.38), channel_id=1, source_target_pairs={{0,4},{1,5},{2,6},{3,7},{4,0},{5,1},{6,2},{7,3},{8,12},{9,13},{10,... | collective-permute-start | bytes 393224 | tf_op jit(solution)/shard_map/ppermute | solution.py:236
  38.0 7.7 %collective-permute-start.10 = (bf16[512,128]{1,0:T(8,128)(2,1)S(1)}, bf16[512,128]{1,0:T(8,128)(2,1)S(1)}, u32[]{:S(2)}, u32[]{:S(2)}) collective-permute-start(bf16[512,128]{1,0:T(8,128)(2,1)S(1)} %get-tuple-element.39), channel_id=1, source_target_pairs={{0,6},{1,7},{2,4},{3,5},{4,2},{5,3},{6,0},{7,1},{8,14},{9,15},{10,... | collective-permute-start | bytes 393224 | tf_op jit(solution)/shard_map/ppermute | solution.py:236
  40.3 9.7 %all-to-all-start.1 = ((bf16[4,8,2176]{2,1,0:T(8,128)(2,1)}), bf16[4,8,2176]{2,1,0:T(8,128)(2,1)S(1)}, u32[]{:S(2)}, u32[]{:S(2)}) async-start(bf16[4,8,2176]{2,1,0:T(8,128)(2,1)} %bitcast.8), calls=%async_computation.1 | async-start | bytes 278528 | tf_op jit(solution)/shard_map/all_to_all | solution.py:329
  45.7 7.8 %collective-permute-start.18 = (bf16[512,128]{1,0:T(8,128)(2,1)S(1)}, bf16[512,128]{1,0:T(8,128)(2,1)S(1)}, u32[]{:S(2)}, u32[]{:S(2)}) collective-permute-start(bf16[512,128]{1,0:T(8,128)(2,1)S(1)} %get-tuple-element.44), channel_id=1, source_target_pairs={{0,8},{8,0},{16,24},{24,16},{1,9},{9,1},{17,25},{25,17},{2,10},{10... | collective-permute-start | bytes 393224 | tf_op jit(solution)/shard_map/ppermute | solution.py:236
  50.0 6.1 %collective-permute-start.16 = (bf16[32,2176]{1,0:T(8,128)(2,1)S(1)}, bf16[32,2176]{1,0:T(8,128)(2,1)S(1)}, u32[]{:S(2)}, u32[]{:S(2)}) collective-permute-start(bf16[32,2176]{1,0:T(8,128)(2,1)S(1)} %bitcast.21), channel_id=1, source_target_pairs={{0,6},{1,7},{2,4},{3,5},{4,2},{5,3},{6,0},{7,1},{8,14},{9,15},{10,... | collective-permute-start | bytes 417800 | tf_op jit(solution)/shard_map/ppermute | solution.py:236
  51.4 6.0 %collective-permute-start.14 = (bf16[32,2176]{1,0:T(8,128)(2,1)S(1)}, bf16[32,2176]{1,0:T(8,128)(2,1)S(1)}, u32[]{:S(2)}, u32[]{:S(2)}) collective-permute-start(bf16[32,2176]{1,0:T(8,128)(2,1)S(1)} %bitcast.22), channel_id=1, source_target_pairs={{0,4},{1,5},{2,6},{3,7},{4,0},{5,1},{6,2},{7,3},{8,12},{9,13},{10,... | collective-permute-start | bytes 417800 | tf_op jit(solution)/shard_map/ppermute | solution.py:236
  52.9 5.1 %collective-permute-start.12 = (bf16[32,2176]{1,0:T(8,128)(2,1)S(1)}, bf16[32,2176]{1,0:T(8,128)(2,1)S(1)}, u32[]{:S(2)}, u32[]{:S(2)}) collective-permute-start(bf16[32,2176]{1,0:T(8,128)(2,1)S(1)} %bitcast.23), channel_id=1, source_target_pairs={{0,2},{1,3},{2,0},{3,1},{4,6},{5,7},{6,4},{7,5},{8,10},{9,11},{10,... | collective-permute-start | bytes 417800 | tf_op jit(solution)/shard_map/ppermute | solution.py:236
  53.5 7.3 %collective-permute-start.19 = (bf16[512,128]{1,0:T(8,128)(2,1)S(1)}, bf16[512,128]{1,0:T(8,128)(2,1)S(1)}, u32[]{:S(2)}, u32[]{:S(2)}) collective-permute-start(bf16[512,128]{1,0:T(8,128)(2,1)S(1)} %fusion.2), channel_id=1, source_target_pairs={{0,16},{8,24},{16,0},{24,8},{1,17},{9,25},{17,1},{25,9},{2,18},{10... | collective-permute-start | bytes 393224 | tf_op jit(solution)/shard_map/ppermute | solution.py:236
  54.9 6.7 %collective-permute-start.11 = (bf16[32,2176]{1,0:T(8,128)(2,1)S(1)}, bf16[32,2176]{1,0:T(8,128)(2,1)S(1)}, u32[]{:S(2)}, u32[]{:S(2)}) collective-permute-start(bf16[32,2176]{1,0:T(8,128)(2,1)S(1)} %bitcast.24), channel_id=1, source_target_pairs={{0,1},{1,0},{2,3},{3,2},{4,5},{5,4},{6,7},{7,6},{8,9},{9,8},{10,11... | collective-permute-start | bytes 417800 | tf_op jit(solution)/shard_map/ppermute | solution.py:236
  56.0 5.5 %collective-permute-start.17 = (bf16[32,2176]{1,0:T(8,128)(2,1)S(1)}, bf16[32,2176]{1,0:T(8,128)(2,1)S(1)}, u32[]{:S(2)}, u32[]{:S(2)}) collective-permute-start(bf16[32,2176]{1,0:T(8,128)(2,1)S(1)} %collective-permute-done.16.refs_6_), channel_id=1, source_target_pairs={{0,1},{1,0},{2,3},{3,2},{4,5},{5,4},{6,7},{7,6},{8,9},{9,8},{10,11... | collective-permute-start | bytes 417800 | tf_op jit(solution)/shard_map/ppermute | solution.py:236
  57.4 4.1 %collective-permute-start.15 = (bf16[32,2176]{1,0:T(8,128)(2,1)S(1)}, bf16[32,2176]{1,0:T(8,128)(2,1)S(1)}, u32[]{:S(2)}, u32[]{:S(2)}) collective-permute-start(bf16[32,2176]{1,0:T(8,128)(2,1)S(1)} %collective-permute-done.14.refs_4_), channel_id=1, source_target_pairs={{0,1},{1,0},{2,3},{3,2},{4,5},{5,4},{6,7},{7,6},{8,9},{9,8},{10,11... | collective-permute-start | bytes 417800 | tf_op jit(solution)/shard_map/ppermute | solution.py:236
  57.9 3.7 %collective-permute-start.13 = (bf16[32,2176]{1,0:T(8,128)(2,1)S(1)}, bf16[32,2176]{1,0:T(8,128)(2,1)S(1)}, u32[]{:S(2)}, u32[]{:S(2)}) collective-permute-start(bf16[32,2176]{1,0:T(8,128)(2,1)S(1)} %collective-permute-done.12.refs_2_), channel_id=1, source_target_pairs={{0,1},{1,0},{2,3},{3,2},{4,5},{5,4},{6,7},{7,6},{8,9},{9,8},{10,11... | collective-permute-start | bytes 417800 | tf_op jit(solution)/shard_map/ppermute | solution.py:236

commit v4 on v3

--- a/solution.py
+++ b/solution.py
@@ -18,10 +18,6 @@
     return pl.BlockSpec(memory_space=pltpu.VMEM)
 
 
-def smem_spec():
-    return pl.BlockSpec(memory_space=pltpu.SMEM)
-
-
 def head_parts(heads, width):
     least = LANES // math.gcd(LANES, width)
     first = heads // 2 // least * least
@@ -33,8 +29,8 @@
 
 
 def attention_kernel(
-    parts, block_ref, pos_hbm, q_hbm, k_hbm, lse_hbm, qi_hbm, hw_hbm, out_ref,
-    pos_ref, q_ref, k_ref, lse_ref, hw_ref, acc_ref, sems, part_sems
+    parts, block_hbm, pos_hbm, q_hbm, k_hbm, lse_hbm, qi_hbm, hw_hbm, out_ref,
+    block_ref, pos_ref, q_ref, k_ref, lse_ref, hw_ref, acc_ref, sems, part_sems
 ):
     rows, keys = q_ref.shape[0], k_ref.shape[0]
     mla_heads, heads = lse_ref.shape[0], hw_ref.shape[0]
@@ -44,10 +40,10 @@
     scale = width ** (-0.5) * log2e
     small = [
         pltpu.make_async_copy(source, target, sems.at[i])
-        for i, (source, target) in enumerate(((lse_hbm, lse_ref), (hw_hbm, hw_ref), (pos_hbm, pos_ref)))
+        for i, (source, target) in enumerate(((lse_hbm, lse_ref), (hw_hbm, hw_ref), (pos_hbm, pos_ref), (block_hbm, block_ref)))
     ]
     share_at = pl.ds(pl.multiple_of(lax.axis_index("seq") * cols, LANES), cols)
-    share_copy = pltpu.make_async_copy(qi_hbm.at[:, share_at], out_ref.at[:, keys : keys + cols], sems.at[3])
+    share_copy = pltpu.make_async_copy(qi_hbm.at[:, share_at], out_ref.at[:, keys : keys + cols], sems.at[4])
     large = []
     first = 0
     for i, n in enumerate(parts):
@@ -150,19 +146,20 @@
 
     total = row_sum(shares)
     norm = row_sum([jnp.where(v, jnp.exp(x - peak), 0.0) for v, x in zip(valids, logits)])
-    log_norm, log_total, inverse = jnp.log(norm), jnp.log(total), 1.0 / total
+    log_norm, log_total = jnp.log(norm), jnp.log(total)
     weighted = jnp.transpose(q_ref[...].astype(F32) * wide_ref[...].reshape(q_ref.shape)).astype(BF16)
     weighted_ref[...] = weighted
     kls = []
     for k in range(n_seq):
-        target = shares[k] * inverse
+        target = shares[k] / total
         log_prob = logits[k] - peak - log_norm
         prob = jnp.where(valids[k], jnp.exp(log_prob), 0.0)
         log_target = jnp.log(jnp.where(valids[k], shares[k], 1.0)) - log_total
         kls.append(jnp.where(valids[k], target * (log_target - log_prob), 0.0))
-        dlogit = jnp.where(valids[k], prob - target, 0.0).astype(BF16).astype(F32)
-        cube = dots_ref[k].astype(F32).reshape(heads_all, own, keys)
-        gated = jnp.where(cube > 0.0, dlogit[None], 0.0).reshape(heads_all * own, keys).astype(BF16)
+        dlogit = jnp.where(valids[k], prob - target, 0.0)
+        twice = jnp.concatenate([dlogit, dlogit], axis=0).astype(BF16)
+        cube = dots_ref[k].reshape(heads_all // 2, 2 * own, keys)
+        gated = jnp.where(cube > 0, twice[None], jnp.zeros_like(twice)[None]).reshape(heads_all * own, keys)
         gated_ref[k] = gated
         if k % 2 == 1:
             side = jnp.dot(weighted, gated, preferred_element_type=F32)
@@ -204,7 +201,7 @@
 
 def place_kernel(n_seq, *refs):
     pieces = refs[:n_seq]
-    gq_ref, hw_ref, kl_ref, side_ref, sems = refs[n_seq:]
+    gq_ref, hw_out, kl_out, side_ref, hw_ref, kl_ref, sems = refs[n_seq:]
     s = lax.axis_index("seq")
     rows, cols = pieces[0].shape[0], gq_ref.shape[1]
     heads = hw_ref.shape[0]
@@ -217,6 +214,9 @@
     side = jnp.transpose(side_ref[...])
     hw_ref[...] = side[:heads, :].astype(BF16)
     kl_ref[...] = side[heads, :].astype(BF16)
+    for source, target in ((hw_ref, hw_out), (kl_ref, kl_out)):
+        copies.append(pltpu.make_async_copy(source, target, sems.at[len(copies)]))
+        copies[-1].start()
     for copy in copies:
         copy.wait()
 
@@ -243,17 +243,18 @@
     hbm = pl.BlockSpec(memory_space=pltpu.HBM)
     sent = pl.pallas_call(
         functools.partial(attention_kernel, parts),
-        in_specs=[smem_spec()] + [hbm] * 6,
+        in_specs=[hbm] * 7,
         out_specs=vmem_spec(),
         out_shape=jax.ShapeDtypeStruct((rows, keys + cols + LANES), BF16),
         scratch_shapes=[
+            pltpu.SMEM((1,), jnp.int32),
             pltpu.VMEM((1, rows), jnp.int32),
             pltpu.VMEM(query_mla.shape, BF16),
             pltpu.VMEM(key_mla.shape, BF16),
             pltpu.VMEM((mla_heads, rows), F32),
             pltpu.VMEM((heads, rows), F32),
             pltpu.VMEM((keys, rows), F32),
-            pltpu.SemaphoreType.DMA((4,)),
+            pltpu.SemaphoreType.DMA((5,)),
             pltpu.SemaphoreType.DMA((2, len(parts))),
         ],
         compiler_params=limit(56),
@@ -341,13 +342,18 @@
     grad_query_index, hw, kl = pl.pallas_call(
         functools.partial(place_kernel, n_seq),
         in_specs=[vmem_spec()] * n_seq,
-        out_specs=[pl.BlockSpec(memory_space=pl.ANY), vmem_spec(), vmem_spec()],
+        out_specs=[pl.BlockSpec(memory_space=pl.ANY)] * 3,
         out_shape=[
             jax.ShapeDtypeStruct((rows, heads * width), BF16),
             jax.ShapeDtypeStruct((heads, rows), BF16),
             jax.ShapeDtypeStruct((rows,), BF16),
         ],
-        scratch_shapes=[pltpu.VMEM((rows, LANES), F32), pltpu.SemaphoreType.DMA((n_seq,))],
+        scratch_shapes=[
+            pltpu.VMEM((rows, LANES), F32),
+            pltpu.VMEM((heads, rows), BF16),
+            pltpu.VMEM((rows,), BF16),
+            pltpu.SemaphoreType.DMA((n_seq + 2,)),
+        ],
         compiler_params=limit(4),
         cost_estimate=pl.CostEstimate(flops=0, bytes_accessed=8 * rows * wide_cols, transcendentals=0),
         name="place",
@@ -424,7 +430,8 @@
 
     def local(*args):
         rows, heads = args[0].shape[0], args[5].shape[1]
-        if rows == 8 * n_seq * n_head and heads % n_seq == 0:
+        paired = all(n & (n - 1) == 0 and n > 1 for n in (n_seq, n_head))
+        if paired and rows == 8 * n_seq * n_head and heads % n_seq == 0:
             return fast_local(n_seq, n_head, *args)
         return plain_local(*args)
 

time: 63.5 us -> 62 us (0.976)
  Pallas kernels: 14.2 us -> 12.6 us
    pallas_call x1, Pallas kernels: 3.64 us -> 2.67 us  [fast_local(): pl.pallas_call(functools.partial(keys_kernel, n_seq, n_head, own), in_spe...]
where the time goes in v4:
time: 62 us; the launch traced here: 61.7 us
  starting transfers between devices  25.2 us (41%)
  waiting for transfers between devices  21.5 us (35%)
  Pallas kernels  12.6 us (20%)
  between operations  1.4 us (2%)
  other arithmetic  0.9 us (1%)
    ppermute x20, starting transfers between devices, swap(): return lax.ppermute(x, axis, [(i, i ^ mask) for i in range(n)])  17.9 us
    ppermute x20, waiting for transfers between devices, swap(): return lax.ppermute(x, axis, [(i, i ^ mask) for i in range(n)])  16.7 us
    pallas_call x1, Pallas kernels, fast_local(): pl.pallas_call(functools.partial(attention_kernel, parts), in_specs=[hbm]...  6.49 us
    all_to_all x1, starting transfers between devices, fast_local(): got = lax.all_to_all(sent, ('seq', 'head'), 0, 0, tiled=True)  3.98 us
    all_to_all x1, waiting for transfers between devices, fast_local(): own_rows = lax.all_to_all(rows_out, 'head', 0, 0, tiled=True)  3.73 us
    all_to_all x1, starting transfers between devices, fast_local(): own_rows = lax.all_to_all(rows_out, 'head', 0, 0, tiled=True)  3.34 us
    pallas_call x1, Pallas kernels, fast_local(): pl.pallas_call(functools.partial(keys_kernel, n_seq, n_head, own), in_spe...  2.67 us
    pallas_call x1, Pallas kernels, fast_local(): pl.pallas_call(functools.partial(products_kernel, n_seq), in_specs=[vmem_...  1.62 us
  transfers between devices with their start and end apart: 22, of which 11 were waited for; matrix products, arithmetic and copies ran while one was open for 1% of the time, Pallas kernels for 14%

profile of v4, /device:TPU:0, one launch (start us, length us, event | category | flops | bytes accessed | tf_op | source)
XLA Modules:
  0.0 61.7 jit_solution(10527421036119604973)
XLA Ops:
  0.6 3.0 %collective-permute-start.1 = (bf16[512,128]{1,0:T(8,128)(2,1)}, bf16[512,128]{1,0:T(8,128)(2,1)S(1)}, u32[]{:S(2)}, u32[]{:S(2)}) collective-permute-start(bf16[512,128]{1,0:T(8,128)(2,1)} %refs_0_.1), channel_id=1, source_target_pairs={{0,4},{1,5},{2,6},{3,7},{4,0},{5,1},{6,2},{7,3},{8,12},{9,13},{10,... | collective-permute-start | bytes 393224 | tf_op jit(solution)/shard_map/ppermute | solution.py:236
  3.7 1.5 %collective-permute-start = (bf16[512,128]{1,0:T(8,128)(2,1)}, bf16[512,128]{1,0:T(8,128)(2,1)S(1)}, u32[]{:S(2)}, u32[]{:S(2)}) collective-permute-start(bf16[512,128]{1,0:T(8,128)(2,1)} %refs_0_.1), channel_id=1, source_target_pairs={{0,2},{1,3},{2,0},{3,1},{4,6},{5,7},{6,4},{7,5},{8,10},{9,11},{10,... | collective-permute-start | bytes 393224 | tf_op jit(solution)/shard_map/ppermute | solution.py:236
  5.8 6.5 %attention.1 = bf16[256,896]{1,0:T(8,128)(2,1)} custom-call(s32[1]{0:T(128)S(6)} %copy.12.block_hbm, s32[1,256]{1,0:T(1,128)} %bitcast.31, bf16[256,6144]{1,0:T(8,128)(2,1)} %q_hbm.1, bf16[512,6144]{1,0:T(8,128)(2,1)} %k_hbm.1, f32[32,256]{1,0:T(8,128)} %bitcast.28, bf16[256,2048]{1,0:T(8,128)(2,1)} %qi_hbm.1, f32[16,256]{1,0:T(8,128)} %bitcast.29), custom_call_target="tpu_custom_call" | custom-call | flops 3221225472 | bytes 9437184 | tf_op jit(solution)/shard_map/attention/pallas_call | solution.py:244
  12.3 0.0 collective-permute-done.1.refs_4_
  12.3 0.0 collective-permute-done.refs_2_
  12.3 4.0 %all-to-all-start = ((bf16[32,8,896]{2,1,0:T(8,128)(2,1)}), bf16[32,8,896]{2,1,0:T(8,128)(2,1)S(1)}, u32[]{:S(2)}, u32[]{:S(2)}) async-start(bf16[32,8,896]{2,1,0:T(8,128)(2,1)} %bitcast.27), calls=%async_computation | async-start | bytes 917504 | tf_op jit(solution)/shard_map/all_to_all | solution.py:272
  16.3 2.7 %collective-permute-start.5 = (bf16[512,128]{1,0:T(8,128)(2,1)S(1)}, bf16[512,128]{1,0:T(8,128)(2,1)S(1)}, u32[]{:S(2)}, u32[]{:S(2)}) collective-permute-start(bf16[512,128]{1,0:T(8,128)(2,1)S(1)} %copy-done), channel_id=1, source_target_pairs={{0,6},{1,7},{2,4},{3,5},{4,2},{5,3},{6,0},{7,1},{8,14},{9,15},{10,... | collective-permute-start | bytes 393224 | tf_op jit(solution)/shard_map/ppermute | solution.py:236
  19.1 0.0 collective-permute-start.2
  19.1 7.3 %collective-permute-done.5.refs_6_ = bf16[512,128]{1,0:T(8,128)(2,1)S(1)} collective-permute-done((bf16[512,128]{1,0:T(8,128)(2,1)S(1)}, bf16[512,128]{1,0:T(8,128)(2,1)S(1)}, u32[]{:S(2)}, u32[]{:S(2)}) %collective-permute-start.5) | collective-permute-done | bytes 131104 | tf_op jit(solution)/shard_map/ppermute | solution.py:236
  26.4 0.0 collective-permute-start.6
  26.4 0.5 collective-permute-start.3
  26.9 0.0 collective-permute-start.4
  26.9 0.8 %collective-permute-done.6.refs_7_ = bf16[512,128]{1,0:T(8,128)(2,1)S(1)} collective-permute-done((bf16[512,128]{1,0:T(8,128)(2,1)S(1)}, bf16[512,128]{1,0:T(8,128)(2,1)S(1)}, u32[]{:S(2)}, u32[]{:S(2)}) %collective-permute-start.6) | collective-permute-done | bytes 131104 | tf_op jit(solution)/shard_map/ppermute | solution.py:236
  27.8 0.0 collective-permute-done.2.refs_1_
  27.8 0.2 collective-permute-done.3.refs_3_
  27.9 0.3 collective-permute-done.4.refs_5_
  28.3 1.2 %all-to-all-done = bf16[32,8,896]{2,1,0:T(8,128)(2,1)S(1)} async-done(((bf16[32,8,896]{2,1,0:T(8,128)(2,1)}), bf16[32,8,896]{2,1,0:T(8,128)(2,1)S(1)}, u32[]{:S(2)}, u32[]{:S(2)}) %all-to-all-start) | async-done | bytes 458784 | tf_op jit(solution)/shard_map/all_to_all | solution.py:272
  29.4 2.7 %key_grad.1 = (bf16[4,512,128]{2,1,0:T(8,128)(2,1)S(1)}, bf16[8,512,512]{2,1,0:T(8,128)(2,1)S(1)}, bf16[512,128]{1,0:T(8,128)(2,1)S(1)}, f32[64,8,128]{2,1,0:T(8...) custom-call(bf16[256,896]{1,0:T(8,128)(2,1)S(1)} %bitcast.26, bf16[512,128]{1,0:T(8,128)(2,1)S(1)} %copy-done, ...), custom_call_target="tpu_custom_call" | custom-call | flops 1073741824 | bytes 2097152 | tf_op jit(solution)/shard_map/key_grad/pallas_call | solution.py:280
  32.1 1.1 %collective-permute-start.7 = (bf16[4,512,128]{2,1,0:T(8,128)(2,1)S(1)}, bf16[4,512,128]{2,1,0:T(8,128)(2,1)S(1)}, u32[]{:S(2)}, u32[]{:S(2)}) collective-permute-start(bf16[4,512,128]{2,1,0:T(8,128)(2,1)S(1)} %get-tuple-element.32), channel_id=1, source_target_pairs={{0,1},{1,0},{2,3},{3,2},{4,5},{5,4},{6,7},{7,6},{8,9},{9,8},{10,11... | collective-permute-start | bytes 1572872 | tf_op jit(solution)/shard_map/ppermute | solution.py:236
  33.2 1.6 %products.1 = (f32[4,512,128]{2,1,0:T(8,128)S(1)}, f32[512,128]{1,0:T(8,128)S(1)}) custom-call(bf16[8,512,512]{2,1,0:T(8,128)(2,1)S(1)} %get-tuple-element.28.gated_ref, bf16[128,512]{1,0:T(8,128)(2,1)S(1)} %get-tuple-element.29.weighted_ref, bf16[512,128]{1,0:T(8,128)(2,1)S(1)} %copy-done, bf16[512,128]{1,0:T(8,128)(2,1)S(1)} %collective-permute-done.2.refs_1_, ...), custom_call_target="tpu_custom_call" | custom-call | flops 1073741824 | bytes 2097152 | tf_op jit(solution)/shard_map/products/pallas_call | solution.py:302
  34.9 0.0 collective-permute-done.7
  34.9 0.1 fusion.5
  35.0 1.5 %collective-permute-start.8 = (bf16[512,128]{1,0:T(8,128)(2,1)S(1)}, bf16[512,128]{1,0:T(8,128)(2,1)S(1)}, u32[]{:S(2)}, u32[]{:S(2)}) collective-permute-start(bf16[512,128]{1,0:T(8,128)(2,1)S(1)} %get-tuple-element.37), channel_id=1, source_target_pairs={{0,2},{1,3},{2,0},{3,1},{4,6},{5,7},{6,4},{7,5},{8,10},{9,11},{10,... | collective-permute-start | bytes 393224 | tf_op jit(solution)/shard_map/ppermute | solution.py:236
  36.5 0.5 collective-permute-start.9
  37.0 1.5 %collective-permute-start.10 = (bf16[512,128]{1,0:T(8,128)(2,1)S(1)}, bf16[512,128]{1,0:T(8,128)(2,1)S(1)}, u32[]{:S(2)}, u32[]{:S(2)}) collective-permute-start(bf16[512,128]{1,0:T(8,128)(2,1)S(1)} %get-tuple-element.39), channel_id=1, source_target_pairs={{0,6},{1,7},{2,4},{3,5},{4,2},{5,3},{6,0},{7,1},{8,14},{9,15},{10,... | collective-permute-start | bytes 393224 | tf_op jit(solution)/shard_map/ppermute | solution.py:236
  38.5 0.8 %query_grad.1 = bf16[32,2176]{1,0:T(8,128)(2,1)} custom-call(f32[512,128]{1,0:T(8,128)S(1)} %get-tuple-element.33.term_ref, bf16[512,128]{1,0:T(8,128)(2,1)S(1)} %get-tuple-element.34.q_ref, f32[64,8,128]{2,1,0:T(8,128)S(1)} %get-tuple-element.35.wide_ref, f32[8,128]{1,0:T(8,128)S(1)} %get-tuple-element.36.kl_ref), custom_call_target="tpu_custom_call" | custom-call | bytes 2097152 | tf_op jit(solution)/shard_map/query_grad/pallas_call | solution.py:321
  39.3 3.3 %all-to-all-start.1 = ((bf16[4,8,2176]{2,1,0:T(8,128)(2,1)}), bf16[4,8,2176]{2,1,0:T(8,128)(2,1)S(1)}, u32[]{:S(2)}, u32[]{:S(2)}) async-start(bf16[4,8,2176]{2,1,0:T(8,128)(2,1)} %bitcast.8), calls=%async_computation.1 | async-start | bytes 278528 | tf_op jit(solution)/shard_map/all_to_all | solution.py:330
  42.7 0.0 collective-permute-done.8
  42.7 2.0 %collective-permute-done.9 = bf16[512,128]{1,0:T(8,128)(2,1)S(1)} collective-permute-done((bf16[512,128]{1,0:T(8,128)(2,1)S(1)}, bf16[512,128]{1,0:T(8,128)(2,1)S(1)}, u32[]{:S(2)}, u32[]{:S(2)}) %collective-permute-start.9) | collective-permute-done | bytes 131104 | tf_op jit(solution)/shard_map/ppermute | solution.py:236
  44.7 0.0 collective-permute-done.10
  44.7 0.1 fusion.6
  44.8 0.5 collective-permute-start.18
  45.3 3.7 %all-to-all-done.1 = bf16[4,8,2176]{2,1,0:T(8,128)(2,1)S(1)} async-done(((bf16[4,8,2176]{2,1,0:T(8,128)(2,1)}), bf16[4,8,2176]{2,1,0:T(8,128)(2,1)S(1)}, u32[]{:S(2)}, u32[]{:S(2)}) %all-to-all-start.1) | async-done | bytes 139296 | tf_op jit(solution)/shard_map/all_to_all | solution.py:330
  49.1 1.4 %collective-permute-start.16 = (bf16[32,2176]{1,0:T(8,128)(2,1)S(1)}, bf16[32,2176]{1,0:T(8,128)(2,1)S(1)}, u32[]{:S(2)}, u32[]{:S(2)}) collective-permute-start(bf16[32,2176]{1,0:T(8,128)(2,1)S(1)} %bitcast.21), channel_id=1, source_target_pairs={{0,6},{1,7},{2,4},{3,5},{4,2},{5,3},{6,0},{7,1},{8,14},{9,15},{10,... | collective-permute-start | bytes 417800 | tf_op jit(solution)/shard_map/ppermute | solution.py:236
  50.5 1.5 %collective-permute-start.14 = (bf16[32,2176]{1,0:T(8,128)(2,1)S(1)}, bf16[32,2176]{1,0:T(8,128)(2,1)S(1)}, u32[]{:S(2)}, u32[]{:S(2)}) collective-permute-start(bf16[32,2176]{1,0:T(8,128)(2,1)S(1)} %bitcast.22), channel_id=1, source_target_pairs={{0,4},{1,5},{2,6},{3,7},{4,0},{5,1},{6,2},{7,3},{8,12},{9,13},{10,... | collective-permute-start | bytes 417800 | tf_op jit(solution)/shard_map/ppermute | solution.py:236
  51.9 0.6 collective-permute-start.12
  52.5 0.0 collective-permute-done.18
  52.6 1.4 %collective-permute-start.19 = (bf16[512,128]{1,0:T(8,128)(2,1)S(1)}, bf16[512,128]{1,0:T(8,128)(2,1)S(1)}, u32[]{:S(2)}, u32[]{:S(2)}) collective-permute-start(bf16[512,128]{1,0:T(8,128)(2,1)S(1)} %fusion.2), channel_id=1, source_target_pairs={{0,16},{8,24},{16,0},{24,8},{1,17},{9,25},{17,1},{25,9},{2,18},{10... | collective-permute-start | bytes 393224 | tf_op jit(solution)/shard_map/ppermute | solution.py:236
  54.0 1.2 %collective-permute-done.16.refs_6_ = bf16[32,2176]{1,0:T(8,128)(2,1)S(1)} collective-permute-done((bf16[32,2176]{1,0:T(8,128)(2,1)S(1)}, bf16[32,2176]{1,0:T(8,128)(2,1)S(1)}, u32[]{:S(2)}, u32[]{:S(2)}) %collective-permute-start.16) | collective-permute-done | bytes 139296 | tf_op jit(solution)/shard_map/ppermute | solution.py:236
  55.1 0.0 collective-permute-start.17
  55.1 1.4 %collective-permute-done.14.refs_4_ = bf16[32,2176]{1,0:T(8,128)(2,1)S(1)} collective-permute-done((bf16[32,2176]{1,0:T(8,128)(2,1)S(1)}, bf16[32,2176]{1,0:T(8,128)(2,1)S(1)}, u32[]{:S(2)}, u32[]{:S(2)}) %collective-permute-start.14) | collective-permute-done | bytes 139296 | tf_op jit(solution)/shard_map/ppermute | solution.py:236
  56.5 0.0 collective-permute-start.15
  56.5 0.5 collective-permute-done.12.refs_2_
  57.0 0.0 collective-permute-start.13
  57.0 2.9 %collective-permute-done.19 = bf16[512,128]{1,0:T(8,128)(2,1)S(1)} collective-permute-done((bf16[512,128]{1,0:T(8,128)(2,1)S(1)}, bf16[512,128]{1,0:T(8,128)(2,1)S(1)}, u32[]{:S(2)}, u32[]{:S(2)}) %collective-permute-start.19) | collective-permute-done | bytes 131104 | tf_op jit(solution)/shard_map/ppermute | solution.py:236
  59.9 0.7 %add_convert_fusion = bf16[512,128]{1,0:T(8,128)(2,1)} fusion(bf16[512,128]{1,0:T(8,128)(2,1)S(1)} %collective-permute-done.19, f32[512,128]{1,0:T(8,128)S(1)} %get-tuple-element.45, bf16[512,128]{1,0:T(8,128)(2,1)S(1)} %collective-permute-done.18), kind=kLoop, calls=%fused_computation.3 | loop fusion | flops 327680 | bytes 655360 | tf_op jit(solution)/shard_map/convert_element_type | solution.py:361
  60.6 0.0 collective-permute-done.13.refs_3_
  60.6 1.1 %place.1 = (bf16[256,2048]{1,0:T(8,128)(2,1)}, bf16[16,256]{1,0:T(8,128)(2,1)}, bf16[256]{0:T(256)(128)(2,1)}) custom-call(bf16[32,2176]{1,0:T(8,128)(2,1)S(1)} %bitcast.25, bf16[32,2176]{1,0:T(8,128)(2,1)S(1)} %collective-permute-done.11.refs_1_, bf16[32,2176]{1,0:T(8,128)(2,1)S(1)} %collective-permute-done.12.refs_2_, ...), custom_call_target="tpu_custom_call" | custom-call | bytes 4456448 | tf_op jit(solution)/shard_map/place/pallas_call | solution.py:342
  (7 shorter events, 0.0 us)
Async XLA Ops:
  0.6 11.7 %collective-permute-start.1 = (bf16[512,128]{1,0:T(8,128)(2,1)}, bf16[512,128]{1,0:T(8,128)(2,1)S(1)}, u32[]{:S(2)}, u32[]{:S(2)}) collective-permute-start(bf16[512,128]{1,0:T(8,128)(2,1)} %refs_0_.1), channel_id=1, source_target_pairs={{0,4},{1,5},{2,6},{3,7},{4,0},{5,1},{6,2},{7,3},{8,12},{9,13},{10,... | collective-permute-start | bytes 393224 | tf_op jit(solution)/shard_map/ppermute | solution.py:236
  3.7 8.7 %collective-permute-start = (bf16[512,128]{1,0:T(8,128)(2,1)}, bf16[512,128]{1,0:T(8,128)(2,1)S(1)}, u32[]{:S(2)}, u32[]{:S(2)}) collective-permute-start(bf16[512,128]{1,0:T(8,128)(2,1)} %refs_0_.1), channel_id=1, source_target_pairs={{0,2},{1,3},{2,0},{3,1},{4,6},{5,7},{6,4},{7,5},{8,10},{9,11},{10,... | collective-permute-start | bytes 393224 | tf_op jit(solution)/shard_map/ppermute | solution.py:236
  5.8 10.5 %copy-start = (bf16[512,128]{1,0:T(8,128)(2,1)S(1)}, bf16[512,128]{1,0:T(8,128)(2,1)}, u32[]{:S(2)}) copy-start(bf16[512,128]{1,0:T(8,128)(2,1)} %refs_0_.1) | copy-start | bytes 393220
  12.3 17.1 %all-to-all-start = ((bf16[32,8,896]{2,1,0:T(8,128)(2,1)}), bf16[32,8,896]{2,1,0:T(8,128)(2,1)S(1)}, u32[]{:S(2)}, u32[]{:S(2)}) async-start(bf16[32,8,896]{2,1,0:T(8,128)(2,1)} %bitcast.27), calls=%async_computation | async-start | bytes 917504 | tf_op jit(solution)/shard_map/all_to_all | solution.py:272
  16.3 10.1 %collective-permute-start.5 = (bf16[512,128]{1,0:T(8,128)(2,1)S(1)}, bf16[512,128]{1,0:T(8,128)(2,1)S(1)}, u32[]{:S(2)}, u32[]{:S(2)}) collective-permute-start(bf16[512,128]{1,0:T(8,128)(2,1)S(1)} %copy-done), channel_id=1, source_target_pairs={{0,6},{1,7},{2,4},{3,5},{4,2},{5,3},{6,0},{7,1},{8,14},{9,15},{10,... | collective-permute-start | bytes 393224 | tf_op jit(solution)/shard_map/ppermute | solution.py:236
  19.1 8.7 %collective-permute-start.2 = (bf16[512,128]{1,0:T(8,128)(2,1)S(1)}, bf16[512,128]{1,0:T(8,128)(2,1)S(1)}, u32[]{:S(2)}, u32[]{:S(2)}) collective-permute-start(bf16[512,128]{1,0:T(8,128)(2,1)S(1)} %copy-done), channel_id=1, source_target_pairs={{0,1},{1,0},{2,3},{3,2},{4,5},{5,4},{6,7},{7,6},{8,9},{9,8},{10,11... | collective-permute-start | bytes 393224 | tf_op jit(solution)/shard_map/ppermute | solution.py:236
  26.4 1.3 %collective-permute-start.6 = (bf16[512,128]{1,0:T(8,128)(2,1)S(1)}, bf16[512,128]{1,0:T(8,128)(2,1)S(1)}, u32[]{:S(2)}, u32[]{:S(2)}) collective-permute-start(bf16[512,128]{1,0:T(8,128)(2,1)S(1)} %collective-permute-done.5.refs_6_), channel_id=1, source_target_pairs={{0,1},{1,0},{2,3},{3,2},{4,5},{5,4},{6,7},{7,6},{8,9},{9,8},{10,11... | collective-permute-start | bytes 393224 | tf_op jit(solution)/shard_map/ppermute | solution.py:236
  26.4 1.5 %collective-permute-start.3 = (bf16[512,128]{1,0:T(8,128)(2,1)S(1)}, bf16[512,128]{1,0:T(8,128)(2,1)S(1)}, u32[]{:S(2)}, u32[]{:S(2)}) collective-permute-start(bf16[512,128]{1,0:T(8,128)(2,1)S(1)} %collective-permute-done.refs_2_), channel_id=1, source_target_pairs={{0,1},{1,0},{2,3},{3,2},{4,5},{5,4},{6,7},{7,6},{8,9},{9,8},{10,11... | collective-permute-start | bytes 393224 | tf_op jit(solution)/shard_map/ppermute | solution.py:236
  26.9 1.3 %collective-permute-start.4 = (bf16[512,128]{1,0:T(8,128)(2,1)S(1)}, bf16[512,128]{1,0:T(8,128)(2,1)S(1)}, u32[]{:S(2)}, u32[]{:S(2)}) collective-permute-start(bf16[512,128]{1,0:T(8,128)(2,1)S(1)} %collective-permute-done.1.refs_4_), channel_id=1, source_target_pairs={{0,1},{1,0},{2,3},{3,2},{4,5},{5,4},{6,7},{7,6},{8,9},{9,8},{10,11... | collective-permute-start | bytes 393224 | tf_op jit(solution)/shard_map/ppermute | solution.py:236
  32.1 2.8 %collective-permute-start.7 = (bf16[4,512,128]{2,1,0:T(8,128)(2,1)S(1)}, bf16[4,512,128]{2,1,0:T(8,128)(2,1)S(1)}, u32[]{:S(2)}, u32[]{:S(2)}) collective-permute-start(bf16[4,512,128]{2,1,0:T(8,128)(2,1)S(1)} %get-tuple-element.32), channel_id=1, source_target_pairs={{0,1},{1,0},{2,3},{3,2},{4,5},{5,4},{6,7},{7,6},{8,9},{9,8},{10,11... | collective-permute-start | bytes 1572872 | tf_op jit(solution)/shard_map/ppermute | solution.py:236
  35.0 7.7 %collective-permute-start.8 = (bf16[512,128]{1,0:T(8,128)(2,1)S(1)}, bf16[512,128]{1,0:T(8,128)(2,1)S(1)}, u32[]{:S(2)}, u32[]{:S(2)}) collective-permute-start(bf16[512,128]{1,0:T(8,128)(2,1)S(1)} %get-tuple-element.37), channel_id=1, source_target_pairs={{0,2},{1,3},{2,0},{3,1},{4,6},{5,7},{6,4},{7,5},{8,10},{9,11},{10,... | collective-permute-start | bytes 393224 | tf_op jit(solution)/shard_map/ppermute | solution.py:236
  36.5 8.2 %collective-permute-start.9 = (bf16[512,128]{1,0:T(8,128)(2,1)S(1)}, bf16[512,128]{1,0:T(8,128)(2,1)S(1)}, u32[]{:S(2)}, u32[]{:S(2)}) collective-permute-start(bf16[512,128]{1,0:T(8,128)(2,1)S(1)} %get-tuple-element.38), channel_id=1, source_target_pairs={{0,4},{1,5},{2,6},{3,7},{4,0},{5,1},{6,2},{7,3},{8,12},{9,13},{10,... | collective-permute-start | bytes 393224 | tf_op jit(solution)/shard_map/ppermute | solution.py:236
  37.0 7.7 %collective-permute-start.10 = (bf16[512,128]{1,0:T(8,128)(2,1)S(1)}, bf16[512,128]{1,0:T(8,128)(2,1)S(1)}, u32[]{:S(2)}, u32[]{:S(2)}) collective-permute-start(bf16[512,128]{1,0:T(8,128)(2,1)S(1)} %get-tuple-element.39), channel_id=1, source_target_pairs={{0,6},{1,7},{2,4},{3,5},{4,2},{5,3},{6,0},{7,1},{8,14},{9,15},{10,... | collective-permute-start | bytes 393224 | tf_op jit(solution)/shard_map/ppermute | solution.py:236
  39.3 9.7 %all-to-all-start.1 = ((bf16[4,8,2176]{2,1,0:T(8,128)(2,1)}), bf16[4,8,2176]{2,1,0:T(8,128)(2,1)S(1)}, u32[]{:S(2)}, u32[]{:S(2)}) async-start(bf16[4,8,2176]{2,1,0:T(8,128)(2,1)} %bitcast.8), calls=%async_computation.1 | async-start | bytes 278528 | tf_op jit(solution)/shard_map/all_to_all | solution.py:330
  44.8 7.8 %collective-permute-start.18 = (bf16[512,128]{1,0:T(8,128)(2,1)S(1)}, bf16[512,128]{1,0:T(8,128)(2,1)S(1)}, u32[]{:S(2)}, u32[]{:S(2)}) collective-permute-start(bf16[512,128]{1,0:T(8,128)(2,1)S(1)} %get-tuple-element.44), channel_id=1, source_target_pairs={{0,8},{8,0},{16,24},{24,16},{1,9},{9,1},{17,25},{25,17},{2,10},{10... | collective-permute-start | bytes 393224 | tf_op jit(solution)/shard_map/ppermute | solution.py:236
  49.1 6.1 %collective-permute-start.16 = (bf16[32,2176]{1,0:T(8,128)(2,1)S(1)}, bf16[32,2176]{1,0:T(8,128)(2,1)S(1)}, u32[]{:S(2)}, u32[]{:S(2)}) collective-permute-start(bf16[32,2176]{1,0:T(8,128)(2,1)S(1)} %bitcast.21), channel_id=1, source_target_pairs={{0,6},{1,7},{2,4},{3,5},{4,2},{5,3},{6,0},{7,1},{8,14},{9,15},{10,... | collective-permute-start | bytes 417800 | tf_op jit(solution)/shard_map/ppermute | solution.py:236
  50.5 6.0 %collective-permute-start.14 = (bf16[32,2176]{1,0:T(8,128)(2,1)S(1)}, bf16[32,2176]{1,0:T(8,128)(2,1)S(1)}, u32[]{:S(2)}, u32[]{:S(2)}) collective-permute-start(bf16[32,2176]{1,0:T(8,128)(2,1)S(1)} %bitcast.22), channel_id=1, source_target_pairs={{0,4},{1,5},{2,6},{3,7},{4,0},{5,1},{6,2},{7,3},{8,12},{9,13},{10,... | collective-permute-start | bytes 417800 | tf_op jit(solution)/shard_map/ppermute | solution.py:236
  51.9 5.1 %collective-permute-start.12 = (bf16[32,2176]{1,0:T(8,128)(2,1)S(1)}, bf16[32,2176]{1,0:T(8,128)(2,1)S(1)}, u32[]{:S(2)}, u32[]{:S(2)}) collective-permute-start(bf16[32,2176]{1,0:T(8,128)(2,1)S(1)} %bitcast.23), channel_id=1, source_target_pairs={{0,2},{1,3},{2,0},{3,1},{4,6},{5,7},{6,4},{7,5},{8,10},{9,11},{10,... | collective-permute-start | bytes 417800 | tf_op jit(solution)/shard_map/ppermute | solution.py:236
  52.6 7.3 %collective-permute-start.19 = (bf16[512,128]{1,0:T(8,128)(2,1)S(1)}, bf16[512,128]{1,0:T(8,128)(2,1)S(1)}, u32[]{:S(2)}, u32[]{:S(2)}) collective-permute-start(bf16[512,128]{1,0:T(8,128)(2,1)S(1)} %fusion.2), channel_id=1, source_target_pairs={{0,16},{8,24},{16,0},{24,8},{1,17},{9,25},{17,1},{25,9},{2,18},{10... | collective-permute-start | bytes 393224 | tf_op jit(solution)/shard_map/ppermute | solution.py:236
  54.0 6.7 %collective-permute-start.11 = (bf16[32,2176]{1,0:T(8,128)(2,1)S(1)}, bf16[32,2176]{1,0:T(8,128)(2,1)S(1)}, u32[]{:S(2)}, u32[]{:S(2)}) collective-permute-start(bf16[32,2176]{1,0:T(8,128)(2,1)S(1)} %bitcast.24), channel_id=1, source_target_pairs={{0,1},{1,0},{2,3},{3,2},{4,5},{5,4},{6,7},{7,6},{8,9},{9,8},{10,11... | collective-permute-start | bytes 417800 | tf_op jit(solution)/shard_map/ppermute | solution.py:236
  55.1 5.5 %collective-permute-start.17 = (bf16[32,2176]{1,0:T(8,128)(2,1)S(1)}, bf16[32,2176]{1,0:T(8,128)(2,1)S(1)}, u32[]{:S(2)}, u32[]{:S(2)}) collective-permute-start(bf16[32,2176]{1,0:T(8,128)(2,1)S(1)} %collective-permute-done.16.refs_6_), channel_id=1, source_target_pairs={{0,1},{1,0},{2,3},{3,2},{4,5},{5,4},{6,7},{7,6},{8,9},{9,8},{10,11... | collective-permute-start | bytes 417800 | tf_op jit(solution)/shard_map/ppermute | solution.py:236
  56.5 4.1 %collective-permute-start.15 = (bf16[32,2176]{1,0:T(8,128)(2,1)S(1)}, bf16[32,2176]{1,0:T(8,128)(2,1)S(1)}, u32[]{:S(2)}, u32[]{:S(2)}) collective-permute-start(bf16[32,2176]{1,0:T(8,128)(2,1)S(1)} %collective-permute-done.14.refs_4_), channel_id=1, source_target_pairs={{0,1},{1,0},{2,3},{3,2},{4,5},{5,4},{6,7},{7,6},{8,9},{9,8},{10,11... | collective-permute-start | bytes 417800 | tf_op jit(solution)/shard_map/ppermute | solution.py:236
  57.0 3.6 %collective-permute-start.13 = (bf16[32,2176]{1,0:T(8,128)(2,1)S(1)}, bf16[32,2176]{1,0:T(8,128)(2,1)S(1)}, u32[]{:S(2)}, u32[]{:S(2)}) collective-permute-start(bf16[32,2176]{1,0:T(8,128)(2,1)S(1)} %collective-permute-done.12.refs_2_), channel_id=1, source_target_pairs={{0,1},{1,0},{2,3},{3,2},{4,5},{5,4},{6,7},{7,6},{8,9},{9,8},{10,11... | collective-permute-start | bytes 417800 | tf_op jit(solution)/shard_map/ppermute | solution.py:236

commit v5 on v4

--- a/solution.py
+++ b/solution.py
@@ -65,13 +65,6 @@
     share_copy.start()
     for copy in small:
         copy.wait()
-    padded = jnp.concatenate([hw_ref[...], jnp.zeros((LANES - heads, rows), F32)], axis=0)
-    weight = jnp.transpose(padded)
-    high = weight.astype(BF16).astype(F32)
-    rest = weight - high
-    mid = rest.astype(BF16).astype(F32)
-    side = high + pltpu.roll(mid, heads, 1) + pltpu.roll(rest - mid, 2 * heads, 1)
-    out_ref[:, keys + cols :] = side.astype(BF16)
     first = 0
     for i, n in enumerate(parts):
         for copy in large[i]:
@@ -93,8 +86,20 @@
             acc_ref[...] += total
         first += n
     position = block_ref[0] * keys + lax.broadcasted_iota(jnp.int32, (keys, rows), 0)
-    share = jnp.where(position <= pos_ref[...], acc_ref[...], -1.0)
+    valid = position <= pos_ref[...]
+    largest = float(jnp.finfo(F32).max)
+    least = jnp.min(jnp.where(valid, acc_ref[...], largest), axis=0, keepdims=True)
+    least = jnp.where(least < largest, least, 0.0)
+    share = jnp.where(valid, acc_ref[...] - least, -1.0)
     out_ref[:, :keys] = jnp.transpose(share).astype(BF16)
+    padded = jnp.concatenate([hw_ref[...], jnp.zeros((LANES - heads, rows), F32)], axis=0)
+    sub = lax.broadcasted_iota(jnp.int32, (LANES, rows), 0)
+    terms = jnp.transpose(jnp.where(sub == heads, least, padded))
+    high = terms.astype(BF16).astype(F32)
+    rest = terms - high
+    mid = rest.astype(BF16).astype(F32)
+    side = high + pltpu.roll(mid, heads + 1, 1) + pltpu.roll(rest - mid, 2 * (heads + 1), 1)
+    out_ref[:, keys + cols :] = side.astype(BF16)
     share_copy.wait()
 
 
@@ -108,6 +113,10 @@
     per = heads // n_seq
     cols = per * width
     group = n_head * own
+
+    def three(terms, i):
+        return sum([terms[:, j : j + 1] for j in range(i + heads + 1, LANES, heads + 1)][:2], terms[:, i : i + 1])
+
     for ss in range(n_seq):
         for pair in range(0, n_head, 2):
             at = ss * group + pair * own
@@ -122,8 +131,7 @@
         for e in range(2):
             side = both[e * own : (e + 1) * own]
             for i in range(heads):
-                one = side[:, i : i + 1] + side[:, heads + i : heads + i + 1] + side[:, 2 * heads + i : 2 * heads + i + 1]
-                wide_ref[(pair + e) * heads + i] = jnp.broadcast_to(one, (own, LANES))
+                wide_ref[(pair + e) * heads + i] = jnp.broadcast_to(three(side, i), (own, LANES))
     for k in range(n_seq):
         dots = lax.dot_general(q_ref[...], key_refs[k][...], NT, preferred_element_type=F32)
         dots_ref[k] = dots.astype(BF16)
@@ -135,8 +143,9 @@
     for k in range(n_seq):
         src = pl.multiple_of((s ^ k) * group, group)
         cube = got_ref[pl.ds(src, group), :keys].astype(F32).reshape(n_head, own, keys)
+        least = three(got_ref[pl.ds(src, group), keys + cols :].astype(F32), heads).reshape(n_head, own, 1)
         valid = cube[0] >= 0.0
-        shares.append(jnp.where(valid, jnp.sum(cube, axis=0), 0.0))
+        shares.append(jnp.where(valid, jnp.sum(cube, axis=0) + jnp.sum(least, axis=0), 0.0))
         valids.append(valid)
         logits.append(jnp.where(valid, logit_ref[k], -1e30))
         peak = jnp.maximum(peak, jnp.max(logits[k], axis=1, keepdims=True))
@@ -431,7 +440,7 @@
     def local(*args):
         rows, heads = args[0].shape[0], args[5].shape[1]
         paired = all(n & (n - 1) == 0 and n > 1 for n in (n_seq, n_head))
-        if paired and rows == 8 * n_seq * n_head and heads % n_seq == 0:
+        if paired and rows == 8 * n_seq * n_head and heads % n_seq == 0 and 3 * heads + 3 <= LANES:
             return fast_local(n_seq, n_head, *args)
         return plain_local(*args)
 

time: 62 us -> 62.2 us (level)
  transfers between devices with their start and end apart: 22 -> 22, of which waited for: 11 -> 11; matrix products, arithmetic and copies ran while one was open for 1% -> 1% of each run, Pallas kernels for 14% -> 15%
where the time goes in v5:
time: 62.2 us; the launch traced here: 61.9 us
  starting transfers between devices  25.2 us (41%)
  waiting for transfers between devices  21.5 us (35%)
  Pallas kernels  12.9 us (21%)
  between operations  1.41 us (2%)
  other arithmetic  0.9 us (1%)
    ppermute x20, starting transfers between devices, swap(): return lax.ppermute(x, axis, [(i, i ^ mask) for i in range(n)])  17.9 us
    ppermute x20, waiting for transfers between devices, swap(): return lax.ppermute(x, axis, [(i, i ^ mask) for i in range(n)])  16.6 us
    pallas_call x1, Pallas kernels, fast_local(): pl.pallas_call(functools.partial(attention_kernel, parts), in_specs=[hbm]...  6.69 us
    all_to_all x1, starting transfers between devices, fast_local(): got = lax.all_to_all(sent, ('seq', 'head'), 0, 0, tiled=True)  3.98 us
    all_to_all x1, waiting for transfers between devices, fast_local(): own_rows = lax.all_to_all(rows_out, 'head', 0, 0, tiled=True)  3.74 us
    all_to_all x1, starting transfers between devices, fast_local(): own_rows = lax.all_to_all(rows_out, 'head', 0, 0, tiled=True)  3.34 us
    pallas_call x1, Pallas kernels, fast_local(): pl.pallas_call(functools.partial(keys_kernel, n_seq, n_head, own), in_spe...  2.67 us
    pallas_call x1, Pallas kernels, fast_local(): pl.pallas_call(functools.partial(products_kernel, n_seq), in_specs=[vmem_...  1.63 us
  transfers between devices with their start and end apart: 22, of which 11 were waited for; matrix products, arithmetic and copies ran while one was open for 1% of the time, Pallas kernels for 15%

profile of v5, /device:TPU:0, one launch (start us, length us, event | category | flops | bytes accessed | tf_op | source)
XLA Modules:
  0.0 61.9 jit_solution(12283523975560483677)
XLA Ops:
  0.6 3.0 %collective-permute-start.1 = (bf16[512,128]{1,0:T(8,128)(2,1)}, bf16[512,128]{1,0:T(8,128)(2,1)S(1)}, u32[]{:S(2)}, u32[]{:S(2)}) collective-permute-start(bf16[512,128]{1,0:T(8,128)(2,1)} %refs_0_.1), channel_id=1, source_target_pairs={{0,4},{1,5},{2,6},{3,7},{4,0},{5,1},{6,2},{7,3},{8,12},{9,13},{10,... | collective-permute-start | bytes 393224 | tf_op jit(solution)/shard_map/ppermute | solution.py:245
  3.7 1.5 %collective-permute-start = (bf16[512,128]{1,0:T(8,128)(2,1)}, bf16[512,128]{1,0:T(8,128)(2,1)S(1)}, u32[]{:S(2)}, u32[]{:S(2)}) collective-permute-start(bf16[512,128]{1,0:T(8,128)(2,1)} %refs_0_.1), channel_id=1, source_target_pairs={{0,2},{1,3},{2,0},{3,1},{4,6},{5,7},{6,4},{7,5},{8,10},{9,11},{10,... | collective-permute-start | bytes 393224 | tf_op jit(solution)/shard_map/ppermute | solution.py:245
  5.8 6.7 %attention.1 = bf16[256,896]{1,0:T(8,128)(2,1)} custom-call(s32[1]{0:T(128)S(6)} %copy.12.block_hbm, s32[1,256]{1,0:T(1,128)} %bitcast.31, bf16[256,6144]{1,0:T(8,128)(2,1)} %q_hbm.1, bf16[512,6144]{1,0:T(8,128)(2,1)} %k_hbm.1, f32[32,256]{1,0:T(8,128)} %bitcast.28, bf16[256,2048]{1,0:T(8,128)(2,1)} %qi_hbm.1, f32[16,256]{1,0:T(8,128)} %bitcast.29), custom_call_target="tpu_custom_call" | custom-call | flops 3221225472 | bytes 9437184 | tf_op jit(solution)/shard_map/attention/pallas_call | solution.py:253
  12.5 0.0 collective-permute-done.1.refs_4_
  12.5 0.0 collective-permute-done.refs_2_
  12.5 4.0 %all-to-all-start = ((bf16[32,8,896]{2,1,0:T(8,128)(2,1)}), bf16[32,8,896]{2,1,0:T(8,128)(2,1)S(1)}, u32[]{:S(2)}, u32[]{:S(2)}) async-start(bf16[32,8,896]{2,1,0:T(8,128)(2,1)} %bitcast.27), calls=%async_computation | async-start | bytes 917504 | tf_op jit(solution)/shard_map/all_to_all | solution.py:281
  16.5 2.7 %collective-permute-start.5 = (bf16[512,128]{1,0:T(8,128)(2,1)S(1)}, bf16[512,128]{1,0:T(8,128)(2,1)S(1)}, u32[]{:S(2)}, u32[]{:S(2)}) collective-permute-start(bf16[512,128]{1,0:T(8,128)(2,1)S(1)} %copy-done), channel_id=1, source_target_pairs={{0,6},{1,7},{2,4},{3,5},{4,2},{5,3},{6,0},{7,1},{8,14},{9,15},{10,... | collective-permute-start | bytes 393224 | tf_op jit(solution)/shard_map/ppermute | solution.py:245
  19.3 0.0 collective-permute-start.2
  19.3 7.3 %collective-permute-done.5.refs_6_ = bf16[512,128]{1,0:T(8,128)(2,1)S(1)} collective-permute-done((bf16[512,128]{1,0:T(8,128)(2,1)S(1)}, bf16[512,128]{1,0:T(8,128)(2,1)S(1)}, u32[]{:S(2)}, u32[]{:S(2)}) %collective-permute-start.5) | collective-permute-done | bytes 131104 | tf_op jit(solution)/shard_map/ppermute | solution.py:245
  26.6 0.0 collective-permute-start.6
  26.6 0.5 collective-permute-start.3
  27.1 0.0 collective-permute-start.4
  27.1 0.8 %collective-permute-done.6.refs_7_ = bf16[512,128]{1,0:T(8,128)(2,1)S(1)} collective-permute-done((bf16[512,128]{1,0:T(8,128)(2,1)S(1)}, bf16[512,128]{1,0:T(8,128)(2,1)S(1)}, u32[]{:S(2)}, u32[]{:S(2)}) %collective-permute-start.6) | collective-permute-done | bytes 131104 | tf_op jit(solution)/shard_map/ppermute | solution.py:245
  28.0 0.0 collective-permute-done.2.refs_1_
  28.0 0.2 collective-permute-done.3.refs_3_
  28.1 0.3 collective-permute-done.4.refs_5_
  28.5 1.2 %all-to-all-done = bf16[32,8,896]{2,1,0:T(8,128)(2,1)S(1)} async-done(((bf16[32,8,896]{2,1,0:T(8,128)(2,1)}), bf16[32,8,896]{2,1,0:T(8,128)(2,1)S(1)}, u32[]{:S(2)}, u32[]{:S(2)}) %all-to-all-start) | async-done | bytes 458784 | tf_op jit(solution)/shard_map/all_to_all | solution.py:281
  29.6 2.7 %key_grad.1 = (bf16[4,512,128]{2,1,0:T(8,128)(2,1)S(1)}, bf16[8,512,512]{2,1,0:T(8,128)(2,1)S(1)}, bf16[512,128]{1,0:T(8,128)(2,1)S(1)}, f32[64,8,128]{2,1,0:T(8...) custom-call(bf16[256,896]{1,0:T(8,128)(2,1)S(1)} %bitcast.26, bf16[512,128]{1,0:T(8,128)(2,1)S(1)} %copy-done, ...), custom_call_target="tpu_custom_call" | custom-call | flops 1073741824 | bytes 2097152 | tf_op jit(solution)/shard_map/key_grad/pallas_call | solution.py:289
  32.3 1.1 %collective-permute-start.7 = (bf16[4,512,128]{2,1,0:T(8,128)(2,1)S(1)}, bf16[4,512,128]{2,1,0:T(8,128)(2,1)S(1)}, u32[]{:S(2)}, u32[]{:S(2)}) collective-permute-start(bf16[4,512,128]{2,1,0:T(8,128)(2,1)S(1)} %get-tuple-element.32), channel_id=1, source_target_pairs={{0,1},{1,0},{2,3},{3,2},{4,5},{5,4},{6,7},{7,6},{8,9},{9,8},{10,11... | collective-permute-start | bytes 1572872 | tf_op jit(solution)/shard_map/ppermute | solution.py:245
  33.4 1.6 %products.1 = (f32[4,512,128]{2,1,0:T(8,128)S(1)}, f32[512,128]{1,0:T(8,128)S(1)}) custom-call(bf16[8,512,512]{2,1,0:T(8,128)(2,1)S(1)} %get-tuple-element.28.gated_ref, bf16[128,512]{1,0:T(8,128)(2,1)S(1)} %get-tuple-element.29.weighted_ref, bf16[512,128]{1,0:T(8,128)(2,1)S(1)} %copy-done, bf16[512,128]{1,0:T(8,128)(2,1)S(1)} %collective-permute-done.2.refs_1_, ...), custom_call_target="tpu_custom_call" | custom-call | flops 1073741824 | bytes 2097152 | tf_op jit(solution)/shard_map/products/pallas_call | solution.py:311
  35.1 0.1 fusion.5
  35.2 1.5 %collective-permute-start.8 = (bf16[512,128]{1,0:T(8,128)(2,1)S(1)}, bf16[512,128]{1,0:T(8,128)(2,1)S(1)}, u32[]{:S(2)}, u32[]{:S(2)}) collective-permute-start(bf16[512,128]{1,0:T(8,128)(2,1)S(1)} %get-tuple-element.37), channel_id=1, source_target_pairs={{0,2},{1,3},{2,0},{3,1},{4,6},{5,7},{6,4},{7,5},{8,10},{9,11},{10,... | collective-permute-start | bytes 393224 | tf_op jit(solution)/shard_map/ppermute | solution.py:245
  36.7 0.5 collective-permute-start.9
  37.2 1.5 %collective-permute-start.10 = (bf16[512,128]{1,0:T(8,128)(2,1)S(1)}, bf16[512,128]{1,0:T(8,128)(2,1)S(1)}, u32[]{:S(2)}, u32[]{:S(2)}) collective-permute-start(bf16[512,128]{1,0:T(8,128)(2,1)S(1)} %get-tuple-element.39), channel_id=1, source_target_pairs={{0,6},{1,7},{2,4},{3,5},{4,2},{5,3},{6,0},{7,1},{8,14},{9,15},{10,... | collective-permute-start | bytes 393224 | tf_op jit(solution)/shard_map/ppermute | solution.py:245
  38.7 0.8 %query_grad.1 = bf16[32,2176]{1,0:T(8,128)(2,1)} custom-call(f32[512,128]{1,0:T(8,128)S(1)} %get-tuple-element.33.term_ref, bf16[512,128]{1,0:T(8,128)(2,1)S(1)} %get-tuple-element.34.q_ref, f32[64,8,128]{2,1,0:T(8,128)S(1)} %get-tuple-element.35.wide_ref, f32[8,128]{1,0:T(8,128)S(1)} %get-tuple-element.36.kl_ref), custom_call_target="tpu_custom_call" | custom-call | bytes 2097152 | tf_op jit(solution)/shard_map/query_grad/pallas_call | solution.py:330
  39.5 3.3 %all-to-all-start.1 = ((bf16[4,8,2176]{2,1,0:T(8,128)(2,1)}), bf16[4,8,2176]{2,1,0:T(8,128)(2,1)S(1)}, u32[]{:S(2)}, u32[]{:S(2)}) async-start(bf16[4,8,2176]{2,1,0:T(8,128)(2,1)} %bitcast.8), calls=%async_computation.1 | async-start | bytes 278528 | tf_op jit(solution)/shard_map/all_to_all | solution.py:339
  42.9 0.0 collective-permute-done.8
  42.9 2.0 %collective-permute-done.9 = bf16[512,128]{1,0:T(8,128)(2,1)S(1)} collective-permute-done((bf16[512,128]{1,0:T(8,128)(2,1)S(1)}, bf16[512,128]{1,0:T(8,128)(2,1)S(1)}, u32[]{:S(2)}, u32[]{:S(2)}) %collective-permute-start.9) | collective-permute-done | bytes 131104 | tf_op jit(solution)/shard_map/ppermute | solution.py:245
  44.9 0.0 collective-permute-done.10
  44.9 0.1 fusion.6
  45.0 0.5 collective-permute-start.18
  45.5 3.7 %all-to-all-done.1 = bf16[4,8,2176]{2,1,0:T(8,128)(2,1)S(1)} async-done(((bf16[4,8,2176]{2,1,0:T(8,128)(2,1)}), bf16[4,8,2176]{2,1,0:T(8,128)(2,1)S(1)}, u32[]{:S(2)}, u32[]{:S(2)}) %all-to-all-start.1) | async-done | bytes 139296 | tf_op jit(solution)/shard_map/all_to_all | solution.py:339
  49.3 1.4 %collective-permute-start.16 = (bf16[32,2176]{1,0:T(8,128)(2,1)S(1)}, bf16[32,2176]{1,0:T(8,128)(2,1)S(1)}, u32[]{:S(2)}, u32[]{:S(2)}) collective-permute-start(bf16[32,2176]{1,0:T(8,128)(2,1)S(1)} %bitcast.21), channel_id=1, source_target_pairs={{0,6},{1,7},{2,4},{3,5},{4,2},{5,3},{6,0},{7,1},{8,14},{9,15},{10,... | collective-permute-start | bytes 417800 | tf_op jit(solution)/shard_map/ppermute | solution.py:245
  50.7 1.5 %collective-permute-start.14 = (bf16[32,2176]{1,0:T(8,128)(2,1)S(1)}, bf16[32,2176]{1,0:T(8,128)(2,1)S(1)}, u32[]{:S(2)}, u32[]{:S(2)}) collective-permute-start(bf16[32,2176]{1,0:T(8,128)(2,1)S(1)} %bitcast.22), channel_id=1, source_target_pairs={{0,4},{1,5},{2,6},{3,7},{4,0},{5,1},{6,2},{7,3},{8,12},{9,13},{10,... | collective-permute-start | bytes 417800 | tf_op jit(solution)/shard_map/ppermute | solution.py:245
  52.1 0.6 collective-permute-start.12
  52.7 0.0 collective-permute-done.18
  52.8 1.4 %collective-permute-start.19 = (bf16[512,128]{1,0:T(8,128)(2,1)S(1)}, bf16[512,128]{1,0:T(8,128)(2,1)S(1)}, u32[]{:S(2)}, u32[]{:S(2)}) collective-permute-start(bf16[512,128]{1,0:T(8,128)(2,1)S(1)} %fusion.2), channel_id=1, source_target_pairs={{0,16},{8,24},{16,0},{24,8},{1,17},{9,25},{17,1},{25,9},{2,18},{10... | collective-permute-start | bytes 393224 | tf_op jit(solution)/shard_map/ppermute | solution.py:245
  54.2 0.0 collective-permute-start.11
  54.2 1.2 %collective-permute-done.16.refs_6_ = bf16[32,2176]{1,0:T(8,128)(2,1)S(1)} collective-permute-done((bf16[32,2176]{1,0:T(8,128)(2,1)S(1)}, bf16[32,2176]{1,0:T(8,128)(2,1)S(1)}, u32[]{:S(2)}, u32[]{:S(2)}) %collective-permute-start.16) | collective-permute-done | bytes 139296 | tf_op jit(solution)/shard_map/ppermute | solution.py:245
  55.3 1.4 %collective-permute-done.14.refs_4_ = bf16[32,2176]{1,0:T(8,128)(2,1)S(1)} collective-permute-done((bf16[32,2176]{1,0:T(8,128)(2,1)S(1)}, bf16[32,2176]{1,0:T(8,128)(2,1)S(1)}, u32[]{:S(2)}, u32[]{:S(2)}) %collective-permute-start.14) | collective-permute-done | bytes 139296 | tf_op jit(solution)/shard_map/ppermute | solution.py:245
  56.7 0.5 collective-permute-done.12.refs_2_
  57.2 0.0 collective-permute-start.13
  57.2 2.9 %collective-permute-done.19 = bf16[512,128]{1,0:T(8,128)(2,1)S(1)} collective-permute-done((bf16[512,128]{1,0:T(8,128)(2,1)S(1)}, bf16[512,128]{1,0:T(8,128)(2,1)S(1)}, u32[]{:S(2)}, u32[]{:S(2)}) %collective-permute-start.19) | collective-permute-done | bytes 131104 | tf_op jit(solution)/shard_map/ppermute | solution.py:245
  60.1 0.7 %add_convert_fusion = bf16[512,128]{1,0:T(8,128)(2,1)} fusion(bf16[512,128]{1,0:T(8,128)(2,1)S(1)} %collective-permute-done.19, f32[512,128]{1,0:T(8,128)S(1)} %get-tuple-element.45, bf16[512,128]{1,0:T(8,128)(2,1)S(1)} %collective-permute-done.18), kind=kLoop, calls=%fused_computation.3 | loop fusion | flops 327680 | bytes 655360 | tf_op jit(solution)/shard_map/convert_element_type | solution.py:370
  60.8 0.0 collective-permute-done.11.refs_1_
  60.8 0.0 collective-permute-done.17.refs_7_
  60.8 0.0 collective-permute-done.15.refs_5_
  60.9 1.1 %place.1 = (bf16[256,2048]{1,0:T(8,128)(2,1)}, bf16[16,256]{1,0:T(8,128)(2,1)}, bf16[256]{0:T(256)(128)(2,1)}) custom-call(bf16[32,2176]{1,0:T(8,128)(2,1)S(1)} %bitcast.25, bf16[32,2176]{1,0:T(8,128)(2,1)S(1)} %collective-permute-done.11.refs_1_, bf16[32,2176]{1,0:T(8,128)(2,1)S(1)} %collective-permute-done.12.refs_2_, ...), custom_call_target="tpu_custom_call" | custom-call | bytes 4456448 | tf_op jit(solution)/shard_map/place/pallas_call | solution.py:351
  (7 shorter events, 0.0 us)
Async XLA Ops:
  0.6 11.9 %collective-permute-start.1 = (bf16[512,128]{1,0:T(8,128)(2,1)}, bf16[512,128]{1,0:T(8,128)(2,1)S(1)}, u32[]{:S(2)}, u32[]{:S(2)}) collective-permute-start(bf16[512,128]{1,0:T(8,128)(2,1)} %refs_0_.1), channel_id=1, source_target_pairs={{0,4},{1,5},{2,6},{3,7},{4,0},{5,1},{6,2},{7,3},{8,12},{9,13},{10,... | collective-permute-start | bytes 393224 | tf_op jit(solution)/shard_map/ppermute | solution.py:245
  3.7 8.9 %collective-permute-start = (bf16[512,128]{1,0:T(8,128)(2,1)}, bf16[512,128]{1,0:T(8,128)(2,1)S(1)}, u32[]{:S(2)}, u32[]{:S(2)}) collective-permute-start(bf16[512,128]{1,0:T(8,128)(2,1)} %refs_0_.1), channel_id=1, source_target_pairs={{0,2},{1,3},{2,0},{3,1},{4,6},{5,7},{6,4},{7,5},{8,10},{9,11},{10,... | collective-permute-start | bytes 393224 | tf_op jit(solution)/shard_map/ppermute | solution.py:245
  5.8 10.7 %copy-start = (bf16[512,128]{1,0:T(8,128)(2,1)S(1)}, bf16[512,128]{1,0:T(8,128)(2,1)}, u32[]{:S(2)}) copy-start(bf16[512,128]{1,0:T(8,128)(2,1)} %refs_0_.1) | copy-start | bytes 393220
  12.5 17.1 %all-to-all-start = ((bf16[32,8,896]{2,1,0:T(8,128)(2,1)}), bf16[32,8,896]{2,1,0:T(8,128)(2,1)S(1)}, u32[]{:S(2)}, u32[]{:S(2)}) async-start(bf16[32,8,896]{2,1,0:T(8,128)(2,1)} %bitcast.27), calls=%async_computation | async-start | bytes 917504 | tf_op jit(solution)/shard_map/all_to_all | solution.py:281
  16.5 10.1 %collective-permute-start.5 = (bf16[512,128]{1,0:T(8,128)(2,1)S(1)}, bf16[512,128]{1,0:T(8,128)(2,1)S(1)}, u32[]{:S(2)}, u32[]{:S(2)}) collective-permute-start(bf16[512,128]{1,0:T(8,128)(2,1)S(1)} %copy-done), channel_id=1, source_target_pairs={{0,6},{1,7},{2,4},{3,5},{4,2},{5,3},{6,0},{7,1},{8,14},{9,15},{10,... | collective-permute-start | bytes 393224 | tf_op jit(solution)/shard_map/ppermute | solution.py:245
  19.3 8.7 %collective-permute-start.2 = (bf16[512,128]{1,0:T(8,128)(2,1)S(1)}, bf16[512,128]{1,0:T(8,128)(2,1)S(1)}, u32[]{:S(2)}, u32[]{:S(2)}) collective-permute-start(bf16[512,128]{1,0:T(8,128)(2,1)S(1)} %copy-done), channel_id=1, source_target_pairs={{0,1},{1,0},{2,3},{3,2},{4,5},{5,4},{6,7},{7,6},{8,9},{9,8},{10,11... | collective-permute-start | bytes 393224 | tf_op jit(solution)/shard_map/ppermute | solution.py:245
  26.6 1.3 %collective-permute-start.6 = (bf16[512,128]{1,0:T(8,128)(2,1)S(1)}, bf16[512,128]{1,0:T(8,128)(2,1)S(1)}, u32[]{:S(2)}, u32[]{:S(2)}) collective-permute-start(bf16[512,128]{1,0:T(8,128)(2,1)S(1)} %collective-permute-done.5.refs_6_), channel_id=1, source_target_pairs={{0,1},{1,0},{2,3},{3,2},{4,5},{5,4},{6,7},{7,6},{8,9},{9,8},{10,11... | collective-permute-start | bytes 393224 | tf_op jit(solution)/shard_map/ppermute | solution.py:245
  26.6 1.5 %collective-permute-start.3 = (bf16[512,128]{1,0:T(8,128)(2,1)S(1)}, bf16[512,128]{1,0:T(8,128)(2,1)S(1)}, u32[]{:S(2)}, u32[]{:S(2)}) collective-permute-start(bf16[512,128]{1,0:T(8,128)(2,1)S(1)} %collective-permute-done.refs_2_), channel_id=1, source_target_pairs={{0,1},{1,0},{2,3},{3,2},{4,5},{5,4},{6,7},{7,6},{8,9},{9,8},{10,11... | collective-permute-start | bytes 393224 | tf_op jit(solution)/shard_map/ppermute | solution.py:245
  27.1 1.3 %collective-permute-start.4 = (bf16[512,128]{1,0:T(8,128)(2,1)S(1)}, bf16[512,128]{1,0:T(8,128)(2,1)S(1)}, u32[]{:S(2)}, u32[]{:S(2)}) collective-permute-start(bf16[512,128]{1,0:T(8,128)(2,1)S(1)} %collective-permute-done.1.refs_4_), channel_id=1, source_target_pairs={{0,1},{1,0},{2,3},{3,2},{4,5},{5,4},{6,7},{7,6},{8,9},{9,8},{10,11... | collective-permute-start | bytes 393224 | tf_op jit(solution)/shard_map/ppermute | solution.py:245
  32.3 2.8 %collective-permute-start.7 = (bf16[4,512,128]{2,1,0:T(8,128)(2,1)S(1)}, bf16[4,512,128]{2,1,0:T(8,128)(2,1)S(1)}, u32[]{:S(2)}, u32[]{:S(2)}) collective-permute-start(bf16[4,512,128]{2,1,0:T(8,128)(2,1)S(1)} %get-tuple-element.32), channel_id=1, source_target_pairs={{0,1},{1,0},{2,3},{3,2},{4,5},{5,4},{6,7},{7,6},{8,9},{9,8},{10,11... | collective-permute-start | bytes 1572872 | tf_op jit(solution)/shard_map/ppermute | solution.py:245
  35.2 7.7 %collective-permute-start.8 = (bf16[512,128]{1,0:T(8,128)(2,1)S(1)}, bf16[512,128]{1,0:T(8,128)(2,1)S(1)}, u32[]{:S(2)}, u32[]{:S(2)}) collective-permute-start(bf16[512,128]{1,0:T(8,128)(2,1)S(1)} %get-tuple-element.37), channel_id=1, source_target_pairs={{0,2},{1,3},{2,0},{3,1},{4,6},{5,7},{6,4},{7,5},{8,10},{9,11},{10,... | collective-permute-start | bytes 393224 | tf_op jit(solution)/shard_map/ppermute | solution.py:245
  36.7 8.2 %collective-permute-start.9 = (bf16[512,128]{1,0:T(8,128)(2,1)S(1)}, bf16[512,128]{1,0:T(8,128)(2,1)S(1)}, u32[]{:S(2)}, u32[]{:S(2)}) collective-permute-start(bf16[512,128]{1,0:T(8,128)(2,1)S(1)} %get-tuple-element.38), channel_id=1, source_target_pairs={{0,4},{1,5},{2,6},{3,7},{4,0},{5,1},{6,2},{7,3},{8,12},{9,13},{10,... | collective-permute-start | bytes 393224 | tf_op jit(solution)/shard_map/ppermute | solution.py:245
  37.2 7.6 %collective-permute-start.10 = (bf16[512,128]{1,0:T(8,128)(2,1)S(1)}, bf16[512,128]{1,0:T(8,128)(2,1)S(1)}, u32[]{:S(2)}, u32[]{:S(2)}) collective-permute-start(bf16[512,128]{1,0:T(8,128)(2,1)S(1)} %get-tuple-element.39), channel_id=1, source_target_pairs={{0,6},{1,7},{2,4},{3,5},{4,2},{5,3},{6,0},{7,1},{8,14},{9,15},{10,... | collective-permute-start | bytes 393224 | tf_op jit(solution)/shard_map/ppermute | solution.py:245
  39.5 9.7 %all-to-all-start.1 = ((bf16[4,8,2176]{2,1,0:T(8,128)(2,1)}), bf16[4,8,2176]{2,1,0:T(8,128)(2,1)S(1)}, u32[]{:S(2)}, u32[]{:S(2)}) async-start(bf16[4,8,2176]{2,1,0:T(8,128)(2,1)} %bitcast.8), calls=%async_computation.1 | async-start | bytes 278528 | tf_op jit(solution)/shard_map/all_to_all | solution.py:339
  45.0 7.8 %collective-permute-start.18 = (bf16[512,128]{1,0:T(8,128)(2,1)S(1)}, bf16[512,128]{1,0:T(8,128)(2,1)S(1)}, u32[]{:S(2)}, u32[]{:S(2)}) collective-permute-start(bf16[512,128]{1,0:T(8,128)(2,1)S(1)} %get-tuple-element.44), channel_id=1, source_target_pairs={{0,8},{8,0},{16,24},{24,16},{1,9},{9,1},{17,25},{25,17},{2,10},{10... | collective-permute-start | bytes 393224 | tf_op jit(solution)/shard_map/ppermute | solution.py:245
  49.3 6.1 %collective-permute-start.16 = (bf16[32,2176]{1,0:T(8,128)(2,1)S(1)}, bf16[32,2176]{1,0:T(8,128)(2,1)S(1)}, u32[]{:S(2)}, u32[]{:S(2)}) collective-permute-start(bf16[32,2176]{1,0:T(8,128)(2,1)S(1)} %bitcast.21), channel_id=1, source_target_pairs={{0,6},{1,7},{2,4},{3,5},{4,2},{5,3},{6,0},{7,1},{8,14},{9,15},{10,... | collective-permute-start | bytes 417800 | tf_op jit(solution)/shard_map/ppermute | solution.py:245
  50.7 6.0 %collective-permute-start.14 = (bf16[32,2176]{1,0:T(8,128)(2,1)S(1)}, bf16[32,2176]{1,0:T(8,128)(2,1)S(1)}, u32[]{:S(2)}, u32[]{:S(2)}) collective-permute-start(bf16[32,2176]{1,0:T(8,128)(2,1)S(1)} %bitcast.22), channel_id=1, source_target_pairs={{0,4},{1,5},{2,6},{3,7},{4,0},{5,1},{6,2},{7,3},{8,12},{9,13},{10,... | collective-permute-start | bytes 417800 | tf_op jit(solution)/shard_map/ppermute | solution.py:245
  52.1 5.1 %collective-permute-start.12 = (bf16[32,2176]{1,0:T(8,128)(2,1)S(1)}, bf16[32,2176]{1,0:T(8,128)(2,1)S(1)}, u32[]{:S(2)}, u32[]{:S(2)}) collective-permute-start(bf16[32,2176]{1,0:T(8,128)(2,1)S(1)} %bitcast.23), channel_id=1, source_target_pairs={{0,2},{1,3},{2,0},{3,1},{4,6},{5,7},{6,4},{7,5},{8,10},{9,11},{10,... | collective-permute-start | bytes 417800 | tf_op jit(solution)/shard_map/ppermute | solution.py:245
  52.8 7.3 %collective-permute-start.19 = (bf16[512,128]{1,0:T(8,128)(2,1)S(1)}, bf16[512,128]{1,0:T(8,128)(2,1)S(1)}, u32[]{:S(2)}, u32[]{:S(2)}) collective-permute-start(bf16[512,128]{1,0:T(8,128)(2,1)S(1)} %fusion.2), channel_id=1, source_target_pairs={{0,16},{8,24},{16,0},{24,8},{1,17},{9,25},{17,1},{25,9},{2,18},{10... | collective-permute-start | bytes 393224 | tf_op jit(solution)/shard_map/ppermute | solution.py:245
  54.2 6.7 %collective-permute-start.11 = (bf16[32,2176]{1,0:T(8,128)(2,1)S(1)}, bf16[32,2176]{1,0:T(8,128)(2,1)S(1)}, u32[]{:S(2)}, u32[]{:S(2)}) collective-permute-start(bf16[32,2176]{1,0:T(8,128)(2,1)S(1)} %bitcast.24), channel_id=1, source_target_pairs={{0,1},{1,0},{2,3},{3,2},{4,5},{5,4},{6,7},{7,6},{8,9},{9,8},{10,11... | collective-permute-start | bytes 417800 | tf_op jit(solution)/shard_map/ppermute | solution.py:245
  55.3 5.5 %collective-permute-start.17 = (bf16[32,2176]{1,0:T(8,128)(2,1)S(1)}, bf16[32,2176]{1,0:T(8,128)(2,1)S(1)}, u32[]{:S(2)}, u32[]{:S(2)}) collective-permute-start(bf16[32,2176]{1,0:T(8,128)(2,1)S(1)} %collective-permute-done.16.refs_6_), channel_id=1, source_target_pairs={{0,1},{1,0},{2,3},{3,2},{4,5},{5,4},{6,7},{7,6},{8,9},{9,8},{10,11... | collective-permute-start | bytes 417800 | tf_op jit(solution)/shard_map/ppermute | solution.py:245
  56.7 4.1 %collective-permute-start.15 = (bf16[32,2176]{1,0:T(8,128)(2,1)S(1)}, bf16[32,2176]{1,0:T(8,128)(2,1)S(1)}, u32[]{:S(2)}, u32[]{:S(2)}) collective-permute-start(bf16[32,2176]{1,0:T(8,128)(2,1)S(1)} %collective-permute-done.14.refs_4_), channel_id=1, source_target_pairs={{0,1},{1,0},{2,3},{3,2},{4,5},{5,4},{6,7},{7,6},{8,9},{9,8},{10,11... | collective-permute-start | bytes 417800 | tf_op jit(solution)/shard_map/ppermute | solution.py:245
  57.2 3.6 %collective-permute-start.13 = (bf16[32,2176]{1,0:T(8,128)(2,1)S(1)}, bf16[32,2176]{1,0:T(8,128)(2,1)S(1)}, u32[]{:S(2)}, u32[]{:S(2)}) collective-permute-start(bf16[32,2176]{1,0:T(8,128)(2,1)S(1)} %collective-permute-done.12.refs_2_), channel_id=1, source_target_pairs={{0,1},{1,0},{2,3},{3,2},{4,5},{5,4},{6,7},{7,6},{8,9},{9,8},{10,11... | collective-permute-start | bytes 417800 | tf_op jit(solution)/shard_map/ppermute | solution.py:245

commit v6 on v5

--- a/solution.py
+++ b/solution.py
@@ -29,13 +29,13 @@
 
 
 def attention_kernel(
-    parts, block_hbm, pos_hbm, q_hbm, k_hbm, lse_hbm, qi_hbm, hw_hbm, out_ref,
-    block_ref, pos_ref, q_ref, k_ref, lse_ref, hw_ref, acc_ref, sems, part_sems
+    parts, block_hbm, pos_hbm, q_hbm, k_hbm, lse_hbm, qi_hbm, hw_hbm, out_hbm,
+    att_ref, side_ref, block_ref, pos_ref, q_ref, k_ref, lse_ref, hw_ref, acc_ref, sems, part_sems
 ):
     rows, keys = q_ref.shape[0], k_ref.shape[0]
     mla_heads, heads = lse_ref.shape[0], hw_ref.shape[0]
     width = q_ref.shape[1] // mla_heads
-    cols = out_ref.shape[1] - keys - LANES
+    cols = out_hbm.shape[1] - keys - LANES
     log2e = math.log2(math.e)
     scale = width ** (-0.5) * log2e
     small = [
@@ -43,7 +43,7 @@
         for i, (source, target) in enumerate(((lse_hbm, lse_ref), (hw_hbm, hw_ref), (pos_hbm, pos_ref), (block_hbm, block_ref)))
     ]
     share_at = pl.ds(pl.multiple_of(lax.axis_index("seq") * cols, LANES), cols)
-    share_copy = pltpu.make_async_copy(qi_hbm.at[:, share_at], out_ref.at[:, keys : keys + cols], sems.at[4])
+    share_copy = pltpu.make_async_copy(qi_hbm.at[:, share_at], out_hbm.at[:, keys : keys + cols], sems.at[4])
     large = []
     first = 0
     for i, n in enumerate(parts):
@@ -91,7 +91,11 @@
     least = jnp.min(jnp.where(valid, acc_ref[...], largest), axis=0, keepdims=True)
     least = jnp.where(least < largest, least, 0.0)
     share = jnp.where(valid, acc_ref[...] - least, -1.0)
-    out_ref[:, :keys] = jnp.transpose(share).astype(BF16)
+    copies = [share_copy]
+    for i, at in enumerate((slice(0, rows // 2), slice(rows // 2, rows))):
+        att_ref[at, :] = jnp.transpose(share[:, at]).astype(BF16)
+        copies.append(pltpu.make_async_copy(att_ref.at[at, :], out_hbm.at[at, :keys], sems.at[5 + i]))
+        copies[-1].start()
     padded = jnp.concatenate([hw_ref[...], jnp.zeros((LANES - heads, rows), F32)], axis=0)
     sub = lax.broadcasted_iota(jnp.int32, (LANES, rows), 0)
     terms = jnp.transpose(jnp.where(sub == heads, least, padded))
@@ -99,8 +103,11 @@
     rest = terms - high
     mid = rest.astype(BF16).astype(F32)
     side = high + pltpu.roll(mid, heads + 1, 1) + pltpu.roll(rest - mid, 2 * (heads + 1), 1)
-    out_ref[:, keys + cols :] = side.astype(BF16)
-    share_copy.wait()
+    side_ref[...] = side.astype(BF16)
+    copies.append(pltpu.make_async_copy(side_ref, out_hbm.at[:, keys + cols :], sems.at[7]))
+    copies[-1].start()
+    for copy in copies:
+        copy.wait()
 
 
 def keys_kernel(n_seq, n_head, own, got_ref, *refs):
@@ -176,36 +183,40 @@
     kl_ref[...] = jnp.broadcast_to(row_sum(kls), kl_ref.shape)
 
 
-def products_kernel(n_seq, gated_ref, weighted_ref, *refs):
-    key_refs, near_ref, term_ref = refs[:n_seq], refs[n_seq], refs[n_seq + 1]
+def products_kernel(n_seq, n_head, gated_ref, weighted_ref, q_ref, kl_ref, *refs):
+    key_refs, near_ref, term_ref, extra_ref = refs[:n_seq], refs[n_seq], refs[n_seq + 1], refs[n_seq + 2]
+    own = kl_ref.shape[0]
+    width = q_ref.shape[1]
+    heads = q_ref.shape[0] // own // n_head
     term = None
     for k in range(n_seq):
-        if k % 2 == 0:
-            side = jnp.dot(weighted_ref[...], gated_ref[k], preferred_element_type=F32)
-            near_ref[k // 2] = jnp.transpose(side)
         part = jnp.dot(gated_ref[k], key_refs[k][...], preferred_element_type=F32)
         term = part if term is None else term + part
     term_ref[...] = term
-
-
-def queries_kernel(n_head, own, term_ref, q_ref, wide_ref, kl_ref, out_ref):
-    width = q_ref.shape[1]
+    for k in range(0, n_seq, 2):
+        side = jnp.dot(weighted_ref[...], gated_ref[k], preferred_element_type=F32)
+        near_ref[k // 2] = jnp.transpose(side)
+    per_head = jnp.sum((term * q_ref[...].astype(F32)).reshape(n_head * heads, own, width), axis=2, keepdims=True)
+    lane = lax.broadcasted_iota(jnp.int32, (own, LANES), 1)
+    for h in range(n_head):
+        extra = jnp.where(lane == heads, kl_ref[...], 0.0)
+        for i in range(heads):
+            extra = jnp.where(lane == i, per_head[h * heads + i], extra)
+        extra_ref[h] = extra
+
+
+def queries_kernel(n_head, own, term_ref, wide_ref, extra_ref, out_ref):
+    width = term_ref.shape[1]
     heads_all = wide_ref.shape[0]
     heads = heads_all // n_head
-    term = term_ref[...]
-    per_head = jnp.sum((term * q_ref[...].astype(F32)).reshape(heads_all, own, width), axis=2, keepdims=True)
-    scaled = term.reshape(heads_all, own, width) * wide_ref[...]
-    lane = lax.broadcasted_iota(jnp.int32, (own, LANES), 1)
+    scaled = term_ref[...].reshape(heads_all, own, width) * wide_ref[...]
     for pair in range(0, n_head, 2):
         rows = slice(pair * own, (pair + 2) * own)
         one, two = pair * heads, (pair + 1) * heads
-        first = second = jnp.where(lane == heads, kl_ref[...], 0.0)
         for i in range(heads):
             both = jnp.concatenate([scaled[one + i], scaled[two + i]], axis=0)
             out_ref[rows, i * width : (i + 1) * width] = both.astype(BF16)
-            first = jnp.where(lane == i, per_head[one + i], first)
-            second = jnp.where(lane == i, per_head[two + i], second)
-        out_ref[rows, heads * width :] = jnp.concatenate([first, second], axis=0).astype(BF16)
+        out_ref[rows, heads * width :] = extra_ref[pair : pair + 2].reshape(2 * own, LANES).astype(BF16)
 
 
 def place_kernel(n_seq, *refs):
@@ -253,9 +264,11 @@
     sent = pl.pallas_call(
         functools.partial(attention_kernel, parts),
         in_specs=[hbm] * 7,
-        out_specs=vmem_spec(),
+        out_specs=hbm,
         out_shape=jax.ShapeDtypeStruct((rows, keys + cols + LANES), BF16),
         scratch_shapes=[
+            pltpu.VMEM((rows, keys), BF16),
+            pltpu.VMEM((rows, LANES), BF16),
             pltpu.SMEM((1,), jnp.int32),
             pltpu.VMEM((1, rows), jnp.int32),
             pltpu.VMEM(query_mla.shape, BF16),
@@ -263,7 +276,7 @@
             pltpu.VMEM((mla_heads, rows), F32),
             pltpu.VMEM((heads, rows), F32),
             pltpu.VMEM((keys, rows), F32),
-            pltpu.SemaphoreType.DMA((5,)),
+            pltpu.SemaphoreType.DMA((8,)),
             pltpu.SemaphoreType.DMA((2, len(parts))),
         ],
         compiler_params=limit(56),
@@ -308,18 +321,19 @@
     )(got, *all_keys)
 
     far = swap(far, "seq", n_seq, 1)
-    near, term = pl.pallas_call(
-        functools.partial(products_kernel, n_seq),
-        in_specs=[vmem_spec()] * (2 + n_seq),
-        out_specs=[vmem_spec()] * 2,
+    near, term, extra = pl.pallas_call(
+        functools.partial(products_kernel, n_seq, n_head),
+        in_specs=[vmem_spec()] * (4 + n_seq),
+        out_specs=[vmem_spec()] * 3,
         out_shape=[
             jax.ShapeDtypeStruct((half, keys, width), F32),
             jax.ShapeDtypeStruct((heads_all * own, width), F32),
+            jax.ShapeDtypeStruct((n_head, own, LANES), F32),
         ],
         compiler_params=limit(16),
         cost_estimate=product,
         name="products",
-    )(gated, weighted, *all_keys)
+    )(gated, weighted, queries, kl_rows, *all_keys)
     paired = [near[e] + far[e].astype(F32) for e in range(half)]
     sides = [x.astype(BF16) for x in paired[1:]]
     term, *sides = lax.optimization_barrier((term, *sides))
@@ -329,13 +343,13 @@
 
     rows_out = pl.pallas_call(
         functools.partial(queries_kernel, n_head, own),
-        in_specs=[vmem_spec()] * 4,
+        in_specs=[vmem_spec()] * 3,
         out_specs=vmem_spec(),
         out_shape=jax.ShapeDtypeStruct((group, wide_cols), BF16),
         compiler_params=limit(16),
         cost_estimate=pl.CostEstimate(flops=0, bytes_accessed=2**21, transcendentals=0),
         name="query_grad",
-    )(term, queries, wide, kl_rows)
+    )(term, wide, extra)
     own_rows = lax.all_to_all(rows_out, "head", 0, 0, tiled=True)
     own_rows, _ = lax.optimization_barrier((own_rows, mine))
     steps = bits(n_head)

time: 62.2 us -> 62 us (level)
  no operation moved by 1% of the time
where the time goes in v6:
time: 62 us; the launch traced here: 61.7 us
  starting transfers between devices  25.3 us (41%)
  waiting for transfers between devices  21.4 us (35%)
  Pallas kernels  12.7 us (20%)
  between operations  1.4 us (2%)
  other arithmetic  0.91 us (1%)
    ppermute x20, starting transfers between devices, swap(): return lax.ppermute(x, axis, [(i, i ^ mask) for i in range(n)])  18 us
    ppermute x20, waiting for transfers between devices, swap(): return lax.ppermute(x, axis, [(i, i ^ mask) for i in range(n)])  16.7 us
    pallas_call x1, Pallas kernels, fast_local(): pl.pallas_call(functools.partial(attention_kernel, parts), in_specs=[hbm]...  6.56 us
    all_to_all x1, starting transfers between devices, fast_local(): got = lax.all_to_all(sent, ('seq', 'head'), 0, 0, tiled=True)  3.97 us
    all_to_all x1, waiting for transfers between devices, fast_local(): own_rows = lax.all_to_all(rows_out, 'head', 0, 0, tiled=True)  3.57 us
    all_to_all x1, starting transfers between devices, fast_local(): own_rows = lax.all_to_all(rows_out, 'head', 0, 0, tiled=True)  3.33 us
    pallas_call x1, Pallas kernels, fast_local(): pl.pallas_call(functools.partial(keys_kernel, n_seq, n_head, own), in_spe...  2.66 us
    pallas_call x1, Pallas kernels, fast_local(): pl.pallas_call(functools.partial(products_kernel, n_seq, n_head), in_spec...  1.71 us
  transfers between devices with their start and end apart: 22, of which 11 were waited for; matrix products, arithmetic and copies ran while one was open for 1% of the time, Pallas kernels for 15%

profile of v6, /device:TPU:0, one launch (start us, length us, event | category | flops | bytes accessed | tf_op | source)
XLA Modules:
  0.0 61.7 jit_solution(7690460083694159201)
XLA Ops:
  0.6 3.0 %collective-permute-start.1 = (bf16[512,128]{1,0:T(8,128)(2,1)}, bf16[512,128]{1,0:T(8,128)(2,1)S(1)}, u32[]{:S(2)}, u32[]{:S(2)}) collective-permute-start(bf16[512,128]{1,0:T(8,128)(2,1)} %refs_0_.1), channel_id=1, source_target_pairs={{0,4},{1,5},{2,6},{3,7},{4,0},{5,1},{6,2},{7,3},{8,12},{9,13},{10,... | collective-permute-start | bytes 393224 | tf_op jit(solution)/shard_map/ppermute | solution.py:256
  3.7 1.5 %collective-permute-start = (bf16[512,128]{1,0:T(8,128)(2,1)}, bf16[512,128]{1,0:T(8,128)(2,1)S(1)}, u32[]{:S(2)}, u32[]{:S(2)}) collective-permute-start(bf16[512,128]{1,0:T(8,128)(2,1)} %refs_0_.1), channel_id=1, source_target_pairs={{0,2},{1,3},{2,0},{3,1},{4,6},{5,7},{6,4},{7,5},{8,10},{9,11},{10,... | collective-permute-start | bytes 393224 | tf_op jit(solution)/shard_map/ppermute | solution.py:256
  5.8 6.6 %attention.1 = bf16[256,896]{1,0:T(8,128)(2,1)} custom-call(s32[1]{0:T(128)S(6)} %copy.12.block_hbm, s32[1,256]{1,0:T(1,128)} %bitcast.31, bf16[256,6144]{1,0:T(8,128)(2,1)} %q_hbm.1, bf16[512,6144]{1,0:T(8,128)(2,1)} %k_hbm.1, f32[32,256]{1,0:T(8,128)} %bitcast.28, bf16[256,2048]{1,0:T(8,128)(2,1)} %qi_hbm.1, f32[16,256]{1,0:T(8,128)} %bitcast.29), custom_call_target="tpu_custom_call" | custom-call | flops 3221225472 | bytes 9437184 | tf_op jit(solution)/shard_map/attention/pallas_call | solution.py:264
  12.4 0.0 collective-permute-done.1.refs_4_
  12.4 0.0 collective-permute-done.refs_2_
  12.4 4.0 %all-to-all-start = ((bf16[32,8,896]{2,1,0:T(8,128)(2,1)}), bf16[32,8,896]{2,1,0:T(8,128)(2,1)S(1)}, u32[]{:S(2)}, u32[]{:S(2)}) async-start(bf16[32,8,896]{2,1,0:T(8,128)(2,1)} %bitcast.27), calls=%async_computation | async-start | bytes 917504 | tf_op jit(solution)/shard_map/all_to_all | solution.py:294
  16.4 2.7 %collective-permute-start.5 = (bf16[512,128]{1,0:T(8,128)(2,1)S(1)}, bf16[512,128]{1,0:T(8,128)(2,1)S(1)}, u32[]{:S(2)}, u32[]{:S(2)}) collective-permute-start(bf16[512,128]{1,0:T(8,128)(2,1)S(1)} %copy-done), channel_id=1, source_target_pairs={{0,6},{1,7},{2,4},{3,5},{4,2},{5,3},{6,0},{7,1},{8,14},{9,15},{10,... | collective-permute-start | bytes 393224 | tf_op jit(solution)/shard_map/ppermute | solution.py:256
  19.1 0.0 collective-permute-start.2
  19.1 7.3 %collective-permute-done.5.refs_6_ = bf16[512,128]{1,0:T(8,128)(2,1)S(1)} collective-permute-done((bf16[512,128]{1,0:T(8,128)(2,1)S(1)}, bf16[512,128]{1,0:T(8,128)(2,1)S(1)}, u32[]{:S(2)}, u32[]{:S(2)}) %collective-permute-start.5) | collective-permute-done | bytes 131104 | tf_op jit(solution)/shard_map/ppermute | solution.py:256
  26.5 0.0 collective-permute-start.6
  26.5 0.5 collective-permute-start.3
  27.0 0.0 collective-permute-start.4
  27.0 0.8 %collective-permute-done.6.refs_7_ = bf16[512,128]{1,0:T(8,128)(2,1)S(1)} collective-permute-done((bf16[512,128]{1,0:T(8,128)(2,1)S(1)}, bf16[512,128]{1,0:T(8,128)(2,1)S(1)}, u32[]{:S(2)}, u32[]{:S(2)}) %collective-permute-start.6) | collective-permute-done | bytes 131104 | tf_op jit(solution)/shard_map/ppermute | solution.py:256
  27.8 0.2 collective-permute-done.3.refs_3_
  28.0 0.3 collective-permute-done.4.refs_5_
  28.3 1.2 %all-to-all-done = bf16[32,8,896]{2,1,0:T(8,128)(2,1)S(1)} async-done(((bf16[32,8,896]{2,1,0:T(8,128)(2,1)}), bf16[32,8,896]{2,1,0:T(8,128)(2,1)S(1)}, u32[]{:S(2)}, u32[]{:S(2)}) %all-to-all-start) | async-done | bytes 458784 | tf_op jit(solution)/shard_map/all_to_all | solution.py:294
  29.5 2.7 %key_grad.1 = (bf16[4,512,128]{2,1,0:T(8,128)(2,1)S(1)}, bf16[8,512,512]{2,1,0:T(8,128)(2,1)S(1)}, bf16[512,128]{1,0:T(8,128)(2,1)S(1)}, f32[64,8,128]{2,1,0:T(8...) custom-call(bf16[256,896]{1,0:T(8,128)(2,1)S(1)} %bitcast.26, bf16[512,128]{1,0:T(8,128)(2,1)S(1)} %copy-done, ...), custom_call_target="tpu_custom_call" | custom-call | flops 1073741824 | bytes 2097152 | tf_op jit(solution)/shard_map/key_grad/pallas_call | solution.py:302
  32.2 1.1 %collective-permute-start.7 = (bf16[4,512,128]{2,1,0:T(8,128)(2,1)S(1)}, bf16[4,512,128]{2,1,0:T(8,128)(2,1)S(1)}, u32[]{:S(2)}, u32[]{:S(2)}) collective-permute-start(bf16[4,512,128]{2,1,0:T(8,128)(2,1)S(1)} %get-tuple-element.35), channel_id=1, source_target_pairs={{0,1},{1,0},{2,3},{3,2},{4,5},{5,4},{6,7},{7,6},{8,9},{9,8},{10,11... | collective-permute-start | bytes 1572872 | tf_op jit(solution)/shard_map/ppermute | solution.py:256
  33.3 1.7 %products.1 = (f32[4,512,128]{2,1,0:T(8,128)S(1)}, f32[512,128]{1,0:T(8,128)S(1)}, f32[4,8,128]{2,1,0:T(8,128)S(1)}) custom-call(bf16[8,512,512]{2,1,0:T(8,128)(2,1)S(1)} %get-tuple-element.29.gated_ref, bf16[128,512]{1,0:T(8,128)(2,1)S(1)} %get-tuple-element.30.weighted_ref, bf16[512,128]{1,0:T(8,128)(2,1)S(1)} %get-tuple-element.31.q_ref, ...), custom_call_target="tpu_custom_call" | custom-call | flops 1073741824 | bytes 2097152 | tf_op jit(solution)/shard_map/products/pallas_call | solution.py:324
  35.0 0.0 collective-permute-done.7
  35.0 0.1 fusion.5
  35.1 1.5 %collective-permute-start.8 = (bf16[512,128]{1,0:T(8,128)(2,1)S(1)}, bf16[512,128]{1,0:T(8,128)(2,1)S(1)}, u32[]{:S(2)}, u32[]{:S(2)}) collective-permute-start(bf16[512,128]{1,0:T(8,128)(2,1)S(1)} %get-tuple-element.39), channel_id=1, source_target_pairs={{0,2},{1,3},{2,0},{3,1},{4,6},{5,7},{6,4},{7,5},{8,10},{9,11},{10,... | collective-permute-start | bytes 393224 | tf_op jit(solution)/shard_map/ppermute | solution.py:256
  36.6 0.6 collective-permute-start.9
  37.2 1.5 %collective-permute-start.10 = (bf16[512,128]{1,0:T(8,128)(2,1)S(1)}, bf16[512,128]{1,0:T(8,128)(2,1)S(1)}, u32[]{:S(2)}, u32[]{:S(2)}) collective-permute-start(bf16[512,128]{1,0:T(8,128)(2,1)S(1)} %get-tuple-element.41), channel_id=1, source_target_pairs={{0,6},{1,7},{2,4},{3,5},{4,2},{5,3},{6,0},{7,1},{8,14},{9,15},{10,... | collective-permute-start | bytes 393224 | tf_op jit(solution)/shard_map/ppermute | solution.py:256
  38.7 0.7 %query_grad.1 = bf16[32,2176]{1,0:T(8,128)(2,1)} custom-call(f32[512,128]{1,0:T(8,128)S(1)} %get-tuple-element.36.term_ref, f32[64,8,128]{2,1,0:T(8,128)S(1)} %get-tuple-element.37.wide_ref, f32[4,8,128]{2,1,0:T(8,128)S(1)} %get-tuple-element.38.extra_ref), custom_call_target="tpu_custom_call" | custom-call | bytes 2097152 | tf_op jit(solution)/shard_map/query_grad/pallas_call | solution.py:344
  39.4 3.3 %all-to-all-start.1 = ((bf16[4,8,2176]{2,1,0:T(8,128)(2,1)}), bf16[4,8,2176]{2,1,0:T(8,128)(2,1)S(1)}, u32[]{:S(2)}, u32[]{:S(2)}) async-start(bf16[4,8,2176]{2,1,0:T(8,128)(2,1)} %bitcast.8), calls=%async_computation.1 | async-start | bytes 278528 | tf_op jit(solution)/shard_map/all_to_all | solution.py:353
  42.7 0.0 collective-permute-done.8
  42.7 2.0 %collective-permute-done.9 = bf16[512,128]{1,0:T(8,128)(2,1)S(1)} collective-permute-done((bf16[512,128]{1,0:T(8,128)(2,1)S(1)}, bf16[512,128]{1,0:T(8,128)(2,1)S(1)}, u32[]{:S(2)}, u32[]{:S(2)}) %collective-permute-start.9) | collective-permute-done | bytes 131104 | tf_op jit(solution)/shard_map/ppermute | solution.py:256
  44.8 0.1 fusion.6
  44.8 0.6 %collective-permute-start.18 = (bf16[512,128]{1,0:T(8,128)(2,1)S(1)}, bf16[512,128]{1,0:T(8,128)(2,1)S(1)}, u32[]{:S(2)}, u32[]{:S(2)}) collective-permute-start(bf16[512,128]{1,0:T(8,128)(2,1)S(1)} %get-tuple-element.46), channel_id=1, source_target_pairs={{0,8},{8,0},{16,24},{24,16},{1,9},{9,1},{17,25},{25,17},{2,10},{10... | collective-permute-start | bytes 393224 | tf_op jit(solution)/shard_map/ppermute | solution.py:256
  45.5 3.6 %all-to-all-done.1 = bf16[4,8,2176]{2,1,0:T(8,128)(2,1)S(1)} async-done(((bf16[4,8,2176]{2,1,0:T(8,128)(2,1)}), bf16[4,8,2176]{2,1,0:T(8,128)(2,1)S(1)}, u32[]{:S(2)}, u32[]{:S(2)}) %all-to-all-start.1) | async-done | bytes 139296 | tf_op jit(solution)/shard_map/all_to_all | solution.py:353
  49.0 1.4 %collective-permute-start.16 = (bf16[32,2176]{1,0:T(8,128)(2,1)S(1)}, bf16[32,2176]{1,0:T(8,128)(2,1)S(1)}, u32[]{:S(2)}, u32[]{:S(2)}) collective-permute-start(bf16[32,2176]{1,0:T(8,128)(2,1)S(1)} %bitcast.21), channel_id=1, source_target_pairs={{0,6},{1,7},{2,4},{3,5},{4,2},{5,3},{6,0},{7,1},{8,14},{9,15},{10,... | collective-permute-start | bytes 417800 | tf_op jit(solution)/shard_map/ppermute | solution.py:256
  50.5 1.5 %collective-permute-start.14 = (bf16[32,2176]{1,0:T(8,128)(2,1)S(1)}, bf16[32,2176]{1,0:T(8,128)(2,1)S(1)}, u32[]{:S(2)}, u32[]{:S(2)}) collective-permute-start(bf16[32,2176]{1,0:T(8,128)(2,1)S(1)} %bitcast.22), channel_id=1, source_target_pairs={{0,4},{1,5},{2,6},{3,7},{4,0},{5,1},{6,2},{7,3},{8,12},{9,13},{10,... | collective-permute-start | bytes 417800 | tf_op jit(solution)/shard_map/ppermute | solution.py:256
  52.0 0.6 collective-permute-start.12
  52.5 0.0 collective-permute-done.18
  52.6 1.4 %collective-permute-start.19 = (bf16[512,128]{1,0:T(8,128)(2,1)S(1)}, bf16[512,128]{1,0:T(8,128)(2,1)S(1)}, u32[]{:S(2)}, u32[]{:S(2)}) collective-permute-start(bf16[512,128]{1,0:T(8,128)(2,1)S(1)} %fusion.2), channel_id=1, source_target_pairs={{0,16},{8,24},{16,0},{24,8},{1,17},{9,25},{17,1},{25,9},{2,18},{10... | collective-permute-start | bytes 393224 | tf_op jit(solution)/shard_map/ppermute | solution.py:256
  53.9 0.0 collective-permute-start.11
  53.9 1.1 %collective-permute-done.16.refs_6_ = bf16[32,2176]{1,0:T(8,128)(2,1)S(1)} collective-permute-done((bf16[32,2176]{1,0:T(8,128)(2,1)S(1)}, bf16[32,2176]{1,0:T(8,128)(2,1)S(1)}, u32[]{:S(2)}, u32[]{:S(2)}) %collective-permute-start.16) | collective-permute-done | bytes 139296 | tf_op jit(solution)/shard_map/ppermute | solution.py:256
  55.1 0.0 collective-permute-start.17
  55.1 1.4 %collective-permute-done.14.refs_4_ = bf16[32,2176]{1,0:T(8,128)(2,1)S(1)} collective-permute-done((bf16[32,2176]{1,0:T(8,128)(2,1)S(1)}, bf16[32,2176]{1,0:T(8,128)(2,1)S(1)}, u32[]{:S(2)}, u32[]{:S(2)}) %collective-permute-start.14) | collective-permute-done | bytes 139296 | tf_op jit(solution)/shard_map/ppermute | solution.py:256
  56.5 0.0 collective-permute-start.15
  56.5 0.5 collective-permute-done.12.refs_2_
  57.0 0.0 collective-permute-start.13
  57.0 2.9 %collective-permute-done.19 = bf16[512,128]{1,0:T(8,128)(2,1)S(1)} collective-permute-done((bf16[512,128]{1,0:T(8,128)(2,1)S(1)}, bf16[512,128]{1,0:T(8,128)(2,1)S(1)}, u32[]{:S(2)}, u32[]{:S(2)}) %collective-permute-start.19) | collective-permute-done | bytes 131104 | tf_op jit(solution)/shard_map/ppermute | solution.py:256
  59.9 0.7 %add_convert_fusion = bf16[512,128]{1,0:T(8,128)(2,1)} fusion(bf16[512,128]{1,0:T(8,128)(2,1)S(1)} %collective-permute-done.19, f32[512,128]{1,0:T(8,128)S(1)} %get-tuple-element.47, bf16[512,128]{1,0:T(8,128)(2,1)S(1)} %collective-permute-done.18), kind=kLoop, calls=%fused_computation.3 | loop fusion | flops 327680 | bytes 655360 | tf_op jit(solution)/shard_map/convert_element_type | solution.py:384
  60.6 0.0 collective-permute-done.11.refs_1_
  60.6 0.0 collective-permute-done.17.refs_7_
  60.6 1.1 %place.1 = (bf16[256,2048]{1,0:T(8,128)(2,1)}, bf16[16,256]{1,0:T(8,128)(2,1)}, bf16[256]{0:T(256)(128)(2,1)}) custom-call(bf16[32,2176]{1,0:T(8,128)(2,1)S(1)} %bitcast.25, bf16[32,2176]{1,0:T(8,128)(2,1)S(1)} %collective-permute-done.11.refs_1_, bf16[32,2176]{1,0:T(8,128)(2,1)S(1)} %collective-permute-done.12.refs_2_, ...), custom_call_target="tpu_custom_call" | custom-call | bytes 4456448 | tf_op jit(solution)/shard_map/place/pallas_call | solution.py:365
  (7 shorter events, 0.0 us)
Async XLA Ops:
  0.6 11.8 %collective-permute-start.1 = (bf16[512,128]{1,0:T(8,128)(2,1)}, bf16[512,128]{1,0:T(8,128)(2,1)S(1)}, u32[]{:S(2)}, u32[]{:S(2)}) collective-permute-start(bf16[512,128]{1,0:T(8,128)(2,1)} %refs_0_.1), channel_id=1, source_target_pairs={{0,4},{1,5},{2,6},{3,7},{4,0},{5,1},{6,2},{7,3},{8,12},{9,13},{10,... | collective-permute-start | bytes 393224 | tf_op jit(solution)/shard_map/ppermute | solution.py:256
  3.7 8.7 %collective-permute-start = (bf16[512,128]{1,0:T(8,128)(2,1)}, bf16[512,128]{1,0:T(8,128)(2,1)S(1)}, u32[]{:S(2)}, u32[]{:S(2)}) collective-permute-start(bf16[512,128]{1,0:T(8,128)(2,1)} %refs_0_.1), channel_id=1, source_target_pairs={{0,2},{1,3},{2,0},{3,1},{4,6},{5,7},{6,4},{7,5},{8,10},{9,11},{10,... | collective-permute-start | bytes 393224 | tf_op jit(solution)/shard_map/ppermute | solution.py:256
  5.8 10.6 %copy-start = (bf16[512,128]{1,0:T(8,128)(2,1)S(1)}, bf16[512,128]{1,0:T(8,128)(2,1)}, u32[]{:S(2)}) copy-start(bf16[512,128]{1,0:T(8,128)(2,1)} %refs_0_.1) | copy-start | bytes 393220
  12.4 17.1 %all-to-all-start = ((bf16[32,8,896]{2,1,0:T(8,128)(2,1)}), bf16[32,8,896]{2,1,0:T(8,128)(2,1)S(1)}, u32[]{:S(2)}, u32[]{:S(2)}) async-start(bf16[32,8,896]{2,1,0:T(8,128)(2,1)} %bitcast.27), calls=%async_computation | async-start | bytes 917504 | tf_op jit(solution)/shard_map/all_to_all | solution.py:294
  16.4 10.1 %collective-permute-start.5 = (bf16[512,128]{1,0:T(8,128)(2,1)S(1)}, bf16[512,128]{1,0:T(8,128)(2,1)S(1)}, u32[]{:S(2)}, u32[]{:S(2)}) collective-permute-start(bf16[512,128]{1,0:T(8,128)(2,1)S(1)} %copy-done), channel_id=1, source_target_pairs={{0,6},{1,7},{2,4},{3,5},{4,2},{5,3},{6,0},{7,1},{8,14},{9,15},{10,... | collective-permute-start | bytes 393224 | tf_op jit(solution)/shard_map/ppermute | solution.py:256
  19.1 8.7 %collective-permute-start.2 = (bf16[512,128]{1,0:T(8,128)(2,1)S(1)}, bf16[512,128]{1,0:T(8,128)(2,1)S(1)}, u32[]{:S(2)}, u32[]{:S(2)}) collective-permute-start(bf16[512,128]{1,0:T(8,128)(2,1)S(1)} %copy-done), channel_id=1, source_target_pairs={{0,1},{1,0},{2,3},{3,2},{4,5},{5,4},{6,7},{7,6},{8,9},{9,8},{10,11... | collective-permute-start | bytes 393224 | tf_op jit(solution)/shard_map/ppermute | solution.py:256
  26.5 1.3 %collective-permute-start.6 = (bf16[512,128]{1,0:T(8,128)(2,1)S(1)}, bf16[512,128]{1,0:T(8,128)(2,1)S(1)}, u32[]{:S(2)}, u32[]{:S(2)}) collective-permute-start(bf16[512,128]{1,0:T(8,128)(2,1)S(1)} %collective-permute-done.5.refs_6_), channel_id=1, source_target_pairs={{0,1},{1,0},{2,3},{3,2},{4,5},{5,4},{6,7},{7,6},{8,9},{9,8},{10,11... | collective-permute-start | bytes 393224 | tf_op jit(solution)/shard_map/ppermute | solution.py:256
  26.5 1.5 %collective-permute-start.3 = (bf16[512,128]{1,0:T(8,128)(2,1)S(1)}, bf16[512,128]{1,0:T(8,128)(2,1)S(1)}, u32[]{:S(2)}, u32[]{:S(2)}) collective-permute-start(bf16[512,128]{1,0:T(8,128)(2,1)S(1)} %collective-permute-done.refs_2_), channel_id=1, source_target_pairs={{0,1},{1,0},{2,3},{3,2},{4,5},{5,4},{6,7},{7,6},{8,9},{9,8},{10,11... | collective-permute-start | bytes 393224 | tf_op jit(solution)/shard_map/ppermute | solution.py:256
  27.0 1.3 %collective-permute-start.4 = (bf16[512,128]{1,0:T(8,128)(2,1)S(1)}, bf16[512,128]{1,0:T(8,128)(2,1)S(1)}, u32[]{:S(2)}, u32[]{:S(2)}) collective-permute-start(bf16[512,128]{1,0:T(8,128)(2,1)S(1)} %collective-permute-done.1.refs_4_), channel_id=1, source_target_pairs={{0,1},{1,0},{2,3},{3,2},{4,5},{5,4},{6,7},{7,6},{8,9},{9,8},{10,11... | collective-permute-start | bytes 393224 | tf_op jit(solution)/shard_map/ppermute | solution.py:256
  32.2 2.9 %collective-permute-start.7 = (bf16[4,512,128]{2,1,0:T(8,128)(2,1)S(1)}, bf16[4,512,128]{2,1,0:T(8,128)(2,1)S(1)}, u32[]{:S(2)}, u32[]{:S(2)}) collective-permute-start(bf16[4,512,128]{2,1,0:T(8,128)(2,1)S(1)} %get-tuple-element.35), channel_id=1, source_target_pairs={{0,1},{1,0},{2,3},{3,2},{4,5},{5,4},{6,7},{7,6},{8,9},{9,8},{10,11... | collective-permute-start | bytes 1572872 | tf_op jit(solution)/shard_map/ppermute | solution.py:256
  35.1 7.6 %collective-permute-start.8 = (bf16[512,128]{1,0:T(8,128)(2,1)S(1)}, bf16[512,128]{1,0:T(8,128)(2,1)S(1)}, u32[]{:S(2)}, u32[]{:S(2)}) collective-permute-start(bf16[512,128]{1,0:T(8,128)(2,1)S(1)} %get-tuple-element.39), channel_id=1, source_target_pairs={{0,2},{1,3},{2,0},{3,1},{4,6},{5,7},{6,4},{7,5},{8,10},{9,11},{10,... | collective-permute-start | bytes 393224 | tf_op jit(solution)/shard_map/ppermute | solution.py:256
  36.6 8.1 %collective-permute-start.9 = (bf16[512,128]{1,0:T(8,128)(2,1)S(1)}, bf16[512,128]{1,0:T(8,128)(2,1)S(1)}, u32[]{:S(2)}, u32[]{:S(2)}) collective-permute-start(bf16[512,128]{1,0:T(8,128)(2,1)S(1)} %get-tuple-element.40), channel_id=1, source_target_pairs={{0,4},{1,5},{2,6},{3,7},{4,0},{5,1},{6,2},{7,3},{8,12},{9,13},{10,... | collective-permute-start | bytes 393224 | tf_op jit(solution)/shard_map/ppermute | solution.py:256
  37.2 7.6 %collective-permute-start.10 = (bf16[512,128]{1,0:T(8,128)(2,1)S(1)}, bf16[512,128]{1,0:T(8,128)(2,1)S(1)}, u32[]{:S(2)}, u32[]{:S(2)}) collective-permute-start(bf16[512,128]{1,0:T(8,128)(2,1)S(1)} %get-tuple-element.41), channel_id=1, source_target_pairs={{0,6},{1,7},{2,4},{3,5},{4,2},{5,3},{6,0},{7,1},{8,14},{9,15},{10,... | collective-permute-start | bytes 393224 | tf_op jit(solution)/shard_map/ppermute | solution.py:256
  39.4 9.7 %all-to-all-start.1 = ((bf16[4,8,2176]{2,1,0:T(8,128)(2,1)}), bf16[4,8,2176]{2,1,0:T(8,128)(2,1)S(1)}, u32[]{:S(2)}, u32[]{:S(2)}) async-start(bf16[4,8,2176]{2,1,0:T(8,128)(2,1)} %bitcast.8), calls=%async_computation.1 | async-start | bytes 278528 | tf_op jit(solution)/shard_map/all_to_all | solution.py:353
  44.8 7.7 %collective-permute-start.18 = (bf16[512,128]{1,0:T(8,128)(2,1)S(1)}, bf16[512,128]{1,0:T(8,128)(2,1)S(1)}, u32[]{:S(2)}, u32[]{:S(2)}) collective-permute-start(bf16[512,128]{1,0:T(8,128)(2,1)S(1)} %get-tuple-element.46), channel_id=1, source_target_pairs={{0,8},{8,0},{16,24},{24,16},{1,9},{9,1},{17,25},{25,17},{2,10},{10... | collective-permute-start | bytes 393224 | tf_op jit(solution)/shard_map/ppermute | solution.py:256
  49.0 6.1 %collective-permute-start.16 = (bf16[32,2176]{1,0:T(8,128)(2,1)S(1)}, bf16[32,2176]{1,0:T(8,128)(2,1)S(1)}, u32[]{:S(2)}, u32[]{:S(2)}) collective-permute-start(bf16[32,2176]{1,0:T(8,128)(2,1)S(1)} %bitcast.21), channel_id=1, source_target_pairs={{0,6},{1,7},{2,4},{3,5},{4,2},{5,3},{6,0},{7,1},{8,14},{9,15},{10,... | collective-permute-start | bytes 417800 | tf_op jit(solution)/shard_map/ppermute | solution.py:256
  50.5 6.0 %collective-permute-start.14 = (bf16[32,2176]{1,0:T(8,128)(2,1)S(1)}, bf16[32,2176]{1,0:T(8,128)(2,1)S(1)}, u32[]{:S(2)}, u32[]{:S(2)}) collective-permute-start(bf16[32,2176]{1,0:T(8,128)(2,1)S(1)} %bitcast.22), channel_id=1, source_target_pairs={{0,4},{1,5},{2,6},{3,7},{4,0},{5,1},{6,2},{7,3},{8,12},{9,13},{10,... | collective-permute-start | bytes 417800 | tf_op jit(solution)/shard_map/ppermute | solution.py:256
  52.0 5.1 %collective-permute-start.12 = (bf16[32,2176]{1,0:T(8,128)(2,1)S(1)}, bf16[32,2176]{1,0:T(8,128)(2,1)S(1)}, u32[]{:S(2)}, u32[]{:S(2)}) collective-permute-start(bf16[32,2176]{1,0:T(8,128)(2,1)S(1)} %bitcast.23), channel_id=1, source_target_pairs={{0,2},{1,3},{2,0},{3,1},{4,6},{5,7},{6,4},{7,5},{8,10},{9,11},{10,... | collective-permute-start | bytes 417800 | tf_op jit(solution)/shard_map/ppermute | solution.py:256
  52.6 7.3 %collective-permute-start.19 = (bf16[512,128]{1,0:T(8,128)(2,1)S(1)}, bf16[512,128]{1,0:T(8,128)(2,1)S(1)}, u32[]{:S(2)}, u32[]{:S(2)}) collective-permute-start(bf16[512,128]{1,0:T(8,128)(2,1)S(1)} %fusion.2), channel_id=1, source_target_pairs={{0,16},{8,24},{16,0},{24,8},{1,17},{9,25},{17,1},{25,9},{2,18},{10... | collective-permute-start | bytes 393224 | tf_op jit(solution)/shard_map/ppermute | solution.py:256
  53.9 6.7 %collective-permute-start.11 = (bf16[32,2176]{1,0:T(8,128)(2,1)S(1)}, bf16[32,2176]{1,0:T(8,128)(2,1)S(1)}, u32[]{:S(2)}, u32[]{:S(2)}) collective-permute-start(bf16[32,2176]{1,0:T(8,128)(2,1)S(1)} %bitcast.24), channel_id=1, source_target_pairs={{0,1},{1,0},{2,3},{3,2},{4,5},{5,4},{6,7},{7,6},{8,9},{9,8},{10,11... | collective-permute-start | bytes 417800 | tf_op jit(solution)/shard_map/ppermute | solution.py:256
  55.1 5.5 %collective-permute-start.17 = (bf16[32,2176]{1,0:T(8,128)(2,1)S(1)}, bf16[32,2176]{1,0:T(8,128)(2,1)S(1)}, u32[]{:S(2)}, u32[]{:S(2)}) collective-permute-start(bf16[32,2176]{1,0:T(8,128)(2,1)S(1)} %collective-permute-done.16.refs_6_), channel_id=1, source_target_pairs={{0,1},{1,0},{2,3},{3,2},{4,5},{5,4},{6,7},{7,6},{8,9},{9,8},{10,11... | collective-permute-start | bytes 417800 | tf_op jit(solution)/shard_map/ppermute | solution.py:256
  56.5 4.1 %collective-permute-start.15 = (bf16[32,2176]{1,0:T(8,128)(2,1)S(1)}, bf16[32,2176]{1,0:T(8,128)(2,1)S(1)}, u32[]{:S(2)}, u32[]{:S(2)}) collective-permute-start(bf16[32,2176]{1,0:T(8,128)(2,1)S(1)} %collective-permute-done.14.refs_4_), channel_id=1, source_target_pairs={{0,1},{1,0},{2,3},{3,2},{4,5},{5,4},{6,7},{7,6},{8,9},{9,8},{10,11... | collective-permute-start | bytes 417800 | tf_op jit(solution)/shard_map/ppermute | solution.py:256
  57.0 3.6 %collective-permute-start.13 = (bf16[32,2176]{1,0:T(8,128)(2,1)S(1)}, bf16[32,2176]{1,0:T(8,128)(2,1)S(1)}, u32[]{:S(2)}, u32[]{:S(2)}) collective-permute-start(bf16[32,2176]{1,0:T(8,128)(2,1)S(1)} %collective-permute-done.12.refs_2_), channel_id=1, source_target_pairs={{0,1},{1,0},{2,3},{3,2},{4,5},{5,4},{6,7},{7,6},{8,9},{9,8},{10,11... | collective-permute-start | bytes 417800 | tf_op jit(solution)/shard_map/ppermute | solution.py:256

commit v7 on v6

--- a/solution.py
+++ b/solution.py
@@ -338,7 +338,7 @@
     sides = [x.astype(BF16) for x in paired[1:]]
     term, *sides = lax.optimization_barrier((term, *sides))
     mine = paired[0]
-    for e in range(1, half):
+    for e in reversed(range(1, half)):
         mine = mine + swap(sides[e - 1], "seq", n_seq, 2 * e).astype(F32)
 
     rows_out = pl.pallas_call(

time: 62 us -> 60.5 us (0.976)
  waiting for transfers between devices: 21.4 us -> 19.3 us
    ppermute x20, waiting for transfers between devices: 16.7 us -> 15.1 us  [swap(): return lax.ppermute(x, axis, [(i, i ^ mask) for i in range(n)])]
where the time goes in v7:
time: 60.5 us; the launch traced here: 60.2 us
  starting transfers between devices  25.8 us (43%)
  waiting for transfers between devices  19.3 us (32%)
  Pallas kernels  12.7 us (21%)
  between operations  1.4 us (2%)
  other arithmetic  0.91 us (2%)
    ppermute x20, starting transfers between devices, swap(): return lax.ppermute(x, axis, [(i, i ^ mask) for i in range(n)])  18.5 us
    ppermute x20, waiting for transfers between devices, swap(): return lax.ppermute(x, axis, [(i, i ^ mask) for i in range(n)])  15.1 us
    pallas_call x1, Pallas kernels, fast_local(): pl.pallas_call(functools.partial(attention_kernel, parts), in_specs=[hbm]...  6.56 us
    all_to_all x1, starting transfers between devices, fast_local(): got = lax.all_to_all(sent, ('seq', 'head'), 0, 0, tiled=True)  3.97 us
    all_to_all x1, starting transfers between devices, fast_local(): own_rows = lax.all_to_all(rows_out, 'head', 0, 0, tiled=True)  3.33 us
    all_to_all x1, waiting for transfers between devices, fast_local(): own_rows = lax.all_to_all(rows_out, 'head', 0, 0, tiled=True)  3.08 us
    pallas_call x1, Pallas kernels, fast_local(): pl.pallas_call(functools.partial(keys_kernel, n_seq, n_head, own), in_spe...  2.66 us
    pallas_call x1, Pallas kernels, fast_local(): pl.pallas_call(functools.partial(products_kernel, n_seq, n_head), in_spec...  1.71 us
  transfers between devices with their start and end apart: 22, of which 11 were waited for; matrix products, arithmetic and copies ran while one was open for 1% of the time, Pallas kernels for 15%

profile of v7, /device:TPU:0, one launch (start us, length us, event | category | flops | bytes accessed | tf_op | source)
XLA Modules:
  0.0 60.2 jit_solution(5418068774532781232)
XLA Ops:
  0.6 3.0 %collective-permute-start.1 = (bf16[512,128]{1,0:T(8,128)(2,1)}, bf16[512,128]{1,0:T(8,128)(2,1)S(1)}, u32[]{:S(2)}, u32[]{:S(2)}) collective-permute-start(bf16[512,128]{1,0:T(8,128)(2,1)} %refs_0_.1), channel_id=1, source_target_pairs={{0,4},{1,5},{2,6},{3,7},{4,0},{5,1},{6,2},{7,3},{8,12},{9,13},{10,... | collective-permute-start | bytes 393224 | tf_op jit(solution)/shard_map/ppermute | solution.py:256
  3.7 1.5 %collective-permute-start = (bf16[512,128]{1,0:T(8,128)(2,1)}, bf16[512,128]{1,0:T(8,128)(2,1)S(1)}, u32[]{:S(2)}, u32[]{:S(2)}) collective-permute-start(bf16[512,128]{1,0:T(8,128)(2,1)} %refs_0_.1), channel_id=1, source_target_pairs={{0,2},{1,3},{2,0},{3,1},{4,6},{5,7},{6,4},{7,5},{8,10},{9,11},{10,... | collective-permute-start | bytes 393224 | tf_op jit(solution)/shard_map/ppermute | solution.py:256
  5.8 6.6 %attention.1 = bf16[256,896]{1,0:T(8,128)(2,1)} custom-call(s32[1]{0:T(128)S(6)} %copy.12.block_hbm, s32[1,256]{1,0:T(1,128)} %bitcast.31, bf16[256,6144]{1,0:T(8,128)(2,1)} %q_hbm.1, bf16[512,6144]{1,0:T(8,128)(2,1)} %k_hbm.1, f32[32,256]{1,0:T(8,128)} %bitcast.28, bf16[256,2048]{1,0:T(8,128)(2,1)} %qi_hbm.1, f32[16,256]{1,0:T(8,128)} %bitcast.29), custom_call_target="tpu_custom_call" | custom-call | flops 3221225472 | bytes 9437184 | tf_op jit(solution)/shard_map/attention/pallas_call | solution.py:264
  12.4 0.0 collective-permute-done.1.refs_4_
  12.4 0.0 collective-permute-done.refs_2_
  12.4 4.0 %all-to-all-start = ((bf16[32,8,896]{2,1,0:T(8,128)(2,1)}), bf16[32,8,896]{2,1,0:T(8,128)(2,1)S(1)}, u32[]{:S(2)}, u32[]{:S(2)}) async-start(bf16[32,8,896]{2,1,0:T(8,128)(2,1)} %bitcast.27), calls=%async_computation | async-start | bytes 917504 | tf_op jit(solution)/shard_map/all_to_all | solution.py:294
  16.4 2.7 %collective-permute-start.5 = (bf16[512,128]{1,0:T(8,128)(2,1)S(1)}, bf16[512,128]{1,0:T(8,128)(2,1)S(1)}, u32[]{:S(2)}, u32[]{:S(2)}) collective-permute-start(bf16[512,128]{1,0:T(8,128)(2,1)S(1)} %copy-done), channel_id=1, source_target_pairs={{0,6},{1,7},{2,4},{3,5},{4,2},{5,3},{6,0},{7,1},{8,14},{9,15},{10,... | collective-permute-start | bytes 393224 | tf_op jit(solution)/shard_map/ppermute | solution.py:256
  19.1 0.0 collective-permute-start.2
  19.1 7.3 %collective-permute-done.5.refs_6_ = bf16[512,128]{1,0:T(8,128)(2,1)S(1)} collective-permute-done((bf16[512,128]{1,0:T(8,128)(2,1)S(1)}, bf16[512,128]{1,0:T(8,128)(2,1)S(1)}, u32[]{:S(2)}, u32[]{:S(2)}) %collective-permute-start.5) | collective-permute-done | bytes 131104 | tf_op jit(solution)/shard_map/ppermute | solution.py:256
  26.5 0.0 collective-permute-start.6
  26.5 0.5 collective-permute-start.3
  27.0 0.0 collective-permute-start.4
  27.0 0.8 %collective-permute-done.6.refs_7_ = bf16[512,128]{1,0:T(8,128)(2,1)S(1)} collective-permute-done((bf16[512,128]{1,0:T(8,128)(2,1)S(1)}, bf16[512,128]{1,0:T(8,128)(2,1)S(1)}, u32[]{:S(2)}, u32[]{:S(2)}) %collective-permute-start.6) | collective-permute-done | bytes 131104 | tf_op jit(solution)/shard_map/ppermute | solution.py:256
  27.8 0.0 collective-permute-done.2.refs_1_
  27.8 0.2 collective-permute-done.3.refs_3_
  28.0 0.3 collective-permute-done.4.refs_5_
  28.3 1.2 %all-to-all-done = bf16[32,8,896]{2,1,0:T(8,128)(2,1)S(1)} async-done(((bf16[32,8,896]{2,1,0:T(8,128)(2,1)}), bf16[32,8,896]{2,1,0:T(8,128)(2,1)S(1)}, u32[]{:S(2)}, u32[]{:S(2)}) %all-to-all-start) | async-done | bytes 458784 | tf_op jit(solution)/shard_map/all_to_all | solution.py:294
  29.5 2.7 %key_grad.1 = (bf16[4,512,128]{2,1,0:T(8,128)(2,1)S(1)}, bf16[8,512,512]{2,1,0:T(8,128)(2,1)S(1)}, bf16[512,128]{1,0:T(8,128)(2,1)S(1)}, f32[64,8,128]{2,1,0:T(8...) custom-call(bf16[256,896]{1,0:T(8,128)(2,1)S(1)} %bitcast.26, bf16[512,128]{1,0:T(8,128)(2,1)S(1)} %copy-done, ...), custom_call_target="tpu_custom_call" | custom-call | flops 1073741824 | bytes 2097152 | tf_op jit(solution)/shard_map/key_grad/pallas_call | solution.py:302
  32.2 1.1 %collective-permute-start.7 = (bf16[4,512,128]{2,1,0:T(8,128)(2,1)S(1)}, bf16[4,512,128]{2,1,0:T(8,128)(2,1)S(1)}, u32[]{:S(2)}, u32[]{:S(2)}) collective-permute-start(bf16[4,512,128]{2,1,0:T(8,128)(2,1)S(1)} %get-tuple-element.35), channel_id=1, source_target_pairs={{0,1},{1,0},{2,3},{3,2},{4,5},{5,4},{6,7},{7,6},{8,9},{9,8},{10,11... | collective-permute-start | bytes 1572872 | tf_op jit(solution)/shard_map/ppermute | solution.py:256
  33.3 1.7 %products.1 = (f32[4,512,128]{2,1,0:T(8,128)S(1)}, f32[512,128]{1,0:T(8,128)S(1)}, f32[4,8,128]{2,1,0:T(8,128)S(1)}) custom-call(bf16[8,512,512]{2,1,0:T(8,128)(2,1)S(1)} %get-tuple-element.29.gated_ref, bf16[128,512]{1,0:T(8,128)(2,1)S(1)} %get-tuple-element.30.weighted_ref, bf16[512,128]{1,0:T(8,128)(2,1)S(1)} %get-tuple-element.31.q_ref, ...), custom_call_target="tpu_custom_call" | custom-call | flops 1073741824 | bytes 2097152 | tf_op jit(solution)/shard_map/products/pallas_call | solution.py:324
  35.0 0.0 collective-permute-done.7
  35.0 0.1 fusion.5
  35.1 1.5 %collective-permute-start.8 = (bf16[512,128]{1,0:T(8,128)(2,1)S(1)}, bf16[512,128]{1,0:T(8,128)(2,1)S(1)}, u32[]{:S(2)}, u32[]{:S(2)}) collective-permute-start(bf16[512,128]{1,0:T(8,128)(2,1)S(1)} %get-tuple-element.39), channel_id=1, source_target_pairs={{0,6},{1,7},{2,4},{3,5},{4,2},{5,3},{6,0},{7,1},{8,14},{9,15},{10,... | collective-permute-start | bytes 393224 | tf_op jit(solution)/shard_map/ppermute | solution.py:256
  36.6 1.5 %collective-permute-start.9 = (bf16[512,128]{1,0:T(8,128)(2,1)S(1)}, bf16[512,128]{1,0:T(8,128)(2,1)S(1)}, u32[]{:S(2)}, u32[]{:S(2)}) collective-permute-start(bf16[512,128]{1,0:T(8,128)(2,1)S(1)} %get-tuple-element.40), channel_id=1, source_target_pairs={{0,4},{1,5},{2,6},{3,7},{4,0},{5,1},{6,2},{7,3},{8,12},{9,13},{10,... | collective-permute-start | bytes 393224 | tf_op jit(solution)/shard_map/ppermute | solution.py:256
  38.1 0.6 collective-permute-start.10
  38.7 0.7 %query_grad.1 = bf16[32,2176]{1,0:T(8,128)(2,1)} custom-call(f32[512,128]{1,0:T(8,128)S(1)} %get-tuple-element.36.term_ref, f32[64,8,128]{2,1,0:T(8,128)S(1)} %get-tuple-element.37.wide_ref, f32[4,8,128]{2,1,0:T(8,128)S(1)} %get-tuple-element.38.extra_ref), custom_call_target="tpu_custom_call" | custom-call | bytes 2097152 | tf_op jit(solution)/shard_map/query_grad/pallas_call | solution.py:344
  39.4 3.3 %all-to-all-start.1 = ((bf16[4,8,2176]{2,1,0:T(8,128)(2,1)}), bf16[4,8,2176]{2,1,0:T(8,128)(2,1)S(1)}, u32[]{:S(2)}, u32[]{:S(2)}) async-start(bf16[4,8,2176]{2,1,0:T(8,128)(2,1)} %bitcast.8), calls=%async_computation.1 | async-start | bytes 278528 | tf_op jit(solution)/shard_map/all_to_all | solution.py:353
  42.7 0.0 collective-permute-done.8
  42.7 1.8 %collective-permute-done.9 = bf16[512,128]{1,0:T(8,128)(2,1)S(1)} collective-permute-done((bf16[512,128]{1,0:T(8,128)(2,1)S(1)}, bf16[512,128]{1,0:T(8,128)(2,1)S(1)}, u32[]{:S(2)}, u32[]{:S(2)}) %collective-permute-start.9) | collective-permute-done | bytes 131104 | tf_op jit(solution)/shard_map/ppermute | solution.py:256
  44.5 0.0 collective-permute-done.10
  44.5 0.1 fusion.6
  44.6 1.2 %collective-permute-start.18 = (bf16[512,128]{1,0:T(8,128)(2,1)S(1)}, bf16[512,128]{1,0:T(8,128)(2,1)S(1)}, u32[]{:S(2)}, u32[]{:S(2)}) collective-permute-start(bf16[512,128]{1,0:T(8,128)(2,1)S(1)} %get-tuple-element.46), channel_id=1, source_target_pairs={{0,8},{8,0},{16,24},{24,16},{1,9},{9,1},{17,25},{25,17},{2,10},{10... | collective-permute-start | bytes 393224 | tf_op jit(solution)/shard_map/ppermute | solution.py:256
  45.8 3.1 %all-to-all-done.1 = bf16[4,8,2176]{2,1,0:T(8,128)(2,1)S(1)} async-done(((bf16[4,8,2176]{2,1,0:T(8,128)(2,1)}), bf16[4,8,2176]{2,1,0:T(8,128)(2,1)S(1)}, u32[]{:S(2)}, u32[]{:S(2)}) %all-to-all-start.1) | async-done | bytes 139296 | tf_op jit(solution)/shard_map/all_to_all | solution.py:353
  48.9 1.6 %collective-permute-start.16 = (bf16[32,2176]{1,0:T(8,128)(2,1)S(1)}, bf16[32,2176]{1,0:T(8,128)(2,1)S(1)}, u32[]{:S(2)}, u32[]{:S(2)}) collective-permute-start(bf16[32,2176]{1,0:T(8,128)(2,1)S(1)} %bitcast.21), channel_id=1, source_target_pairs={{0,6},{1,7},{2,4},{3,5},{4,2},{5,3},{6,0},{7,1},{8,14},{9,15},{10,... | collective-permute-start | bytes 417800 | tf_op jit(solution)/shard_map/ppermute | solution.py:256
  50.5 1.5 %collective-permute-start.14 = (bf16[32,2176]{1,0:T(8,128)(2,1)S(1)}, bf16[32,2176]{1,0:T(8,128)(2,1)S(1)}, u32[]{:S(2)}, u32[]{:S(2)}) collective-permute-start(bf16[32,2176]{1,0:T(8,128)(2,1)S(1)} %bitcast.22), channel_id=1, source_target_pairs={{0,4},{1,5},{2,6},{3,7},{4,0},{5,1},{6,2},{7,3},{8,12},{9,13},{10,... | collective-permute-start | bytes 417800 | tf_op jit(solution)/shard_map/ppermute | solution.py:256
  52.0 0.5 collective-permute-start.12
  52.4 0.0 collective-permute-done.18
  52.5 1.3 %collective-permute-start.19 = (bf16[512,128]{1,0:T(8,128)(2,1)S(1)}, bf16[512,128]{1,0:T(8,128)(2,1)S(1)}, u32[]{:S(2)}, u32[]{:S(2)}) collective-permute-start(bf16[512,128]{1,0:T(8,128)(2,1)S(1)} %fusion.2), channel_id=1, source_target_pairs={{0,16},{8,24},{16,0},{24,8},{1,17},{9,25},{17,1},{25,9},{2,18},{10... | collective-permute-start | bytes 393224 | tf_op jit(solution)/shard_map/ppermute | solution.py:256
  53.8 1.2 %collective-permute-done.16.refs_6_ = bf16[32,2176]{1,0:T(8,128)(2,1)S(1)} collective-permute-done((bf16[32,2176]{1,0:T(8,128)(2,1)S(1)}, bf16[32,2176]{1,0:T(8,128)(2,1)S(1)}, u32[]{:S(2)}, u32[]{:S(2)}) %collective-permute-start.16) | collective-permute-done | bytes 139296 | tf_op jit(solution)/shard_map/ppermute | solution.py:256
  55.0 0.0 collective-permute-start.17
  55.0 1.4 %collective-permute-done.14.refs_4_ = bf16[32,2176]{1,0:T(8,128)(2,1)S(1)} collective-permute-done((bf16[32,2176]{1,0:T(8,128)(2,1)S(1)}, bf16[32,2176]{1,0:T(8,128)(2,1)S(1)}, u32[]{:S(2)}, u32[]{:S(2)}) %collective-permute-start.14) | collective-permute-done | bytes 139296 | tf_op jit(solution)/shard_map/ppermute | solution.py:256
  56.4 0.6 %collective-permute-done.12.refs_2_ = bf16[32,2176]{1,0:T(8,128)(2,1)S(1)} collective-permute-done((bf16[32,2176]{1,0:T(8,128)(2,1)S(1)}, bf16[32,2176]{1,0:T(8,128)(2,1)S(1)}, u32[]{:S(2)}, u32[]{:S(2)}) %collective-permute-start.12) | collective-permute-done | bytes 139296 | tf_op jit(solution)/shard_map/ppermute | solution.py:256
  57.0 1.4 %collective-permute-done.19 = bf16[512,128]{1,0:T(8,128)(2,1)S(1)} collective-permute-done((bf16[512,128]{1,0:T(8,128)(2,1)S(1)}, bf16[512,128]{1,0:T(8,128)(2,1)S(1)}, u32[]{:S(2)}, u32[]{:S(2)}) %collective-permute-start.19) | collective-permute-done | bytes 131104 | tf_op jit(solution)/shard_map/ppermute | solution.py:256
  58.4 0.7 %add_convert_fusion = bf16[512,128]{1,0:T(8,128)(2,1)} fusion(bf16[512,128]{1,0:T(8,128)(2,1)S(1)} %collective-permute-done.19, f32[512,128]{1,0:T(8,128)S(1)} %get-tuple-element.47, bf16[512,128]{1,0:T(8,128)(2,1)S(1)} %collective-permute-done.18), kind=kLoop, calls=%fused_computation.3 | loop fusion | flops 327680 | bytes 655360 | tf_op jit(solution)/shard_map/convert_element_type | solution.py:384
  59.1 0.0 collective-permute-done.11.refs_1_
  59.1 0.0 collective-permute-done.17.refs_7_
  59.1 0.0 collective-permute-done.13.refs_3_
  59.1 1.1 %place.1 = (bf16[256,2048]{1,0:T(8,128)(2,1)}, bf16[16,256]{1,0:T(8,128)(2,1)}, bf16[256]{0:T(256)(128)(2,1)}) custom-call(bf16[32,2176]{1,0:T(8,128)(2,1)S(1)} %bitcast.25, bf16[32,2176]{1,0:T(8,128)(2,1)S(1)} %collective-permute-done.11.refs_1_, bf16[32,2176]{1,0:T(8,128)(2,1)S(1)} %collective-permute-done.12.refs_2_, ...), custom_call_target="tpu_custom_call" | custom-call | bytes 4456448 | tf_op jit(solution)/shard_map/place/pallas_call | solution.py:365
  (7 shorter events, 0.0 us)
Async XLA Ops:
  0.6 11.8 %collective-permute-start.1 = (bf16[512,128]{1,0:T(8,128)(2,1)}, bf16[512,128]{1,0:T(8,128)(2,1)S(1)}, u32[]{:S(2)}, u32[]{:S(2)}) collective-permute-start(bf16[512,128]{1,0:T(8,128)(2,1)} %refs_0_.1), channel_id=1, source_target_pairs={{0,4},{1,5},{2,6},{3,7},{4,0},{5,1},{6,2},{7,3},{8,12},{9,13},{10,... | collective-permute-start | bytes 393224 | tf_op jit(solution)/shard_map/ppermute | solution.py:256
  3.7 8.7 %collective-permute-start = (bf16[512,128]{1,0:T(8,128)(2,1)}, bf16[512,128]{1,0:T(8,128)(2,1)S(1)}, u32[]{:S(2)}, u32[]{:S(2)}) collective-permute-start(bf16[512,128]{1,0:T(8,128)(2,1)} %refs_0_.1), channel_id=1, source_target_pairs={{0,2},{1,3},{2,0},{3,1},{4,6},{5,7},{6,4},{7,5},{8,10},{9,11},{10,... | collective-permute-start | bytes 393224 | tf_op jit(solution)/shard_map/ppermute | solution.py:256
  5.8 10.6 %copy-start = (bf16[512,128]{1,0:T(8,128)(2,1)S(1)}, bf16[512,128]{1,0:T(8,128)(2,1)}, u32[]{:S(2)}) copy-start(bf16[512,128]{1,0:T(8,128)(2,1)} %refs_0_.1) | copy-start | bytes 393220
  12.4 17.1 %all-to-all-start = ((bf16[32,8,896]{2,1,0:T(8,128)(2,1)}), bf16[32,8,896]{2,1,0:T(8,128)(2,1)S(1)}, u32[]{:S(2)}, u32[]{:S(2)}) async-start(bf16[32,8,896]{2,1,0:T(8,128)(2,1)} %bitcast.27), calls=%async_computation | async-start | bytes 917504 | tf_op jit(solution)/shard_map/all_to_all | solution.py:294
  16.4 10.1 %collective-permute-start.5 = (bf16[512,128]{1,0:T(8,128)(2,1)S(1)}, bf16[512,128]{1,0:T(8,128)(2,1)S(1)}, u32[]{:S(2)}, u32[]{:S(2)}) collective-permute-start(bf16[512,128]{1,0:T(8,128)(2,1)S(1)} %copy-done), channel_id=1, source_target_pairs={{0,6},{1,7},{2,4},{3,5},{4,2},{5,3},{6,0},{7,1},{8,14},{9,15},{10,... | collective-permute-start | bytes 393224 | tf_op jit(solution)/shard_map/ppermute | solution.py:256
  19.1 8.7 %collective-permute-start.2 = (bf16[512,128]{1,0:T(8,128)(2,1)S(1)}, bf16[512,128]{1,0:T(8,128)(2,1)S(1)}, u32[]{:S(2)}, u32[]{:S(2)}) collective-permute-start(bf16[512,128]{1,0:T(8,128)(2,1)S(1)} %copy-done), channel_id=1, source_target_pairs={{0,1},{1,0},{2,3},{3,2},{4,5},{5,4},{6,7},{7,6},{8,9},{9,8},{10,11... | collective-permute-start | bytes 393224 | tf_op jit(solution)/shard_map/ppermute | solution.py:256
  26.5 1.3 %collective-permute-start.6 = (bf16[512,128]{1,0:T(8,128)(2,1)S(1)}, bf16[512,128]{1,0:T(8,128)(2,1)S(1)}, u32[]{:S(2)}, u32[]{:S(2)}) collective-permute-start(bf16[512,128]{1,0:T(8,128)(2,1)S(1)} %collective-permute-done.5.refs_6_), channel_id=1, source_target_pairs={{0,1},{1,0},{2,3},{3,2},{4,5},{5,4},{6,7},{7,6},{8,9},{9,8},{10,11... | collective-permute-start | bytes 393224 | tf_op jit(solution)/shard_map/ppermute | solution.py:256
  26.5 1.5 %collective-permute-start.3 = (bf16[512,128]{1,0:T(8,128)(2,1)S(1)}, bf16[512,128]{1,0:T(8,128)(2,1)S(1)}, u32[]{:S(2)}, u32[]{:S(2)}) collective-permute-start(bf16[512,128]{1,0:T(8,128)(2,1)S(1)} %collective-permute-done.refs_2_), channel_id=1, source_target_pairs={{0,1},{1,0},{2,3},{3,2},{4,5},{5,4},{6,7},{7,6},{8,9},{9,8},{10,11... | collective-permute-start | bytes 393224 | tf_op jit(solution)/shard_map/ppermute | solution.py:256
  27.0 1.3 %collective-permute-start.4 = (bf16[512,128]{1,0:T(8,128)(2,1)S(1)}, bf16[512,128]{1,0:T(8,128)(2,1)S(1)}, u32[]{:S(2)}, u32[]{:S(2)}) collective-permute-start(bf16[512,128]{1,0:T(8,128)(2,1)S(1)} %collective-permute-done.1.refs_4_), channel_id=1, source_target_pairs={{0,1},{1,0},{2,3},{3,2},{4,5},{5,4},{6,7},{7,6},{8,9},{9,8},{10,11... | collective-permute-start | bytes 393224 | tf_op jit(solution)/shard_map/ppermute | solution.py:256
  32.2 2.9 %collective-permute-start.7 = (bf16[4,512,128]{2,1,0:T(8,128)(2,1)S(1)}, bf16[4,512,128]{2,1,0:T(8,128)(2,1)S(1)}, u32[]{:S(2)}, u32[]{:S(2)}) collective-permute-start(bf16[4,512,128]{2,1,0:T(8,128)(2,1)S(1)} %get-tuple-element.35), channel_id=1, source_target_pairs={{0,1},{1,0},{2,3},{3,2},{4,5},{5,4},{6,7},{7,6},{8,9},{9,8},{10,11... | collective-permute-start | bytes 1572872 | tf_op jit(solution)/shard_map/ppermute | solution.py:256
  35.1 7.6 %collective-permute-start.8 = (bf16[512,128]{1,0:T(8,128)(2,1)S(1)}, bf16[512,128]{1,0:T(8,128)(2,1)S(1)}, u32[]{:S(2)}, u32[]{:S(2)}) collective-permute-start(bf16[512,128]{1,0:T(8,128)(2,1)S(1)} %get-tuple-element.39), channel_id=1, source_target_pairs={{0,6},{1,7},{2,4},{3,5},{4,2},{5,3},{6,0},{7,1},{8,14},{9,15},{10,... | collective-permute-start | bytes 393224 | tf_op jit(solution)/shard_map/ppermute | solution.py:256
  36.6 7.9 %collective-permute-start.9 = (bf16[512,128]{1,0:T(8,128)(2,1)S(1)}, bf16[512,128]{1,0:T(8,128)(2,1)S(1)}, u32[]{:S(2)}, u32[]{:S(2)}) collective-permute-start(bf16[512,128]{1,0:T(8,128)(2,1)S(1)} %get-tuple-element.40), channel_id=1, source_target_pairs={{0,4},{1,5},{2,6},{3,7},{4,0},{5,1},{6,2},{7,3},{8,12},{9,13},{10,... | collective-permute-start | bytes 393224 | tf_op jit(solution)/shard_map/ppermute | solution.py:256
  38.1 6.4 %collective-permute-start.10 = (bf16[512,128]{1,0:T(8,128)(2,1)S(1)}, bf16[512,128]{1,0:T(8,128)(2,1)S(1)}, u32[]{:S(2)}, u32[]{:S(2)}) collective-permute-start(bf16[512,128]{1,0:T(8,128)(2,1)S(1)} %get-tuple-element.41), channel_id=1, source_target_pairs={{0,2},{1,3},{2,0},{3,1},{4,6},{5,7},{6,4},{7,5},{8,10},{9,11},{10,... | collective-permute-start | bytes 393224 | tf_op jit(solution)/shard_map/ppermute | solution.py:256
  39.4 9.6 %all-to-all-start.1 = ((bf16[4,8,2176]{2,1,0:T(8,128)(2,1)}), bf16[4,8,2176]{2,1,0:T(8,128)(2,1)S(1)}, u32[]{:S(2)}, u32[]{:S(2)}) async-start(bf16[4,8,2176]{2,1,0:T(8,128)(2,1)} %bitcast.8), calls=%async_computation.1 | async-start | bytes 278528 | tf_op jit(solution)/shard_map/all_to_all | solution.py:353
  44.6 7.8 %collective-permute-start.18 = (bf16[512,128]{1,0:T(8,128)(2,1)S(1)}, bf16[512,128]{1,0:T(8,128)(2,1)S(1)}, u32[]{:S(2)}, u32[]{:S(2)}) collective-permute-start(bf16[512,128]{1,0:T(8,128)(2,1)S(1)} %get-tuple-element.46), channel_id=1, source_target_pairs={{0,8},{8,0},{16,24},{24,16},{1,9},{9,1},{17,25},{25,17},{2,10},{10... | collective-permute-start | bytes 393224 | tf_op jit(solution)/shard_map/ppermute | solution.py:256
  48.9 6.0 %collective-permute-start.16 = (bf16[32,2176]{1,0:T(8,128)(2,1)S(1)}, bf16[32,2176]{1,0:T(8,128)(2,1)S(1)}, u32[]{:S(2)}, u32[]{:S(2)}) collective-permute-start(bf16[32,2176]{1,0:T(8,128)(2,1)S(1)} %bitcast.21), channel_id=1, source_target_pairs={{0,6},{1,7},{2,4},{3,5},{4,2},{5,3},{6,0},{7,1},{8,14},{9,15},{10,... | collective-permute-start | bytes 417800 | tf_op jit(solution)/shard_map/ppermute | solution.py:256
  50.5 5.9 %collective-permute-start.14 = (bf16[32,2176]{1,0:T(8,128)(2,1)S(1)}, bf16[32,2176]{1,0:T(8,128)(2,1)S(1)}, u32[]{:S(2)}, u32[]{:S(2)}) collective-permute-start(bf16[32,2176]{1,0:T(8,128)(2,1)S(1)} %bitcast.22), channel_id=1, source_target_pairs={{0,4},{1,5},{2,6},{3,7},{4,0},{5,1},{6,2},{7,3},{8,12},{9,13},{10,... | collective-permute-start | bytes 417800 | tf_op jit(solution)/shard_map/ppermute | solution.py:256
  52.0 5.1 %collective-permute-start.12 = (bf16[32,2176]{1,0:T(8,128)(2,1)S(1)}, bf16[32,2176]{1,0:T(8,128)(2,1)S(1)}, u32[]{:S(2)}, u32[]{:S(2)}) collective-permute-start(bf16[32,2176]{1,0:T(8,128)(2,1)S(1)} %bitcast.23), channel_id=1, source_target_pairs={{0,2},{1,3},{2,0},{3,1},{4,6},{5,7},{6,4},{7,5},{8,10},{9,11},{10,... | collective-permute-start | bytes 417800 | tf_op jit(solution)/shard_map/ppermute | solution.py:256
  52.5 5.9 %collective-permute-start.19 = (bf16[512,128]{1,0:T(8,128)(2,1)S(1)}, bf16[512,128]{1,0:T(8,128)(2,1)S(1)}, u32[]{:S(2)}, u32[]{:S(2)}) collective-permute-start(bf16[512,128]{1,0:T(8,128)(2,1)S(1)} %fusion.2), channel_id=1, source_target_pairs={{0,16},{8,24},{16,0},{24,8},{1,17},{9,25},{17,1},{25,9},{2,18},{10... | collective-permute-start | bytes 393224 | tf_op jit(solution)/shard_map/ppermute | solution.py:256
  53.8 5.3 %collective-permute-start.11 = (bf16[32,2176]{1,0:T(8,128)(2,1)S(1)}, bf16[32,2176]{1,0:T(8,128)(2,1)S(1)}, u32[]{:S(2)}, u32[]{:S(2)}) collective-permute-start(bf16[32,2176]{1,0:T(8,128)(2,1)S(1)} %bitcast.24), channel_id=1, source_target_pairs={{0,1},{1,0},{2,3},{3,2},{4,5},{5,4},{6,7},{7,6},{8,9},{9,8},{10,11... | collective-permute-start | bytes 417800 | tf_op jit(solution)/shard_map/ppermute | solution.py:256
  55.0 4.1 %collective-permute-start.17 = (bf16[32,2176]{1,0:T(8,128)(2,1)S(1)}, bf16[32,2176]{1,0:T(8,128)(2,1)S(1)}, u32[]{:S(2)}, u32[]{:S(2)}) collective-permute-start(bf16[32,2176]{1,0:T(8,128)(2,1)S(1)} %collective-permute-done.16.refs_6_), channel_id=1, source_target_pairs={{0,1},{1,0},{2,3},{3,2},{4,5},{5,4},{6,7},{7,6},{8,9},{9,8},{10,11... | collective-permute-start | bytes 417800 | tf_op jit(solution)/shard_map/ppermute | solution.py:256
  56.4 2.7 %collective-permute-start.15 = (bf16[32,2176]{1,0:T(8,128)(2,1)S(1)}, bf16[32,2176]{1,0:T(8,128)(2,1)S(1)}, u32[]{:S(2)}, u32[]{:S(2)}) collective-permute-start(bf16[32,2176]{1,0:T(8,128)(2,1)S(1)} %collective-permute-done.14.refs_4_), channel_id=1, source_target_pairs={{0,1},{1,0},{2,3},{3,2},{4,5},{5,4},{6,7},{7,6},{8,9},{9,8},{10,11... | collective-permute-start | bytes 417800 | tf_op jit(solution)/shard_map/ppermute | solution.py:256
  57.0 2.1 %collective-permute-start.13 = (bf16[32,2176]{1,0:T(8,128)(2,1)S(1)}, bf16[32,2176]{1,0:T(8,128)(2,1)S(1)}, u32[]{:S(2)}, u32[]{:S(2)}) collective-permute-start(bf16[32,2176]{1,0:T(8,128)(2,1)S(1)} %collective-permute-done.12.refs_2_), channel_id=1, source_target_pairs={{0,1},{1,0},{2,3},{3,2},{4,5},{5,4},{6,7},{7,6},{8,9},{9,8},{10,11... | collective-permute-start | bytes 417800 | tf_op jit(solution)/shard_map/ppermute | solution.py:256

commit v8 on v7

--- a/solution.py
+++ b/solution.py
@@ -338,7 +338,7 @@
     sides = [x.astype(BF16) for x in paired[1:]]
     term, *sides = lax.optimization_barrier((term, *sides))
     mine = paired[0]
-    for e in reversed(range(1, half)):
+    for e in [half - 1, *range(1, half - 1)]:
         mine = mine + swap(sides[e - 1], "seq", n_seq, 2 * e).astype(F32)
 
     rows_out = pl.pallas_call(

time: 60.5 us -> 60.5 us (level)
  no operation moved by 1% of the time
where the time goes in v8:
time: 60.5 us; the launch traced here: 60.2 us
  starting transfers between devices  26.4 us (44%)
  waiting for transfers between devices  18.9 us (31%)
  Pallas kernels  12.7 us (21%)
  between operations  1.4 us (2%)
  other arithmetic  0.91 us (2%)
    ppermute x20, starting transfers between devices, swap(): return lax.ppermute(x, axis, [(i, i ^ mask) for i in range(n)])  19.1 us
    ppermute x20, waiting for transfers between devices, swap(): return lax.ppermute(x, axis, [(i, i ^ mask) for i in range(n)])  15 us
    pallas_call x1, Pallas kernels, fast_local(): pl.pallas_call(functools.partial(attention_kernel, parts), in_specs=[hbm]...  6.56 us
    all_to_all x1, starting transfers between devices, fast_local(): got = lax.all_to_all(sent, ('seq', 'head'), 0, 0, tiled=True)  3.97 us
    all_to_all x1, starting transfers between devices, fast_local(): own_rows = lax.all_to_all(rows_out, 'head', 0, 0, tiled=True)  3.33 us
    all_to_all x1, waiting for transfers between devices, fast_local(): own_rows = lax.all_to_all(rows_out, 'head', 0, 0, tiled=True)  2.7 us
    pallas_call x1, Pallas kernels, fast_local(): pl.pallas_call(functools.partial(keys_kernel, n_seq, n_head, own), in_spe...  2.66 us
    pallas_call x1, Pallas kernels, fast_local(): pl.pallas_call(functools.partial(products_kernel, n_seq, n_head), in_spec...  1.71 us
  transfers between devices with their start and end apart: 22, of which 11 were waited for; matrix products, arithmetic and copies ran while one was open for 1% of the time, Pallas kernels for 15%

profile of v8, /device:TPU:0, one launch (start us, length us, event | category | flops | bytes accessed | tf_op | source)
XLA Modules:
  0.0 60.2 jit_solution(10950316981060563339)
XLA Ops:
  0.6 3.0 %collective-permute-start.1 = (bf16[512,128]{1,0:T(8,128)(2,1)}, bf16[512,128]{1,0:T(8,128)(2,1)S(1)}, u32[]{:S(2)}, u32[]{:S(2)}) collective-permute-start(bf16[512,128]{1,0:T(8,128)(2,1)} %refs_0_.1), channel_id=1, source_target_pairs={{0,4},{1,5},{2,6},{3,7},{4,0},{5,1},{6,2},{7,3},{8,12},{9,13},{10,... | collective-permute-start | bytes 393224 | tf_op jit(solution)/shard_map/ppermute | solution.py:256
  3.7 1.5 %collective-permute-start = (bf16[512,128]{1,0:T(8,128)(2,1)}, bf16[512,128]{1,0:T(8,128)(2,1)S(1)}, u32[]{:S(2)}, u32[]{:S(2)}) collective-permute-start(bf16[512,128]{1,0:T(8,128)(2,1)} %refs_0_.1), channel_id=1, source_target_pairs={{0,2},{1,3},{2,0},{3,1},{4,6},{5,7},{6,4},{7,5},{8,10},{9,11},{10,... | collective-permute-start | bytes 393224 | tf_op jit(solution)/shard_map/ppermute | solution.py:256
  5.8 6.6 %attention.1 = bf16[256,896]{1,0:T(8,128)(2,1)} custom-call(s32[1]{0:T(128)S(6)} %copy.12.block_hbm, s32[1,256]{1,0:T(1,128)} %bitcast.31, bf16[256,6144]{1,0:T(8,128)(2,1)} %q_hbm.1, bf16[512,6144]{1,0:T(8,128)(2,1)} %k_hbm.1, f32[32,256]{1,0:T(8,128)} %bitcast.28, bf16[256,2048]{1,0:T(8,128)(2,1)} %qi_hbm.1, f32[16,256]{1,0:T(8,128)} %bitcast.29), custom_call_target="tpu_custom_call" | custom-call | flops 3221225472 | bytes 9437184 | tf_op jit(solution)/shard_map/attention/pallas_call | solution.py:264
  12.4 0.0 collective-permute-done.1.refs_4_
  12.4 0.0 collective-permute-done.refs_2_
  12.4 4.0 %all-to-all-start = ((bf16[32,8,896]{2,1,0:T(8,128)(2,1)}), bf16[32,8,896]{2,1,0:T(8,128)(2,1)S(1)}, u32[]{:S(2)}, u32[]{:S(2)}) async-start(bf16[32,8,896]{2,1,0:T(8,128)(2,1)} %bitcast.27), calls=%async_computation | async-start | bytes 917504 | tf_op jit(solution)/shard_map/all_to_all | solution.py:294
  16.4 2.7 %collective-permute-start.5 = (bf16[512,128]{1,0:T(8,128)(2,1)S(1)}, bf16[512,128]{1,0:T(8,128)(2,1)S(1)}, u32[]{:S(2)}, u32[]{:S(2)}) collective-permute-start(bf16[512,128]{1,0:T(8,128)(2,1)S(1)} %copy-done), channel_id=1, source_target_pairs={{0,6},{1,7},{2,4},{3,5},{4,2},{5,3},{6,0},{7,1},{8,14},{9,15},{10,... | collective-permute-start | bytes 393224 | tf_op jit(solution)/shard_map/ppermute | solution.py:256
  19.1 0.0 collective-permute-start.2
  19.1 7.3 %collective-permute-done.5.refs_6_ = bf16[512,128]{1,0:T(8,128)(2,1)S(1)} collective-permute-done((bf16[512,128]{1,0:T(8,128)(2,1)S(1)}, bf16[512,128]{1,0:T(8,128)(2,1)S(1)}, u32[]{:S(2)}, u32[]{:S(2)}) %collective-permute-start.5) | collective-permute-done | bytes 131104 | tf_op jit(solution)/shard_map/ppermute | solution.py:256
  26.5 0.0 collective-permute-start.6
  26.5 0.5 collective-permute-start.3
  27.0 0.0 collective-permute-start.4
  27.0 0.8 %collective-permute-done.6.refs_7_ = bf16[512,128]{1,0:T(8,128)(2,1)S(1)} collective-permute-done((bf16[512,128]{1,0:T(8,128)(2,1)S(1)}, bf16[512,128]{1,0:T(8,128)(2,1)S(1)}, u32[]{:S(2)}, u32[]{:S(2)}) %collective-permute-start.6) | collective-permute-done | bytes 131104 | tf_op jit(solution)/shard_map/ppermute | solution.py:256
  27.8 0.2 collective-permute-done.3.refs_3_
  28.0 0.3 collective-permute-done.4.refs_5_
  28.3 1.2 %all-to-all-done = bf16[32,8,896]{2,1,0:T(8,128)(2,1)S(1)} async-done(((bf16[32,8,896]{2,1,0:T(8,128)(2,1)}), bf16[32,8,896]{2,1,0:T(8,128)(2,1)S(1)}, u32[]{:S(2)}, u32[]{:S(2)}) %all-to-all-start) | async-done | bytes 458784 | tf_op jit(solution)/shard_map/all_to_all | solution.py:294
  29.5 2.7 %key_grad.1 = (bf16[4,512,128]{2,1,0:T(8,128)(2,1)S(1)}, bf16[8,512,512]{2,1,0:T(8,128)(2,1)S(1)}, bf16[512,128]{1,0:T(8,128)(2,1)S(1)}, f32[64,8,128]{2,1,0:T(8...) custom-call(bf16[256,896]{1,0:T(8,128)(2,1)S(1)} %bitcast.26, bf16[512,128]{1,0:T(8,128)(2,1)S(1)} %copy-done, ...), custom_call_target="tpu_custom_call" | custom-call | flops 1073741824 | bytes 2097152 | tf_op jit(solution)/shard_map/key_grad/pallas_call | solution.py:302
  32.2 1.1 %collective-permute-start.7 = (bf16[4,512,128]{2,1,0:T(8,128)(2,1)S(1)}, bf16[4,512,128]{2,1,0:T(8,128)(2,1)S(1)}, u32[]{:S(2)}, u32[]{:S(2)}) collective-permute-start(bf16[4,512,128]{2,1,0:T(8,128)(2,1)S(1)} %get-tuple-element.35), channel_id=1, source_target_pairs={{0,1},{1,0},{2,3},{3,2},{4,5},{5,4},{6,7},{7,6},{8,9},{9,8},{10,11... | collective-permute-start | bytes 1572872 | tf_op jit(solution)/shard_map/ppermute | solution.py:256
  33.3 1.7 %products.1 = (f32[4,512,128]{2,1,0:T(8,128)S(1)}, f32[512,128]{1,0:T(8,128)S(1)}, f32[4,8,128]{2,1,0:T(8,128)S(1)}) custom-call(bf16[8,512,512]{2,1,0:T(8,128)(2,1)S(1)} %get-tuple-element.29.gated_ref, bf16[128,512]{1,0:T(8,128)(2,1)S(1)} %get-tuple-element.30.weighted_ref, bf16[512,128]{1,0:T(8,128)(2,1)S(1)} %get-tuple-element.31.q_ref, ...), custom_call_target="tpu_custom_call" | custom-call | flops 1073741824 | bytes 2097152 | tf_op jit(solution)/shard_map/products/pallas_call | solution.py:324
  35.0 0.0 collective-permute-done.7
  35.0 0.1 fusion.5
  35.1 1.5 %collective-permute-start.8 = (bf16[512,128]{1,0:T(8,128)(2,1)S(1)}, bf16[512,128]{1,0:T(8,128)(2,1)S(1)}, u32[]{:S(2)}, u32[]{:S(2)}) collective-permute-start(bf16[512,128]{1,0:T(8,128)(2,1)S(1)} %get-tuple-element.39), channel_id=1, source_target_pairs={{0,6},{1,7},{2,4},{3,5},{4,2},{5,3},{6,0},{7,1},{8,14},{9,15},{10,... | collective-permute-start | bytes 393224 | tf_op jit(solution)/shard_map/ppermute | solution.py:256
  36.6 1.5 %collective-permute-start.9 = (bf16[512,128]{1,0:T(8,128)(2,1)S(1)}, bf16[512,128]{1,0:T(8,128)(2,1)S(1)}, u32[]{:S(2)}, u32[]{:S(2)}) collective-permute-start(bf16[512,128]{1,0:T(8,128)(2,1)S(1)} %get-tuple-element.40), channel_id=1, source_target_pairs={{0,2},{1,3},{2,0},{3,1},{4,6},{5,7},{6,4},{7,5},{8,10},{9,11},{10,... | collective-permute-start | bytes 393224 | tf_op jit(solution)/shard_map/ppermute | solution.py:256
  38.1 0.6 collective-permute-start.10
  38.7 0.7 %query_grad.1 = bf16[32,2176]{1,0:T(8,128)(2,1)} custom-call(f32[512,128]{1,0:T(8,128)S(1)} %get-tuple-element.36.term_ref, f32[64,8,128]{2,1,0:T(8,128)S(1)} %get-tuple-element.37.wide_ref, f32[4,8,128]{2,1,0:T(8,128)S(1)} %get-tuple-element.38.extra_ref), custom_call_target="tpu_custom_call" | custom-call | bytes 2097152 | tf_op jit(solution)/shard_map/query_grad/pallas_call | solution.py:344
  39.4 3.3 %all-to-all-start.1 = ((bf16[4,8,2176]{2,1,0:T(8,128)(2,1)}), bf16[4,8,2176]{2,1,0:T(8,128)(2,1)S(1)}, u32[]{:S(2)}, u32[]{:S(2)}) async-start(bf16[4,8,2176]{2,1,0:T(8,128)(2,1)} %bitcast.8), calls=%async_computation.1 | async-start | bytes 278528 | tf_op jit(solution)/shard_map/all_to_all | solution.py:353
  42.7 0.0 collective-permute-done.8
  42.7 1.8 %collective-permute-done.9 = bf16[512,128]{1,0:T(8,128)(2,1)S(1)} collective-permute-done((bf16[512,128]{1,0:T(8,128)(2,1)S(1)}, bf16[512,128]{1,0:T(8,128)(2,1)S(1)}, u32[]{:S(2)}, u32[]{:S(2)}) %collective-permute-start.9) | collective-permute-done | bytes 131104 | tf_op jit(solution)/shard_map/ppermute | solution.py:256
  44.5 0.0 collective-permute-done.10
  44.5 0.1 fusion.6
  44.6 1.7 %collective-permute-start.18 = (bf16[512,128]{1,0:T(8,128)(2,1)S(1)}, bf16[512,128]{1,0:T(8,128)(2,1)S(1)}, u32[]{:S(2)}, u32[]{:S(2)}) collective-permute-start(bf16[512,128]{1,0:T(8,128)(2,1)S(1)} %get-tuple-element.46), channel_id=1, source_target_pairs={{0,8},{8,0},{16,24},{24,16},{1,9},{9,1},{17,25},{25,17},{2,10},{10... | collective-permute-start | bytes 393224 | tf_op jit(solution)/shard_map/ppermute | solution.py:256
  46.3 2.7 %all-to-all-done.1 = bf16[4,8,2176]{2,1,0:T(8,128)(2,1)S(1)} async-done(((bf16[4,8,2176]{2,1,0:T(8,128)(2,1)}), bf16[4,8,2176]{2,1,0:T(8,128)(2,1)S(1)}, u32[]{:S(2)}, u32[]{:S(2)}) %all-to-all-start.1) | async-done | bytes 139296 | tf_op jit(solution)/shard_map/all_to_all | solution.py:353
  49.0 1.5 %collective-permute-start.16 = (bf16[32,2176]{1,0:T(8,128)(2,1)S(1)}, bf16[32,2176]{1,0:T(8,128)(2,1)S(1)}, u32[]{:S(2)}, u32[]{:S(2)}) collective-permute-start(bf16[32,2176]{1,0:T(8,128)(2,1)S(1)} %bitcast.21), channel_id=1, source_target_pairs={{0,6},{1,7},{2,4},{3,5},{4,2},{5,3},{6,0},{7,1},{8,14},{9,15},{10,... | collective-permute-start | bytes 417800 | tf_op jit(solution)/shard_map/ppermute | solution.py:256
  50.5 1.5 %collective-permute-start.14 = (bf16[32,2176]{1,0:T(8,128)(2,1)S(1)}, bf16[32,2176]{1,0:T(8,128)(2,1)S(1)}, u32[]{:S(2)}, u32[]{:S(2)}) collective-permute-start(bf16[32,2176]{1,0:T(8,128)(2,1)S(1)} %bitcast.22), channel_id=1, source_target_pairs={{0,4},{1,5},{2,6},{3,7},{4,0},{5,1},{6,2},{7,3},{8,12},{9,13},{10,... | collective-permute-start | bytes 417800 | tf_op jit(solution)/shard_map/ppermute | solution.py:256
  52.0 0.5 collective-permute-start.12
  52.5 0.0 collective-permute-done.18
  52.5 1.4 %collective-permute-start.19 = (bf16[512,128]{1,0:T(8,128)(2,1)S(1)}, bf16[512,128]{1,0:T(8,128)(2,1)S(1)}, u32[]{:S(2)}, u32[]{:S(2)}) collective-permute-start(bf16[512,128]{1,0:T(8,128)(2,1)S(1)} %fusion.2), channel_id=1, source_target_pairs={{0,16},{8,24},{16,0},{24,8},{1,17},{9,25},{17,1},{25,9},{2,18},{10... | collective-permute-start | bytes 393224 | tf_op jit(solution)/shard_map/ppermute | solution.py:256
  53.9 0.0 collective-permute-start.11
  53.9 1.1 %collective-permute-done.16.refs_6_ = bf16[32,2176]{1,0:T(8,128)(2,1)S(1)} collective-permute-done((bf16[32,2176]{1,0:T(8,128)(2,1)S(1)}, bf16[32,2176]{1,0:T(8,128)(2,1)S(1)}, u32[]{:S(2)}, u32[]{:S(2)}) %collective-permute-start.16) | collective-permute-done | bytes 139296 | tf_op jit(solution)/shard_map/ppermute | solution.py:256
  55.0 0.0 collective-permute-start.17
  55.0 1.4 %collective-permute-done.14.refs_4_ = bf16[32,2176]{1,0:T(8,128)(2,1)S(1)} collective-permute-done((bf16[32,2176]{1,0:T(8,128)(2,1)S(1)}, bf16[32,2176]{1,0:T(8,128)(2,1)S(1)}, u32[]{:S(2)}, u32[]{:S(2)}) %collective-permute-start.14) | collective-permute-done | bytes 139296 | tf_op jit(solution)/shard_map/ppermute | solution.py:256
  56.4 0.0 collective-permute-start.15
  56.4 0.6 collective-permute-done.12.refs_2_
  57.0 0.0 collective-permute-start.13
  57.0 1.4 %collective-permute-done.19 = bf16[512,128]{1,0:T(8,128)(2,1)S(1)} collective-permute-done((bf16[512,128]{1,0:T(8,128)(2,1)S(1)}, bf16[512,128]{1,0:T(8,128)(2,1)S(1)}, u32[]{:S(2)}, u32[]{:S(2)}) %collective-permute-start.19) | collective-permute-done | bytes 131104 | tf_op jit(solution)/shard_map/ppermute | solution.py:256
  58.4 0.7 %add_convert_fusion = bf16[512,128]{1,0:T(8,128)(2,1)} fusion(bf16[512,128]{1,0:T(8,128)(2,1)S(1)} %collective-permute-done.19, f32[512,128]{1,0:T(8,128)S(1)} %get-tuple-element.47, bf16[512,128]{1,0:T(8,128)(2,1)S(1)} %collective-permute-done.18), kind=kLoop, calls=%fused_computation.3 | loop fusion | flops 327680 | bytes 655360 | tf_op jit(solution)/shard_map/convert_element_type | solution.py:384
  59.2 0.0 collective-permute-done.15.refs_5_
  59.2 1.1 %place.1 = (bf16[256,2048]{1,0:T(8,128)(2,1)}, bf16[16,256]{1,0:T(8,128)(2,1)}, bf16[256]{0:T(256)(128)(2,1)}) custom-call(bf16[32,2176]{1,0:T(8,128)(2,1)S(1)} %bitcast.25, bf16[32,2176]{1,0:T(8,128)(2,1)S(1)} %collective-permute-done.11.refs_1_, bf16[32,2176]{1,0:T(8,128)(2,1)S(1)} %collective-permute-done.12.refs_2_, ...), custom_call_target="tpu_custom_call" | custom-call | bytes 4456448 | tf_op jit(solution)/shard_map/place/pallas_call | solution.py:365
  (7 shorter events, 0.0 us)
Async XLA Ops:
  0.6 11.8 %collective-permute-start.1 = (bf16[512,128]{1,0:T(8,128)(2,1)}, bf16[512,128]{1,0:T(8,128)(2,1)S(1)}, u32[]{:S(2)}, u32[]{:S(2)}) collective-permute-start(bf16[512,128]{1,0:T(8,128)(2,1)} %refs_0_.1), channel_id=1, source_target_pairs={{0,4},{1,5},{2,6},{3,7},{4,0},{5,1},{6,2},{7,3},{8,12},{9,13},{10,... | collective-permute-start | bytes 393224 | tf_op jit(solution)/shard_map/ppermute | solution.py:256
  3.7 8.7 %collective-permute-start = (bf16[512,128]{1,0:T(8,128)(2,1)}, bf16[512,128]{1,0:T(8,128)(2,1)S(1)}, u32[]{:S(2)}, u32[]{:S(2)}) collective-permute-start(bf16[512,128]{1,0:T(8,128)(2,1)} %refs_0_.1), channel_id=1, source_target_pairs={{0,2},{1,3},{2,0},{3,1},{4,6},{5,7},{6,4},{7,5},{8,10},{9,11},{10,... | collective-permute-start | bytes 393224 | tf_op jit(solution)/shard_map/ppermute | solution.py:256
  5.8 10.6 %copy-start = (bf16[512,128]{1,0:T(8,128)(2,1)S(1)}, bf16[512,128]{1,0:T(8,128)(2,1)}, u32[]{:S(2)}) copy-start(bf16[512,128]{1,0:T(8,128)(2,1)} %refs_0_.1) | copy-start | bytes 393220
  12.4 17.1 %all-to-all-start = ((bf16[32,8,896]{2,1,0:T(8,128)(2,1)}), bf16[32,8,896]{2,1,0:T(8,128)(2,1)S(1)}, u32[]{:S(2)}, u32[]{:S(2)}) async-start(bf16[32,8,896]{2,1,0:T(8,128)(2,1)} %bitcast.27), calls=%async_computation | async-start | bytes 917504 | tf_op jit(solution)/shard_map/all_to_all | solution.py:294
  16.4 10.1 %collective-permute-start.5 = (bf16[512,128]{1,0:T(8,128)(2,1)S(1)}, bf16[512,128]{1,0:T(8,128)(2,1)S(1)}, u32[]{:S(2)}, u32[]{:S(2)}) collective-permute-start(bf16[512,128]{1,0:T(8,128)(2,1)S(1)} %copy-done), channel_id=1, source_target_pairs={{0,6},{1,7},{2,4},{3,5},{4,2},{5,3},{6,0},{7,1},{8,14},{9,15},{10,... | collective-permute-start | bytes 393224 | tf_op jit(solution)/shard_map/ppermute | solution.py:256
  19.1 8.7 %collective-permute-start.2 = (bf16[512,128]{1,0:T(8,128)(2,1)S(1)}, bf16[512,128]{1,0:T(8,128)(2,1)S(1)}, u32[]{:S(2)}, u32[]{:S(2)}) collective-permute-start(bf16[512,128]{1,0:T(8,128)(2,1)S(1)} %copy-done), channel_id=1, source_target_pairs={{0,1},{1,0},{2,3},{3,2},{4,5},{5,4},{6,7},{7,6},{8,9},{9,8},{10,11... | collective-permute-start | bytes 393224 | tf_op jit(solution)/shard_map/ppermute | solution.py:256
  26.5 1.3 %collective-permute-start.6 = (bf16[512,128]{1,0:T(8,128)(2,1)S(1)}, bf16[512,128]{1,0:T(8,128)(2,1)S(1)}, u32[]{:S(2)}, u32[]{:S(2)}) collective-permute-start(bf16[512,128]{1,0:T(8,128)(2,1)S(1)} %collective-permute-done.5.refs_6_), channel_id=1, source_target_pairs={{0,1},{1,0},{2,3},{3,2},{4,5},{5,4},{6,7},{7,6},{8,9},{9,8},{10,11... | collective-permute-start | bytes 393224 | tf_op jit(solution)/shard_map/ppermute | solution.py:256
  26.5 1.5 %collective-permute-start.3 = (bf16[512,128]{1,0:T(8,128)(2,1)S(1)}, bf16[512,128]{1,0:T(8,128)(2,1)S(1)}, u32[]{:S(2)}, u32[]{:S(2)}) collective-permute-start(bf16[512,128]{1,0:T(8,128)(2,1)S(1)} %collective-permute-done.refs_2_), channel_id=1, source_target_pairs={{0,1},{1,0},{2,3},{3,2},{4,5},{5,4},{6,7},{7,6},{8,9},{9,8},{10,11... | collective-permute-start | bytes 393224 | tf_op jit(solution)/shard_map/ppermute | solution.py:256
  27.0 1.3 %collective-permute-start.4 = (bf16[512,128]{1,0:T(8,128)(2,1)S(1)}, bf16[512,128]{1,0:T(8,128)(2,1)S(1)}, u32[]{:S(2)}, u32[]{:S(2)}) collective-permute-start(bf16[512,128]{1,0:T(8,128)(2,1)S(1)} %collective-permute-done.1.refs_4_), channel_id=1, source_target_pairs={{0,1},{1,0},{2,3},{3,2},{4,5},{5,4},{6,7},{7,6},{8,9},{9,8},{10,11... | collective-permute-start | bytes 393224 | tf_op jit(solution)/shard_map/ppermute | solution.py:256
  32.2 2.9 %collective-permute-start.7 = (bf16[4,512,128]{2,1,0:T(8,128)(2,1)S(1)}, bf16[4,512,128]{2,1,0:T(8,128)(2,1)S(1)}, u32[]{:S(2)}, u32[]{:S(2)}) collective-permute-start(bf16[4,512,128]{2,1,0:T(8,128)(2,1)S(1)} %get-tuple-element.35), channel_id=1, source_target_pairs={{0,1},{1,0},{2,3},{3,2},{4,5},{5,4},{6,7},{7,6},{8,9},{9,8},{10,11... | collective-permute-start | bytes 1572872 | tf_op jit(solution)/shard_map/ppermute | solution.py:256
  35.1 7.6 %collective-permute-start.8 = (bf16[512,128]{1,0:T(8,128)(2,1)S(1)}, bf16[512,128]{1,0:T(8,128)(2,1)S(1)}, u32[]{:S(2)}, u32[]{:S(2)}) collective-permute-start(bf16[512,128]{1,0:T(8,128)(2,1)S(1)} %get-tuple-element.39), channel_id=1, source_target_pairs={{0,6},{1,7},{2,4},{3,5},{4,2},{5,3},{6,0},{7,1},{8,14},{9,15},{10,... | collective-permute-start | bytes 393224 | tf_op jit(solution)/shard_map/ppermute | solution.py:256
  36.6 7.9 %collective-permute-start.9 = (bf16[512,128]{1,0:T(8,128)(2,1)S(1)}, bf16[512,128]{1,0:T(8,128)(2,1)S(1)}, u32[]{:S(2)}, u32[]{:S(2)}) collective-permute-start(bf16[512,128]{1,0:T(8,128)(2,1)S(1)} %get-tuple-element.40), channel_id=1, source_target_pairs={{0,2},{1,3},{2,0},{3,1},{4,6},{5,7},{6,4},{7,5},{8,10},{9,11},{10,... | collective-permute-start | bytes 393224 | tf_op jit(solution)/shard_map/ppermute | solution.py:256
  38.1 6.4 %collective-permute-start.10 = (bf16[512,128]{1,0:T(8,128)(2,1)S(1)}, bf16[512,128]{1,0:T(8,128)(2,1)S(1)}, u32[]{:S(2)}, u32[]{:S(2)}) collective-permute-start(bf16[512,128]{1,0:T(8,128)(2,1)S(1)} %get-tuple-element.41), channel_id=1, source_target_pairs={{0,4},{1,5},{2,6},{3,7},{4,0},{5,1},{6,2},{7,3},{8,12},{9,13},{10,... | collective-permute-start | bytes 393224 | tf_op jit(solution)/shard_map/ppermute | solution.py:256
  39.4 9.6 %all-to-all-start.1 = ((bf16[4,8,2176]{2,1,0:T(8,128)(2,1)}), bf16[4,8,2176]{2,1,0:T(8,128)(2,1)S(1)}, u32[]{:S(2)}, u32[]{:S(2)}) async-start(bf16[4,8,2176]{2,1,0:T(8,128)(2,1)} %bitcast.8), calls=%async_computation.1 | async-start | bytes 278528 | tf_op jit(solution)/shard_map/all_to_all | solution.py:353
  44.6 7.9 %collective-permute-start.18 = (bf16[512,128]{1,0:T(8,128)(2,1)S(1)}, bf16[512,128]{1,0:T(8,128)(2,1)S(1)}, u32[]{:S(2)}, u32[]{:S(2)}) collective-permute-start(bf16[512,128]{1,0:T(8,128)(2,1)S(1)} %get-tuple-element.46), channel_id=1, source_target_pairs={{0,8},{8,0},{16,24},{24,16},{1,9},{9,1},{17,25},{25,17},{2,10},{10... | collective-permute-start | bytes 393224 | tf_op jit(solution)/shard_map/ppermute | solution.py:256
  49.0 6.0 %collective-permute-start.16 = (bf16[32,2176]{1,0:T(8,128)(2,1)S(1)}, bf16[32,2176]{1,0:T(8,128)(2,1)S(1)}, u32[]{:S(2)}, u32[]{:S(2)}) collective-permute-start(bf16[32,2176]{1,0:T(8,128)(2,1)S(1)} %bitcast.21), channel_id=1, source_target_pairs={{0,6},{1,7},{2,4},{3,5},{4,2},{5,3},{6,0},{7,1},{8,14},{9,15},{10,... | collective-permute-start | bytes 417800 | tf_op jit(solution)/shard_map/ppermute | solution.py:256
  50.5 5.9 %collective-permute-start.14 = (bf16[32,2176]{1,0:T(8,128)(2,1)S(1)}, bf16[32,2176]{1,0:T(8,128)(2,1)S(1)}, u32[]{:S(2)}, u32[]{:S(2)}) collective-permute-start(bf16[32,2176]{1,0:T(8,128)(2,1)S(1)} %bitcast.22), channel_id=1, source_target_pairs={{0,4},{1,5},{2,6},{3,7},{4,0},{5,1},{6,2},{7,3},{8,12},{9,13},{10,... | collective-permute-start | bytes 417800 | tf_op jit(solution)/shard_map/ppermute | solution.py:256
  52.0 5.1 %collective-permute-start.12 = (bf16[32,2176]{1,0:T(8,128)(2,1)S(1)}, bf16[32,2176]{1,0:T(8,128)(2,1)S(1)}, u32[]{:S(2)}, u32[]{:S(2)}) collective-permute-start(bf16[32,2176]{1,0:T(8,128)(2,1)S(1)} %bitcast.23), channel_id=1, source_target_pairs={{0,2},{1,3},{2,0},{3,1},{4,6},{5,7},{6,4},{7,5},{8,10},{9,11},{10,... | collective-permute-start | bytes 417800 | tf_op jit(solution)/shard_map/ppermute | solution.py:256
  52.5 5.9 %collective-permute-start.19 = (bf16[512,128]{1,0:T(8,128)(2,1)S(1)}, bf16[512,128]{1,0:T(8,128)(2,1)S(1)}, u32[]{:S(2)}, u32[]{:S(2)}) collective-permute-start(bf16[512,128]{1,0:T(8,128)(2,1)S(1)} %fusion.2), channel_id=1, source_target_pairs={{0,16},{8,24},{16,0},{24,8},{1,17},{9,25},{17,1},{25,9},{2,18},{10... | collective-permute-start | bytes 393224 | tf_op jit(solution)/shard_map/ppermute | solution.py:256
  53.9 5.3 %collective-permute-start.11 = (bf16[32,2176]{1,0:T(8,128)(2,1)S(1)}, bf16[32,2176]{1,0:T(8,128)(2,1)S(1)}, u32[]{:S(2)}, u32[]{:S(2)}) collective-permute-start(bf16[32,2176]{1,0:T(8,128)(2,1)S(1)} %bitcast.24), channel_id=1, source_target_pairs={{0,1},{1,0},{2,3},{3,2},{4,5},{5,4},{6,7},{7,6},{8,9},{9,8},{10,11... | collective-permute-start | bytes 417800 | tf_op jit(solution)/shard_map/ppermute | solution.py:256
  55.0 4.1 %collective-permute-start.17 = (bf16[32,2176]{1,0:T(8,128)(2,1)S(1)}, bf16[32,2176]{1,0:T(8,128)(2,1)S(1)}, u32[]{:S(2)}, u32[]{:S(2)}) collective-permute-start(bf16[32,2176]{1,0:T(8,128)(2,1)S(1)} %collective-permute-done.16.refs_6_), channel_id=1, source_target_pairs={{0,1},{1,0},{2,3},{3,2},{4,5},{5,4},{6,7},{7,6},{8,9},{9,8},{10,11... | collective-permute-start | bytes 417800 | tf_op jit(solution)/shard_map/ppermute | solution.py:256
  56.4 2.7 %collective-permute-start.15 = (bf16[32,2176]{1,0:T(8,128)(2,1)S(1)}, bf16[32,2176]{1,0:T(8,128)(2,1)S(1)}, u32[]{:S(2)}, u32[]{:S(2)}) collective-permute-start(bf16[32,2176]{1,0:T(8,128)(2,1)S(1)} %collective-permute-done.14.refs_4_), channel_id=1, source_target_pairs={{0,1},{1,0},{2,3},{3,2},{4,5},{5,4},{6,7},{7,6},{8,9},{9,8},{10,11... | collective-permute-start | bytes 417800 | tf_op jit(solution)/shard_map/ppermute | solution.py:256
  57.0 2.2 %collective-permute-start.13 = (bf16[32,2176]{1,0:T(8,128)(2,1)S(1)}, bf16[32,2176]{1,0:T(8,128)(2,1)S(1)}, u32[]{:S(2)}, u32[]{:S(2)}) collective-permute-start(bf16[32,2176]{1,0:T(8,128)(2,1)S(1)} %collective-permute-done.12.refs_2_), channel_id=1, source_target_pairs={{0,1},{1,0},{2,3},{3,2},{4,5},{5,4},{6,7},{7,6},{8,9},{9,8},{10,11... | collective-permute-start | bytes 417800 | tf_op jit(solution)/shard_map/ppermute | solution.py:256
